TPU v7x, 32 devices: a whole 2x2x4 slice. The times are simulated.
32 devices in a mesh: seq: 32 (over z, y, x, core).
Axes of the slice: x: 2, y: 2, z: 4, core: 2. Of those that a mesh axis runs over, the one named last changes fastest.
Arguments:
- tokens: bfloat16 [16384, 1024], P('seq'), may hold values from -6 to 6
- out_grad: bfloat16 [16384, 1024], P('seq'), may hold values from -6 to 6
- caption_states: bfloat16 [512, 1024], replicated, may hold values from -6 to 6
- query_weight: bfloat16 [1024, 1024], replicated, may hold values from -0.1875 to 0.1875
- key_weight: bfloat16 [1024, 1024], replicated, may hold values from -0.1875 to 0.1875
- value_weight: bfloat16 [1024, 1024], replicated, may hold values from -0.1875 to 0.1875
- output_weight: bfloat16 [1024, 1024], replicated, may hold values from -0.75 to 0.75
- cross_query: bfloat16 [1024, 1024], replicated, may hold values from -0.1875 to 0.1875
- cross_key: bfloat16 [1024, 1024], replicated, may hold values from -0.1875 to 0.1875
- cross_value: bfloat16 [1024, 1024], replicated, may hold values from -0.1875 to 0.1875
- cross_output: bfloat16 [1024, 1024], replicated, may hold values from -0.5 to 0.5
- up_weight: bfloat16 [1024, 4096], replicated, may hold values from -0.1875 to 0.1875
- down_weight: bfloat16 [4096, 1024], replicated, may hold values from -0.09375 to 0.09375
- attn_gain: float32 [1024], replicated, may hold values from 0.5 to 1.5
- attn_bias: float32 [1024], replicated, may hold values from -1.5 to 1.5
- cross_gain: float32 [1024], replicated, may hold values from 0.5 to 1.5
- cross_bias: float32 [1024], replicated, may hold values from -1.5 to 1.5
- mlp_gain: float32 [1024], replicated, may hold values from 0.5 to 1.5
- mlp_bias: float32 [1024], replicated, may hold values from -1.5 to 1.5
- item_ids: int32 [16384], replicated, may hold values from 0 to 23, never falling along the last dimension, each value on 1 to 1024 neighbouring positions
- caption_segments: int32 [4, 128], replicated, may hold values from 0 to 3, never falling along the last dimension, each value on 1 to 64 neighbouring positions
- item_rows: int32 [24], replicated, may hold values from 0 to 3
- item_segments: int32 [24], replicated, may hold values from 0 to 3
Outputs:
- block_output: bfloat16 [16384, 1024], P('seq')
- input_grad: float32 [16384, 1024], P('seq')
- caption_grad: float32 [512, 1024], P('seq')
- query_weight_grad: float32 [1024, 1024], P('seq')
- key_weight_grad: float32 [1024, 1024], P('seq')
- value_weight_grad: float32 [1024, 1024], P('seq')
- output_weight_grad: float32 [1024, 1024], P('seq')
- cross_query_grad: float32 [1024, 1024], P('seq')
- cross_key_grad: float32 [1024, 1024], P('seq')
- cross_value_grad: float32 [1024, 1024], P('seq')
- cross_output_grad: float32 [1024, 1024], P('seq')
- up_weight_grad: float32 [1024, 4096], P('seq')
- down_weight_grad: float32 [4096, 1024], P('seq')
- attn_gain_grad: float32 [1024], P('seq')
- attn_bias_grad: float32 [1024], P('seq')
- cross_gain_grad: float32 [1024], P('seq')
- cross_bias_grad: float32 [1024], P('seq')
- mlp_gain_grad: float32 [1024], P('seq')
- mlp_bias_grad: float32 [1024], P('seq')
Inputs may be any that keep to these rules, and one draw needn't show every extreme that they name: `item_ids`: item ids never fall along the stream; each item holds 1 to 1024 consecutive tokens, and one holds exactly 1024. `caption_segments`: within each caption row the ids never fall; every caption has 1 to 64 tokens.
All inputs are finite; a program needn't handle non-finite values.
Results may differ from a plain program's by a relative error of at most 0.017.
Values may be sent and summed in bfloat16 or wider, within the bound.
A program may use at most 256 MiB of HBM per device.

v0:
```python
import jax
import jax.numpy as jnp
from jax import lax
from jax.sharding import PartitionSpec as P

HEADS = 16
REACH = 2


EPS = 1e-05
NEG = -1e30


def from_behind(array, axis, by):
    peers = lax.axis_size(axis)
    pairs = [(i, i + by) for i in range(peers) if 0 <= i + by < peers]
    return lax.ppermute(array, axis, pairs)


def layer_norm(value, gain, bias):
    mean = jnp.mean(value, axis=-1, keepdims=True)
    centred = value - mean
    spread = jnp.mean(centred * centred, axis=-1, keepdims=True)
    return centred * lax.rsqrt(spread + EPS) * gain + bias


def split_heads(value, heads):
    return value.reshape(value.shape[0], heads, -1).transpose(1, 0, 2)


def merge_heads(value):
    return value.transpose(1, 0, 2).reshape(value.shape[1], -1)


def matmul(left, right):
    return jnp.dot(left, right, preferred_element_type=jnp.float32)


def left_product(left, right):
    return jnp.einsum("ta,tb->ab", left, right, preferred_element_type=jnp.float32)


def right_product(left, right):
    return jnp.einsum("tb,ab->ta", left, right, preferred_element_type=jnp.float32)


def attend_forward(queries, keys, values, allowed, heads):

    def one_head(parts):
        head_q, head_k, head_v = parts
        scaling = head_q.shape[-1] ** (-0.5)
        scores = (
            jnp.einsum("qd,kd->qk", head_q, head_k, preferred_element_type=jnp.float32) * scaling
        )
        scores = jnp.where(allowed, scores, NEG)
        row_max = jnp.max(scores, axis=-1, keepdims=True)
        weights = jnp.exp(scores - row_max)
        summed = jnp.sum(weights, axis=-1, keepdims=True)
        attn_probs = (weights / summed).astype(jnp.bfloat16)
        result = jnp.einsum("qk,kd->qd", attn_probs, head_v, preferred_element_type=jnp.float32)
        return (result, (row_max + jnp.log(summed))[:, 0])

    results, log_norm = lax.map(
        one_head,
        (split_heads(queries, heads), split_heads(keys, heads), split_heads(values, heads)),
    )
    return (merge_heads(results).astype(jnp.bfloat16), log_norm)


def attend_backward(queries, keys, values, allowed, log_norm, grad_att, heads):

    def one_head(parts):
        head_q, head_k, head_v, head_norm, head_grad = parts
        scaling = head_q.shape[-1] ** (-0.5)
        scores = (
            jnp.einsum("qd,kd->qk", head_q, head_k, preferred_element_type=jnp.float32) * scaling
        )
        attn_probs = jnp.where(allowed, jnp.exp(scores - head_norm[:, None]), 0.0)
        grad_probs = jnp.einsum("qd,kd->qk", head_grad, head_v, preferred_element_type=jnp.float32)
        row_inner = jnp.sum(attn_probs * grad_probs, axis=-1, keepdims=True)
        grad_scores = (attn_probs * (grad_probs - row_inner)).astype(jnp.bfloat16)
        grad_q = (
            jnp.einsum("qk,kd->qd", grad_scores, head_k, preferred_element_type=jnp.float32)
            * scaling
        )
        grad_k = (
            jnp.einsum("qk,qd->kd", grad_scores, head_q, preferred_element_type=jnp.float32)
            * scaling
        )
        grad_v = jnp.einsum(
            "qk,qd->kd",
            attn_probs.astype(jnp.bfloat16),
            head_grad,
            preferred_element_type=jnp.float32,
        )
        return (grad_q, grad_k, grad_v)

    grad_q, grad_k, grad_v = lax.map(
        one_head,
        (
            split_heads(queries, heads),
            split_heads(keys, heads),
            split_heads(values, heads),
            log_norm,
            split_heads(grad_att, heads),
        ),
    )
    return (merge_heads(grad_q), merge_heads(grad_k), merge_heads(grad_v))


def body(
    tokens,
    out_grad,
    caption_states,
    query_weight,
    key_weight,
    value_weight,
    output_weight,
    cross_query,
    cross_key,
    cross_value,
    cross_output,
    up_weight,
    down_weight,
    attn_gain,
    attn_bias,
    cross_gain,
    cross_bias,
    mlp_gain,
    mlp_bias,
    item_ids,
    caption_segments,
    item_rows,
    item_segments,
):
    device = lax.axis_index("seq")
    count = lax.axis_size("seq")
    rows_here = tokens.shape[0]
    heads = HEADS
    inputs = tokens.astype(jnp.float32)
    normed_one = layer_norm(inputs, attn_gain, attn_bias)
    low_one = normed_one.astype(jnp.bfloat16)
    queries = matmul(low_one, query_weight).astype(jnp.bfloat16)
    keys_here = matmul(low_one, key_weight).astype(jnp.bfloat16)
    values_here = matmul(low_one, value_weight).astype(jnp.bfloat16)
    key_blocks = [keys_here]
    value_blocks = [values_here]
    for offset in range(1, REACH + 1):
        moved_keys, moved_values = from_behind((keys_here, values_here), "seq", offset)
        key_blocks.insert(0, moved_keys)
        value_blocks.insert(0, moved_values)
    near_keys = jnp.concatenate(key_blocks, 0)
    near_values = jnp.concatenate(value_blocks, 0)
    all_tokens = item_ids.shape[0]
    query_pos = device * rows_here + jnp.arange(rows_here, dtype=jnp.int32)
    key_pos = (device - REACH) * rows_here + jnp.arange((REACH + 1) * rows_here, dtype=jnp.int32)
    query_item = lax.dynamic_slice_in_dim(item_ids, device * rows_here, rows_here)
    key_item = item_ids[jnp.clip(key_pos, 0, all_tokens - 1)]
    self_mask = (
        (key_pos[None, :] >= 0)
        & (key_pos[None, :] <= query_pos[:, None])
        & (key_item[None, :] == query_item[:, None])
    )
    self_att, self_norm = attend_forward(queries, near_keys, near_values, self_mask, heads)
    after_one = inputs + matmul(self_att, output_weight)
    normed_two = layer_norm(after_one, cross_gain, cross_bias)
    low_two = normed_two.astype(jnp.bfloat16)
    cross_q = matmul(low_two, cross_query).astype(jnp.bfloat16)
    text_total = caption_states.shape[0]
    text_rows = text_total // count
    own_text = lax.dynamic_slice_in_dim(caption_states, device * text_rows, text_rows)
    text_keys = matmul(caption_states, cross_key).astype(jnp.bfloat16)
    text_values = matmul(caption_states, cross_value).astype(jnp.bfloat16)
    item_range = jnp.arange(item_rows.shape[0], dtype=jnp.int32)
    member = query_item[:, None] == item_range[None, :]
    query_row = jnp.sum(jnp.where(member, item_rows[None, :], 0), axis=1)
    query_seg = jnp.sum(jnp.where(member, item_segments[None, :], 0), axis=1)
    caption_len = caption_segments.shape[1]
    key_row = jnp.arange(text_total, dtype=jnp.int32) // caption_len
    key_seg = caption_segments.reshape(-1)
    cross_mask = (key_row[None, :] == query_row[:, None]) & (key_seg[None, :] == query_seg[:, None])
    cross_att, cross_norm = attend_forward(cross_q, text_keys, text_values, cross_mask, heads)
    after_two = after_one + matmul(cross_att, cross_output)
    normed_three = layer_norm(after_two, mlp_gain, mlp_bias)
    low_three = normed_three.astype(jnp.bfloat16)
    hidden_pre = matmul(low_three, up_weight)
    hidden_low = jax.nn.gelu(hidden_pre).astype(jnp.bfloat16)
    block_output = (after_two + matmul(hidden_low, down_weight)).astype(jnp.bfloat16)
    down_grad = left_product(hidden_low, out_grad)
    grad_hidden = right_product(out_grad, down_weight)
    unused, gelu_back = jax.vjp(jax.nn.gelu, hidden_pre)
    grad_pre = gelu_back(grad_hidden)[0].astype(jnp.bfloat16)
    up_grad = left_product(low_three, grad_pre)
    unused, norm_three_back = jax.vjp(layer_norm, after_two, mlp_gain, mlp_bias)
    part_three, mlp_gain_grad, mlp_bias_grad = norm_three_back(right_product(grad_pre, up_weight))
    grad_two = out_grad.astype(jnp.float32) + part_three
    grad_branch_two = grad_two.astype(jnp.bfloat16)
    cross_output_grad = left_product(cross_att, grad_branch_two)
    grad_cross = right_product(grad_branch_two, cross_output).astype(jnp.bfloat16)
    grad_cq, grad_tk, grad_tv = attend_backward(
        cross_q, text_keys, text_values, cross_mask, cross_norm, grad_cross, heads
    )
    grad_cq = grad_cq.astype(jnp.bfloat16)
    cross_query_grad = left_product(low_two, grad_cq)
    summed_tk, summed_tv = lax.psum((grad_tk, grad_tv), "seq")
    own_tk = lax.dynamic_slice_in_dim(summed_tk, device * text_rows, text_rows)
    own_tv = lax.dynamic_slice_in_dim(summed_tv, device * text_rows, text_rows)
    own_tk = own_tk.astype(jnp.bfloat16)
    own_tv = own_tv.astype(jnp.bfloat16)
    cross_key_grad = left_product(own_text, own_tk)
    cross_value_grad = left_product(own_text, own_tv)
    caption_grad = right_product(own_tk, cross_key) + right_product(own_tv, cross_value)
    unused, norm_two_back = jax.vjp(layer_norm, after_one, cross_gain, cross_bias)
    part_two, cross_gain_grad, cross_bias_grad = norm_two_back(right_product(grad_cq, cross_query))
    grad_one = grad_two + part_two
    grad_branch_one = grad_one.astype(jnp.bfloat16)
    output_weight_grad = left_product(self_att, grad_branch_one)
    grad_self = right_product(grad_branch_one, output_weight).astype(jnp.bfloat16)
    grad_q, grad_near_k, grad_near_v = attend_backward(
        queries, near_keys, near_values, self_mask, self_norm, grad_self, heads
    )
    key_sum = grad_near_k[REACH * rows_here :]
    value_sum = grad_near_v[REACH * rows_here :]
    for offset in range(1, REACH + 1):
        start = (REACH - offset) * rows_here
        back_keys, back_values = (
            from_behind(
                grad_near_k[start : start + rows_here].astype(jnp.bfloat16), "seq", -offset
            ).astype(jnp.float32),
            from_behind(
                grad_near_v[start : start + rows_here].astype(jnp.bfloat16), "seq", -offset
            ).astype(jnp.float32),
        )
        key_sum = key_sum + back_keys
        value_sum = value_sum + back_values
    grad_q = grad_q.astype(jnp.bfloat16)
    key_low = key_sum.astype(jnp.bfloat16)
    value_low = value_sum.astype(jnp.bfloat16)
    query_grad = left_product(low_one, grad_q)
    key_grad = left_product(low_one, key_low)
    value_grad = left_product(low_one, value_low)
    grad_norm_one = (
        right_product(grad_q, query_weight)
        + right_product(key_low, key_weight)
        + right_product(value_low, value_weight)
    )
    unused, norm_one_back = jax.vjp(layer_norm, inputs, attn_gain, attn_bias)
    part_one, attn_gain_grad, attn_bias_grad = norm_one_back(grad_norm_one)
    input_grad = grad_one + part_one
    shards = (
        lax.psum_scatter(query_grad, "seq", scatter_dimension=0, tiled=True),
        lax.psum_scatter(key_grad, "seq", scatter_dimension=0, tiled=True),
        lax.psum_scatter(value_grad, "seq", scatter_dimension=0, tiled=True),
        lax.psum_scatter(output_weight_grad, "seq", scatter_dimension=0, tiled=True),
        lax.psum_scatter(cross_query_grad, "seq", scatter_dimension=0, tiled=True),
        lax.psum_scatter(cross_key_grad, "seq", scatter_dimension=0, tiled=True),
        lax.psum_scatter(cross_value_grad, "seq", scatter_dimension=0, tiled=True),
        lax.psum_scatter(cross_output_grad, "seq", scatter_dimension=0, tiled=True),
        lax.psum_scatter(up_grad, "seq", scatter_dimension=0, tiled=True),
        lax.psum_scatter(down_grad, "seq", scatter_dimension=0, tiled=True),
        lax.psum_scatter(attn_gain_grad, "seq", scatter_dimension=0, tiled=True),
        lax.psum_scatter(attn_bias_grad, "seq", scatter_dimension=0, tiled=True),
        lax.psum_scatter(cross_gain_grad, "seq", scatter_dimension=0, tiled=True),
        lax.psum_scatter(cross_bias_grad, "seq", scatter_dimension=0, tiled=True),
        lax.psum_scatter(mlp_gain_grad, "seq", scatter_dimension=0, tiled=True),
        lax.psum_scatter(mlp_bias_grad, "seq", scatter_dimension=0, tiled=True),
    )
    return (
        block_output,
        input_grad,
        caption_grad,
        shards[0],
        shards[1],
        shards[2],
        shards[3],
        shards[4],
        shards[5],
        shards[6],
        shards[7],
        shards[8],
        shards[9],
        shards[10],
        shards[11],
        shards[12],
        shards[13],
        shards[14],
        shards[15],
    )


def solution(mesh):
    placed = (
        P("seq", None),
        P("seq", None),
        P(),
        P(),
        P(),
        P(),
        P(),
        P(),
        P(),
        P(),
        P(),
        P(),
        P(),
        P(),
        P(),
        P(),
        P(),
        P(),
        P(),
        P(),
        P(),
        P(),
        P(),
    )
    return jax.shard_map(
        body,
        mesh=mesh,
        in_specs=placed,
        out_specs=(
            P("seq", None),
            P("seq", None),
            P("seq", None),
            P("seq", None),
            P("seq", None),
            P("seq", None),
            P("seq", None),
            P("seq", None),
            P("seq", None),
            P("seq", None),
            P("seq", None),
            P("seq", None),
            P("seq", None),
            P("seq"),
            P("seq"),
            P("seq"),
            P("seq"),
            P("seq"),
            P("seq"),
        ),
        check_vma=False,
    )
```

profile of v0, /device:TPU:0, one launch (start us, length us, event | category | flops | bytes accessed | tf_op | source)
XLA Modules:
  0.0 2052.6 jit_solution(7178638589317877712)
XLA Ops:
  11.2 4.0 convolution_convert_fusion.6
  15.2 6.0 collective-permute-start
  26.0 3.2 collective-permute-start.2
  29.2 4.0 collective-permute-start.3
  37.9 6.9 fusion.158
  60.2 8.4 gather_fusion
  78.8 3.2 pad_maximum_fusion
  82.0 4.7 copy.95
  86.8 6.7 copy.98
  93.4 3.2 pad_maximum_fusion.1
  96.6 4.7 copy.96
  101.3 6.7 copy.99
  108.0 127.5 %while.60 = (s32[]{:T(128)}, bf16[16,512,64]{1,2,0:T(8,128)(2,1)}, f32[16,512]{1,0:T(8,128)S(1)}, bf16[16,512,64]{2,1,0:T(8,128)(2,1)}, bf16[16,1536,64]{2,1,0:T...) while((s32[]{:T(128)}, bf16[16,512,64]{1,2,0:T(8,128)(2,1)}, ...), condition=%wide.region_5.6_spmd.clone.clone, body=%wide.region_2.5_spmd.clone.sunk.clone | while | flops 210763264 | bytes 23109260 | solution.py:63
  112.7 3.4 fusion.273
  120.6 3.4 fusion.273
  128.6 3.4 fusion.273
  136.6 3.4 fusion.273
  144.5 3.4 fusion.273
  152.5 3.4 fusion.273
  160.5 3.4 fusion.273
  168.4 3.4 fusion.273
  176.4 3.4 fusion.273
  184.4 3.4 fusion.273
  192.4 3.3 fusion.273
  200.3 3.4 fusion.273
  208.3 3.4 fusion.273
  216.3 3.4 fusion.273
  224.2 3.4 fusion.273
  232.2 3.4 fusion.273
  235.6 3.3 fusion.156
  244.8 2.9 copy.103
  247.8 76.5 %while.61 = (s32[]{:T(128)}, bf16[16,512,64]{1,2,0:T(8,128)(2,1)}, f32[16,512]{1,0:T(8,128)S(1)}, bf16[16,512,64]{2,1,0:T(8,128)(2,1)}, bf16[16,512,64]{2,1,0:T(...) while((s32[]{:T(128)}, bf16[16,512,64]{1,2,0:T(8,128)(2,1)}, ...), condition=%wide.region_13.14_spmd.clone.clone, body=%wide.region_10.13_spmd.clone.sunk.clone | while | flops 69991936 | bytes 7895173 | solution.py:63
  324.3 4.0 fusion.157
  329.1 15.6 fusion.98
  344.7 5.0 multiply_reduce_fusion.2
  357.5 133.9 %while.62 = (s32[]{:T(128)}, bf16[16,512,64]{1,2,0:T(8,128)(2,1)}, f32[16,512,64]{1,2,0:T(8,128)}, f32[16,512,64]{1,2,0:T(8,128)}, bf16[16,512,64]{2,1,0:T(8,128...) while((s32[]{:T(128)}, bf16[16,512,64]{1,2,0:T(8,128)(2,1)}, ...), condition=%wide.region_20.21_spmd.clone.clone, body=%wide.region_18.20_spmd.clone.sunk.clone | while | flops 170982912 | bytes 9067649 | solution.py:98
  491.4 5.3 fusion.135
  496.8 4.7 fusion.161
  501.8 4.0 multiply_reduce_fusion.3
  513.8 4.5 fusion.115
  518.5 178.5 %while.63 = (s32[]{:T(128)}, bf16[16,512,64]{1,2,0:T(8,128)(2,1)}, f32[16,1536,64]{1,2,0:T(8,128)}, f32[16,1536,64]{1,2,0:T(8,128)}, bf16[16,512,64]{2,1,0:T(8,1...) while((s32[]{:T(128)}, bf16[16,512,64]{1,2,0:T(8,128)(2,1)}, ...), condition=%wide.region_25.26_spmd.clone.clone, body=%wide.region_23.25_spmd.clone.sunk.clone | while | flops 513670656 | bytes 26116744 | solution.py:98
  542.5 2.8 multiply_reduce_fusion.13
  576.0 2.8 multiply_reduce_fusion.13
  609.4 2.8 multiply_reduce_fusion.13
  665.2 2.8 multiply_reduce_fusion.13
  697.0 4.7 fusion.143
  701.8 5.5 bitcast_convert_fusion
  722.8 37.0 %collective-permute-done.5 = bf16[512,1024]{0,1:T(8,128)(2,1)} collective-permute-done((bf16[512,1024]{0,1:T(8,128)(2,1)}, bf16[512,1024]{0,1:T(8,128)(2,1)}, u32[]{:S(2)}, u32[]{:S(2)}) %collective-permute-start.5) | collective-permute-done | bytes 1048608 | tf_op jit(solution)/shard_map/ppermute | solution.py:17
  761.9 21.2 %collective-permute-done.7 = bf16[512,1024]{0,1:T(8,128)(2,1)} collective-permute-done((bf16[512,1024]{0,1:T(8,128)(2,1)}, bf16[512,1024]{0,1:T(8,128)(2,1)}, u32[]{:S(2)}, u32[]{:S(2)}) %collective-permute-start.7) | collective-permute-done | bytes 1048608 | tf_op jit(solution)/shard_map/ppermute | solution.py:17
  790.1 122.2 %all-reduce.8 = (bf16[512,1024]{0,1:T(8,128)(2,1)}, bf16[512,1024]{0,1:T(8,128)(2,1)}, f32[1024]{0:T(1024)S(1)}, f32[1024]{0:T(1024)S(1)}, f32[1024]{0:T(1024)S(...) all-reduce(f32[512,1024]{0,1:T(8,128)} %bitcast.336, ...), channel_id=1, replica_groups=mesh['seq'=32] {'seq'}, use_global_device_ids=true, to_apply=%region_28.29 | all-reduce | flops 1054720 | bytes 6340608 | tf_op jit(solution)/shard_map/psum | solution.py:205
  912.3 3.7 fusion.118
  916.1 3.8 fusion.120
  921.1 3.5 fusion.141
  925.8 3.5 fusion.139
  930.9 10.4 fusion.136
  941.6 15.2 fusion.138
  956.9 12.1 add_convert_fusion
  979.1 139.0 %reduce-scatter.11.cloned.1.call-done = f32[32,1024]{1,0:T(8,128)} async-done(((f32[1024,1024]{1,0:T(8,128)}), f32[32,1024]{1,0:T(8,128)}) %reduce-scatter.11.cloned.1.call-update) | async-done | bytes 131088 | tf_op jit(solution)/shard_map/reduce_scatter | solution.py:251
  1118.1 139.6 %reduce-scatter.21.cloned.1.call-done = f32[32,1024]{1,0:T(8,128)} async-done(((f32[1024,1024]{1,0:T(8,128)}), f32[32,1024]{1,0:T(8,128)}) %reduce-scatter.21.cloned.1.call-update) | async-done | bytes 131088 | tf_op jit(solution)/shard_map/reduce_scatter | solution.py:256
  1257.7 139.4 %reduce-scatter.23.cloned.1.call-done = f32[32,1024]{1,0:T(8,128)} async-done(((f32[1024,1024]{1,0:T(8,128)}), f32[32,1024]{1,0:T(8,128)}) %reduce-scatter.23.cloned.1.call-update) | async-done | bytes 131088 | tf_op jit(solution)/shard_map/reduce_scatter | solution.py:257
  1397.2 139.7 %reduce-scatter.13.cloned.1.call-done = f32[32,1024]{1,0:T(8,128)} async-done(((f32[1024,1024]{1,0:T(8,128)}), f32[32,1024]{1,0:T(8,128)}) %reduce-scatter.13.cloned.1.call-update) | async-done | bytes 131088 | tf_op jit(solution)/shard_map/reduce_scatter | solution.py:252
  1536.8 139.7 %reduce-scatter.15.cloned.1.call-done = f32[32,1024]{1,0:T(8,128)} async-done(((f32[1024,1024]{1,0:T(8,128)}), f32[32,1024]{1,0:T(8,128)}) %reduce-scatter.15.cloned.1.call-update) | async-done | bytes 131088 | tf_op jit(solution)/shard_map/reduce_scatter | solution.py:253
  1676.5 181.8 %reduce-scatter.27.cloned.1.call-done = f32[32,4096]{1,0:T(8,128)} async-done(((f32[1024,4096]{1,0:T(8,128)}), f32[32,4096]{1,0:T(8,128)}) %reduce-scatter.27.cloned.1.call-update) | async-done | bytes 524304 | tf_op jit(solution)/shard_map/reduce_scatter | solution.py:259
  1858.3 187.3 %reduce-scatter.29.cloned.1.call-done = f32[128,1024]{1,0:T(8,128)} async-done(((f32[4096,1024]{1,0:T(8,128)}), f32[128,1024]{1,0:T(8,128)}) %reduce-scatter.29.cloned.1.call-update) | async-done | bytes 524304 | tf_op jit(solution)/shard_map/reduce_scatter | solution.py:260
  (649 shorter events, 550.6 us)
Async XLA Ops:
  7.2 233.0 %copy-start = (bf16[1024,1024]{1,0:T(8,128)(2,1)S(1)}, bf16[1024,1024]{1,0:T(8,128)(2,1)}, u32[]{:S(2)}) copy-start(bf16[1024,1024]{1,0:T(8,128)(2,1)} %param.38) | copy-start | bytes 6291460
  7.2 3.9 copy-start.4
  7.2 3.9 copy-start.33
  7.2 3.9 copy-start.49
  7.2 971.9 %reduce-scatter.19.cloned.1.call-start = ((), (), s32[]{:S(2)}) async-start(), calls=%async_computation.14 | async-start | bytes 4325376 | tf_op jit(solution)/shard_map/reduce_scatter | solution.py:255
  8.9 24.4 %copy-start.31 = (f32[512]{0:T(512)}, f32[512]{0:T(512)S(1)}, u32[]{:S(2)}) copy-start(f32[512]{0:T(512)S(1)} %broadcast_multiply_fusion.2) | copy-start | bytes 6148
  11.1 22.2 %copy-start.37 = (f32[512]{0:T(512)}, f32[512]{0:T(512)S(1)}, u32[]{:S(2)}) copy-start(f32[512]{0:T(512)S(1)} %fusion.127) | copy-start | bytes 6148
  11.1 12.5 copy-start.26
  15.2 18.1 copy-start.45
  15.2 63.6 %collective-permute-start = (bf16[512,1024]{1,0:T(8,128)(2,1)}, bf16[512,1024]{1,0:T(8,128)(2,1)}, u32[]{:S(2)}, u32[]{:S(2)}) collective-permute-start(bf16[512,1024]{1,0:T(8,128)(2,1)} %convolution_convert_fusion.6), channel_id=1, source_target_pairs={{0,2},{1,3},{2,4},{3,5},{4,6},{5,7},{6,8},{7,9},{8,10},{9,11},{10,... | collective-permute-start | bytes 3145736 | tf_op jit(solution)/shard_map/ppermute | solution.py:17
  21.2 57.7 %collective-permute-start.1 = (bf16[512,1024]{1,0:T(8,128)(2,1)}, bf16[512,1024]{1,0:T(8,128)(2,1)}, u32[]{:S(2)}, u32[]{:S(2)}) collective-permute-start(bf16[512,1024]{1,0:T(8,128)(2,1)} %convolution_convert_fusion.6), channel_id=1, source_target_pairs={{0,1},{1,2},{2,3},{3,4},{4,5},{5,6},{6,7},{7,8},{8,9},{9,10},{10,1... | collective-permute-start | bytes 3145736 | tf_op jit(solution)/shard_map/ppermute | solution.py:17
  23.7 14.2 slice-start.2
  26.0 9.6 copy-start.22
  26.0 9.6 copy-start.39
  26.0 11.9 slice-start.3
  26.0 67.5 %collective-permute-start.2 = (bf16[512,1024]{1,0:T(8,128)(2,1)}, bf16[512,1024]{1,0:T(8,128)(2,1)}, u32[]{:S(2)}, u32[]{:S(2)}) collective-permute-start(bf16[512,1024]{1,0:T(8,128)(2,1)} %convolution_convert_fusion.5), channel_id=1, source_target_pairs={{0,2},{1,3},{2,4},{3,5},{4,6},{5,7},{6,8},{7,9},{8,10},{9,11},{10,... | collective-permute-start | bytes 3145736 | tf_op jit(solution)/shard_map/ppermute | solution.py:17
  29.2 64.2 %collective-permute-start.3 = (bf16[512,1024]{1,0:T(8,128)(2,1)}, bf16[512,1024]{1,0:T(8,128)(2,1)}, u32[]{:S(2)}, u32[]{:S(2)}) collective-permute-start(bf16[512,1024]{1,0:T(8,128)(2,1)} %convolution_convert_fusion.5), channel_id=1, source_target_pairs={{0,1},{1,2},{2,3},{3,4},{4,5},{5,6},{6,7},{7,8},{8,9},{9,10},{10,1... | collective-permute-start | bytes 3145736 | tf_op jit(solution)/shard_map/ppermute | solution.py:17
  35.6 2.3 copy-start.16
  37.9 7.0 copy-start.24
  57.3 2.7 copy-start.2
  75.9 2.8 copy-start.42
  75.9 2.8 copy-start.43
  110.4 1.6 copy-start.3
  118.3 1.6 copy-start.3
  126.3 1.6 copy-start.3
  134.3 1.6 copy-start.3
  142.2 1.6 copy-start.3
  244.8 2.9 copy-start.52
  324.3 20.4 slice-start
  328.3 21.4 %copy-start.14 = (f32[512,1024]{1,0:T(8,128)}, f32[512,1024]{1,0:T(8,128)S(1)}, u32[]{:S(2)}) copy-start(f32[512,1024]{1,0:T(8,128)S(1)} %get-tuple-element.618) | copy-start | bytes 6291460
  329.1 15.7 slice-start.1
  344.7 5.0 copy-start.53
  351.0 1.9 copy-start.44
  496.7 482.4 %reduce-scatter.25.cloned.1.call-start = ((), (), s32[]{:S(2)}) async-start(), calls=%async_computation.17 | async-start | bytes 4325376 | tf_op jit(solution)/shard_map/reduce_scatter | solution.py:258
  501.5 477.6 %reduce-scatter.17.cloned.1.call-start = ((), (), s32[]{:S(2)}) async-start(), calls=%async_computation.13 | async-start | bytes 4325376 | tf_op jit(solution)/shard_map/reduce_scatter | solution.py:254
  501.7 4.0 copy-start.11
  505.8 1.8 copy-start.18
  509.2 4.6 copy-start.6
  518.4 599.7 %reduce-scatter.11.cloned.1.call-start = ((), (), s32[]{:S(2)}) async-start(), calls=%async_computation.10 | async-start | bytes 4325376 | tf_op jit(solution)/shard_map/reduce_scatter | solution.py:251
  518.4 178.5 %copy-start.32 = (f32[512]{0:T(512)S(1)}, f32[512]{0:T(512)}, u32[]{:S(2)}) copy-start(f32[512]{0:T(512)} %copy-done.31) | copy-start | bytes 6148
  518.5 178.5 %copy-start.34 = (f32[1024]{0:T(1024)S(1)}, f32[1024]{0:T(1024)}, u32[]{:S(2)}) copy-start(f32[1024]{0:T(1024)} %param.44) | copy-start | bytes 12292
  518.5 178.5 %copy-start.38 = (f32[512]{0:T(512)S(1)}, f32[512]{0:T(512)}, u32[]{:S(2)}) copy-start(f32[512]{0:T(512)} %copy-done.37) | copy-start | bytes 6148
  518.5 178.5 %copy-start.50 = (f32[1024]{0:T(1024)S(1)}, f32[1024]{0:T(1024)}, u32[]{:S(2)}) copy-start(f32[1024]{0:T(1024)} %param.45) | copy-start | bytes 12292
  701.7 556.0 %reduce-scatter.21.cloned.1.call-start = ((), (), s32[]{:S(2)}) async-start(), calls=%async_computation.15 | async-start | bytes 4325376 | tf_op jit(solution)/shard_map/reduce_scatter | solution.py:256
  709.0 13.8 collective-permute-start.4
  710.3 49.5 %collective-permute-start.5 = (bf16[512,1024]{0,1:T(8,128)(2,1)}, bf16[512,1024]{0,1:T(8,128)(2,1)}, u32[]{:S(2)}, u32[]{:S(2)}) collective-permute-start(bf16[512,1024]{0,1:T(8,128)(2,1)} %bitcast.34), channel_id=1, source_target_pairs={{2,0},{3,1},{4,2},{5,3},{6,4},{7,5},{8,6},{9,7},{10,8},{11,9},{12,... | collective-permute-start | bytes 3145736 | tf_op jit(solution)/shard_map/ppermute | solution.py:17
  713.2 48.7 %collective-permute-start.6 = (bf16[512,1024]{0,1:T(8,128)(2,1)}, bf16[512,1024]{0,1:T(8,128)(2,1)}, u32[]{:S(2)}, u32[]{:S(2)}) collective-permute-start(bf16[512,1024]{0,1:T(8,128)(2,1)} %bitcast.37), channel_id=1, source_target_pairs={{1,0},{2,1},{3,2},{4,3},{5,4},{6,5},{7,6},{8,7},{9,8},{10,9},{11,1... | collective-permute-start | bytes 3145736 | tf_op jit(solution)/shard_map/ppermute | solution.py:17
  714.5 68.7 %collective-permute-start.7 = (bf16[512,1024]{0,1:T(8,128)(2,1)}, bf16[512,1024]{0,1:T(8,128)(2,1)}, u32[]{:S(2)}, u32[]{:S(2)}) collective-permute-start(bf16[512,1024]{0,1:T(8,128)(2,1)} %bitcast.38), channel_id=1, source_target_pairs={{2,0},{3,1},{4,2},{5,3},{6,4},{7,5},{8,6},{9,7},{10,8},{11,9},{12,... | collective-permute-start | bytes 3145736 | tf_op jit(solution)/shard_map/ppermute | solution.py:17
  718.0 2.3 copy-start.46
  761.9 23.4 %copy-start.28 = (bf16[512,1024]{0,1:T(8,128)(2,1)}, bf16[512,1024]{0,1:T(8,128)(2,1)S(1)}, u32[]{:S(2)}) copy-start(bf16[512,1024]{0,1:T(8,128)(2,1)S(1)} %fusion.113) | copy-start | bytes 3145732
  761.9 23.4 %copy-start.47 = (bf16[1024,1024]{1,0:T(8,128)(2,1)S(1)}, bf16[1024,1024]{1,0:T(8,128)(2,1)}, u32[]{:S(2)}) copy-start(bf16[1024,1024]{1,0:T(8,128)(2,1)} %param.35) | copy-start | bytes 6291460
  785.4 2.0 copy-start.27
  787.4 1.8 copy-start.36
  789.1 123.2 %copy-start.12 = (f32[512,1024]{1,0:T(8,128)}, f32[512,1024]{1,0:T(8,128)S(1)}, u32[]{:S(2)}) copy-start(f32[512,1024]{1,0:T(8,128)S(1)} %get-tuple-element.623) | copy-start | bytes 6291460
  916.1 481.1 %reduce-scatter.23.cloned.1.call-start = ((), (), s32[]{:S(2)}) async-start(), calls=%async_computation.16 | async-start | bytes 4325376 | tf_op jit(solution)/shard_map/reduce_scatter | solution.py:257
  919.9 616.9 %reduce-scatter.13.cloned.1.call-start = ((), (), s32[]{:S(2)}) async-start(), calls=%async_computation.11 | async-start | bytes 4325376 | tf_op jit(solution)/shard_map/reduce_scatter | solution.py:252
  924.6 751.9 %reduce-scatter.15.cloned.1.call-start = ((), (), s32[]{:S(2)}) async-start(), calls=%async_computation.12 | async-start | bytes 4325376 | tf_op jit(solution)/shard_map/reduce_scatter | solution.py:253
  929.4 928.9 %reduce-scatter.27.cloned.1.call-start = ((), (), s32[]{:S(2)}) async-start(), calls=%async_computation.18 | async-start | bytes 17301504 | tf_op jit(solution)/shard_map/reduce_scatter | solution.py:259
  941.4 1104.2 %reduce-scatter.29.cloned.1.call-start = ((), (), s32[]{:S(2)}) async-start(), calls=%async_computation.19 | async-start | bytes 17301504 | tf_op jit(solution)/shard_map/reduce_scatter | solution.py:260
  956.9 15.6 copy-start.23
  956.9 17.6 copy-start.25
  972.5 4.6 copy-start.7
  972.5 4.6 copy-start.13
  974.5 1071.1 %copy-start.1 = (bf16[1024,1024]{1,0:T(8,128)(2,1)S(1)}, bf16[1024,1024]{1,0:T(8,128)(2,1)}, u32[]{:S(2)}) copy-start(bf16[1024,1024]{1,0:T(8,128)(2,1)} %param.38) | copy-start | bytes 6291460
  (42 other events, 52.2 us)
Sparse Core Ops, SparseCore 0:
  496.8 139.4 reduce-scatter.18
  639.1 193.8 reduce-scatter.24
  835.9 142.5 reduce-scatter.16
  981.2 136.8 reduce-scatter.10
  1120.8 136.9 reduce-scatter.20
  1260.4 136.6 reduce-scatter.22
  1400.0 136.7 reduce-scatter.12
  1539.7 136.7 reduce-scatter.14
  1679.4 178.8 reduce-scatter.26
  1861.0 184.5 reduce-scatter.28
where the time goes:
time: 2060 us; the launch traced here: 2050 us
  waiting for transfers between devices  1120 us (54%)
  matrix products  589 us (29%)
  local copies, waits for them, and re-layouts  129 us (6%)
  blocking collectives  122 us (6%)
  other arithmetic  48.7 us (2%)
  starting transfers between devices  22 us (1%)
    reduce_scatter x1, waiting for transfers between devices, body(): lax.psum_scatter(down_grad, 'seq', scatter_dimension=0, tiled=True)  187 us
    reduce_scatter x1, waiting for transfers between devices, body(): lax.psum_scatter(up_grad, 'seq', scatter_dimension=0, tiled=True)  182 us
    reduce_scatter x1, waiting for transfers between devices, body(): lax.psum_scatter(key_grad, 'seq', scatter_dimension=0, tiled=True)  140 us
    reduce_scatter x1, waiting for transfers between devices, body(): lax.psum_scatter(value_grad, 'seq', scatter_dimension=0, tiled=True)  140 us
    reduce_scatter x1, waiting for transfers between devices, body(): lax.psum_scatter(cross_key_grad, 'seq', scatter_dimension=0, tiled=True)  140 us
    reduce_scatter x1, waiting for transfers between devices, body(): lax.psum_scatter(cross_value_grad, 'seq', scatter_dimension=0, tiled=True)  139 us
    reduce_scatter x1, waiting for transfers between devices, body(): lax.psum_scatter(query_grad, 'seq', scatter_dimension=0, tiled=True)  139 us
    dot_general x64, matrix products, one_head(): jnp.einsum('qd,kd->qk', head_q, head_k, preferred_element_type=jnp.float32)  128 us
  transfers between devices with their start and end apart: 18, of which 9 were waited for; matrix products, arithmetic and copies ran while one was open for 17% of the time, Pallas kernels for 0%

commit v1 on v0

v1 whole, which is shorter than its diff:
```python
import functools

import jax
import jax.numpy as jnp
from jax import lax
from jax.experimental import pallas as pl
from jax.experimental.pallas import tpu as pltpu
from jax.sharding import PartitionSpec as P

HEADS = 16
REACH = 2
EPS = 1e-05
NEG = -1e30
TILE = 256
LANES = 128
AXIS = "seq"
F32 = jnp.float32
BF16 = jnp.bfloat16

NT = (((1,), (1,)), ((), ()))
TN = (((0,), (0,)), ((), ()))


def head_lanes(value, half):
    lane = lax.broadcasted_iota(jnp.int32, value.shape, 1)
    keep = (lane < LANES // 2) if half == 0 else (lane >= LANES // 2)
    return jnp.where(keep, value, jnp.zeros_like(value))


def forward_kernel(causal, sizes, ends, n_ref, qid_ref, kid_ref, q_ref, k_ref, v_ref, o_ref, lse_ref, bias_ref):
    tile = pl.program_id(1)
    span = bias_ref.shape[2]

    @pl.when(pl.program_id(0) == 0)
    def _():
        last = ends[0] + tile * ends[1]
        kid = kid_ref[tile]
        qid = qid_ref[...]
        allowed = kid == qid
        if causal:
            kpos = lax.broadcasted_iota(jnp.int32, (TILE, span), 1)
            qpos = lax.broadcasted_iota(jnp.int32, (TILE, span), 0) + (span - TILE)
            allowed = allowed & (kpos <= qpos)
        bias_ref[tile] = jnp.where(allowed, 0.0, NEG)

    def run(size):
        start = pl.multiple_of(ends[0] + tile * ends[1] - size, TILE)
        keys = k_ref[pl.ds(start, size), :]
        values = v_ref[pl.ds(start, size), :]
        query = q_ref[...] * jnp.asarray(0.125, BF16)
        outs = []
        lses = []
        for half in range(2):
            scores = lax.dot_general(head_lanes(query, half), keys, NT, preferred_element_type=F32)
            scores = scores + bias_ref[tile, :, span - size :]
            row_max = jnp.max(scores, axis=1, keepdims=True)
            weights = jnp.exp(scores - row_max)
            summed = jnp.sum(weights, axis=1, keepdims=True)
            out = jnp.dot(weights.astype(BF16), values, preferred_element_type=F32)
            outs.append(out / summed)
            lses.append(row_max + jnp.log(summed))
        lane = lax.broadcasted_iota(jnp.int32, (TILE, LANES), 1)
        o_ref[...] = jnp.where(lane < LANES // 2, outs[0], outs[1]).astype(BF16)
        lse_ref[0] = jnp.where(lane < LANES // 2, lses[0], lses[1])

    if len(sizes) == 1:
        run(sizes[0])
    else:
        number = n_ref[tile]
        for size in sizes:
            pl.when(number == size // TILE)(functools.partial(run, size))


def attend_forward(queries, keys, values, qid, kid, numbers, causal, sizes, ends):
    rows, width = queries.shape
    tiles = rows // TILE
    pairs = width // LANES
    key_rows = keys.shape[0]
    span = max(sizes)
    flops = 4 * rows * span * width
    return pl.pallas_call(
        functools.partial(forward_kernel, causal, sizes, ends),
        grid_spec=pltpu.PrefetchScalarGridSpec(
            num_scalar_prefetch=1,
            grid=(pairs, tiles),
            in_specs=[
                pl.BlockSpec((TILE, 1), lambda h, t, n: (t, 0)),
                pl.BlockSpec((tiles, 1, span), lambda h, t, n: (0, 0, 0)),
                pl.BlockSpec((TILE, LANES), lambda h, t, n: (t, h)),
                pl.BlockSpec((key_rows, LANES), lambda h, t, n: (0, h)),
                pl.BlockSpec((key_rows, LANES), lambda h, t, n: (0, h)),
            ],
            out_specs=[
                pl.BlockSpec((TILE, LANES), lambda h, t, n: (t, h)),
                pl.BlockSpec((1, TILE, LANES), lambda h, t, n: (h, t, 0)),
            ],
            scratch_shapes=[pltpu.VMEM((tiles, TILE, span), F32)],
        ),
        out_shape=[
            jax.ShapeDtypeStruct((rows, width), BF16),
            jax.ShapeDtypeStruct((pairs, rows, LANES), F32),
        ],
        compiler_params=pltpu.CompilerParams(vmem_limit_bytes=48 << 20),
        cost_estimate=pl.CostEstimate(flops=4 * flops, bytes_accessed=8 << 20, transcendentals=rows * span * HEADS),
    )(numbers, qid, kid, queries, keys, values)


def backward_kernel(
    causal, sizes, ends, n_ref, qid_ref, kid_ref, q_ref, k_ref, v_ref, g_ref, o_ref, lse_ref,
    dq_ref, dk_ref, dv_ref, bias_ref, dk_sum, dv_sum,
):
    tile = pl.program_id(1)
    tiles = pl.num_programs(1)
    span = bias_ref.shape[1]

    @pl.when(pl.program_id(0) == 0)
    def _():
        kid = kid_ref[tile]
        qid = qid_ref[...]
        allowed = kid == qid
        if causal:
            kpos = lax.broadcasted_iota(jnp.int32, (span, TILE), 0)
            qpos = lax.broadcasted_iota(jnp.int32, (span, TILE), 1) + (span - TILE)
            allowed = allowed & (kpos <= qpos)
        bias_ref[tile] = jnp.where(allowed, 0.0, NEG)

    @pl.when(tile == 0)
    def _():
        dk_sum[...] = jnp.zeros_like(dk_sum)
        dv_sum[...] = jnp.zeros_like(dv_sum)

    def run(size):
        start = pl.multiple_of(ends[0] + tile * ends[1] - size, TILE)
        window = pl.ds(start, size)
        keys = k_ref[window, :]
        values = v_ref[window, :]
        query = q_ref[...] * jnp.asarray(0.125, BF16)
        grad = g_ref[...]
        inner = grad.astype(F32) * o_ref[...].astype(F32)
        lse_rows = jnp.transpose(lse_ref[0])
        inner_rows = jnp.transpose(inner)
        half_lanes = LANES // 2
        parts_dq = []
        dk = None
        dv = None
        for half in range(2):
            head_q = head_lanes(query, half)
            head_g = head_lanes(grad, half)
            lse = lse_rows[half * half_lanes : half * half_lanes + 1, :]
            delta = jnp.sum(inner_rows[half * half_lanes : (half + 1) * half_lanes, :], axis=0, keepdims=True)
            scores = lax.dot_general(keys, head_q, NT, preferred_element_type=F32)
            probs = jnp.exp(scores + bias_ref[tile, span - size :, :] - lse)
            grad_probs = lax.dot_general(values, head_g, NT, preferred_element_type=F32)
            grad_scores = (probs * (grad_probs - delta)).astype(BF16)
            probs = probs.astype(BF16)
            part_k = jnp.dot(grad_scores, head_q, preferred_element_type=F32)
            part_v = jnp.dot(probs, head_g, preferred_element_type=F32)
            dk = part_k if dk is None else dk + part_k
            dv = part_v if dv is None else dv + part_v
            parts_dq.append(lax.dot_general(grad_scores, keys, TN, preferred_element_type=F32))
        lane = lax.broadcasted_iota(jnp.int32, (TILE, LANES), 1)
        dq_ref[...] = (jnp.where(lane < half_lanes, parts_dq[0], parts_dq[1]) * 0.125).astype(BF16)
        dk_sum[window, :] += dk
        dv_sum[window, :] += dv

    if len(sizes) == 1:
        run(sizes[0])
    else:
        number = n_ref[tile]
        for size in sizes:
            pl.when(number == size // TILE)(functools.partial(run, size))

    @pl.when(tile == tiles - 1)
    def _():
        dk_ref[...] = dk_sum[...].astype(BF16)
        dv_ref[...] = dv_sum[...].astype(BF16)


def attend_backward(queries, keys, values, grad, out, lse, qid, kid, numbers, causal, sizes, ends):
    rows, width = queries.shape
    tiles = rows // TILE
    pairs = width // LANES
    key_rows = keys.shape[0]
    span = max(sizes)
    flops = 10 * rows * span * width
    near = pl.BlockSpec((TILE, LANES), lambda h, t, n: (t, h))
    wide = pl.BlockSpec((key_rows, LANES), lambda h, t, n: (0, h))
    return pl.pallas_call(
        functools.partial(backward_kernel, causal, sizes, ends),
        grid_spec=pltpu.PrefetchScalarGridSpec(
            num_scalar_prefetch=1,
            grid=(pairs, tiles),
            in_specs=[
                pl.BlockSpec((1, TILE), lambda h, t, n: (0, t)),
                pl.BlockSpec((tiles, span, 1), lambda h, t, n: (0, 0, 0)),
                near,
                wide,
                wide,
                near,
                near,
                pl.BlockSpec((1, TILE, LANES), lambda h, t, n: (h, t, 0)),
            ],
            out_specs=[near, wide, wide],
            scratch_shapes=[
                pltpu.VMEM((tiles, span, TILE), F32),
                pltpu.VMEM((key_rows, LANES), F32),
                pltpu.VMEM((key_rows, LANES), F32),
            ],
        ),
        out_shape=[
            jax.ShapeDtypeStruct((rows, width), BF16),
            jax.ShapeDtypeStruct((key_rows, width), BF16),
            jax.ShapeDtypeStruct((key_rows, width), BF16),
        ],
        compiler_params=pltpu.CompilerParams(vmem_limit_bytes=48 << 20),
        cost_estimate=pl.CostEstimate(flops=4 * flops, bytes_accessed=12 << 20, transcendentals=rows * span * HEADS),
    )(numbers, qid, kid, queries, keys, values, grad, out, lse)


def factors(count):
    return {32: (4, 2, 2, 2), 128: (4, 4, 4, 2)}.get(count, (count,))


def coordinates(count):
    sizes = factors(count)
    left = lax.axis_index(AXIS)
    places = []
    for size in reversed(sizes):
        places.insert(0, lax.rem(left, size))
        left = lax.div(left, size)
    return places


def peers_along(count, axis, step):
    sizes = factors(count)
    stride = 1
    for size in sizes[axis + 1 :]:
        stride *= size
    size = sizes[axis]
    pairs = []
    for device in range(count):
        place = (device // stride) % size
        pairs.append((device, device + ((place + step) % size - place) * stride))
    return pairs


def take(value, place, axis):
    return lax.dynamic_slice_in_dim(value, place, 1, axis)


def total(terms):
    summed = terms[0].astype(F32)
    for term in terms[1:]:
        summed = summed + term.astype(F32)
    return summed


def reduce_scatter(value, order, kind, count):
    sizes = factors(count)
    places = coordinates(count)
    rows, width = value.shape
    terms = [value.reshape(*sizes, rows // count, width)]
    for axis in order:
        size = sizes[axis]
        arrived = []
        for step in range(1, size):
            other = lax.rem(places[axis] + step, size)
            sent = total([take(term, other, axis) for term in terms]).astype(kind)
            arrived.append(lax.ppermute(sent, AXIS, peers_along(count, axis, step)))
        terms = [take(term, places[axis], axis) for term in terms] + arrived
    return total(terms).reshape(rows // count, width)


def all_gather(value, order, count):
    sizes = factors(count)
    places = coordinates(count)
    rows, width = value.shape
    held = value.reshape(*([1] * len(sizes)), rows, width)
    for axis in order:
        size = sizes[axis]
        shape = list(held.shape)
        shape[axis] = size
        gathered = lax.dynamic_update_slice_in_dim(jnp.zeros(shape, held.dtype), held, places[axis], axis)
        for step in range(1, size):
            arrived = lax.ppermute(held, AXIS, peers_along(count, axis, step))
            source = lax.rem(places[axis] + size - step, size)
            gathered = lax.dynamic_update_slice_in_dim(gathered, arrived, source, axis)
        held = gathered
    return held.reshape(rows * count, width)


def matmul(left, right):
    return jnp.dot(left, right, preferred_element_type=F32)


def left_product(left, right):
    return lax.dot_general(left, right, TN, preferred_element_type=F32)


def right_product(left, right):
    return lax.dot_general(left, right, NT, preferred_element_type=F32)


def normalise(value):
    mean = jnp.mean(value, axis=-1, keepdims=True)
    centred = value - mean
    scale = lax.rsqrt(jnp.mean(centred * centred, axis=-1, keepdims=True) + EPS)
    return centred * scale, scale


def norm_back(grad, unit, scale, gain):
    scaled = grad * gain
    return scale * (
        scaled
        - jnp.mean(scaled, axis=-1, keepdims=True)
        - unit * jnp.mean(scaled * unit, axis=-1, keepdims=True)
    )


GELU_A = 0.7978845608028654
GELU_B = 0.044715


def gelu_and_slope(value):
    square = value * value
    bend = jnp.tanh(GELU_A * (value + GELU_B * value * square))
    gate = 0.5 * (1.0 + bend)
    slope = gate + value * 0.5 * (1.0 - bend * bend) * (GELU_A * (1.0 + 3.0 * GELU_B * square))
    return value * gate, slope


def body(
    tokens, out_grad, caption_states,
    query_weight, key_weight, value_weight, output_weight,
    cross_query, cross_key, cross_value, cross_output,
    up_weight, down_weight,
    attn_gain, attn_bias, cross_gain, cross_bias, mlp_gain, mlp_bias,
    item_ids, caption_segments, item_rows, item_segments,
):
    device = lax.axis_index(AXIS)
    count = lax.axis_size(AXIS)
    rows = tokens.shape[0]
    tiles = rows // TILE
    odd = lax.rem(device, 2) == 1
    swap = [(i, i ^ 1) for i in range(count)]
    ahead = [(i, i + 2) for i in range(count - 2)]
    behind = [(i + 2, i) for i in range(count - 2)]

    block_two = lax.ppermute(tokens, AXIS, ahead)
    block_one = lax.ppermute(jnp.where(odd, block_two, tokens), AXIS, swap)
    near_tokens = jnp.concatenate([block_two, block_one, tokens], 0)

    all_ids = jnp.concatenate([jnp.full((REACH * rows,), -1, jnp.int32), item_ids])
    near_ids = lax.dynamic_slice_in_dim(all_ids, device * rows, (REACH + 1) * rows)
    own_ids = near_ids[REACH * rows :]
    near_rows = (REACH + 1) * rows
    span = REACH * rows + TILE
    windows = jnp.stack([near_ids[t * TILE : t * TILE + span] for t in range(tiles)])
    firsts = own_ids[::TILE]
    before = jnp.sum((near_ids[None, :] < firsts[:, None]).astype(jnp.int32), axis=1)
    lasts = REACH * rows + TILE * (1 + jnp.arange(tiles, dtype=jnp.int32))
    numbers = lasts // TILE - before // TILE
    numbers = jnp.clip(numbers, 1, span // TILE)
    self_sizes = tuple(TILE * (i + 1) for i in range(span // TILE))
    self_ends = (REACH * rows + TILE, TILE)

    text = caption_states.shape[0]
    caption_len = caption_segments.shape[1]
    member = own_ids[:, None] == jnp.arange(item_rows.shape[0], dtype=jnp.int32)[None, :]
    codes = item_rows * caption_len + item_segments
    query_code = jnp.sum(jnp.where(member, codes[None, :], 0), axis=1)
    key_code = (jnp.arange(text, dtype=jnp.int32) // caption_len) * caption_len + caption_segments.reshape(-1)
    text_code = jnp.broadcast_to(key_code[None], (tiles, text))
    no_numbers = jnp.zeros((tiles,), jnp.int32)
    text_ends = (text, 0)

    inputs = tokens.astype(F32)
    near_unit, near_scale = normalise(near_tokens.astype(F32))
    near_low = (near_unit * attn_gain + attn_bias).astype(BF16)
    low_one = near_low[REACH * rows :]
    queries = matmul(low_one, query_weight).astype(BF16)
    near_keys = matmul(near_low, key_weight).astype(BF16)
    near_values = matmul(near_low, value_weight).astype(BF16)
    self_att, self_lse = attend_forward(
        queries, near_keys, near_values, own_ids[:, None], windows[:, None, :], numbers, True, self_sizes, self_ends
    )
    after_one = inputs + matmul(self_att, output_weight)
    unit_two, scale_two = normalise(after_one)
    low_two = (unit_two * cross_gain + cross_bias).astype(BF16)
    cross_q = matmul(low_two, cross_query).astype(BF16)
    text_keys = matmul(caption_states, cross_key).astype(BF16)
    text_values = matmul(caption_states, cross_value).astype(BF16)
    cross_att, cross_lse = attend_forward(
        cross_q, text_keys, text_values, query_code[:, None], text_code[:, None, :], no_numbers, False, (text,), text_ends
    )
    after_two = after_one + matmul(cross_att, cross_output)
    unit_three, scale_three = normalise(after_two)
    low_three = (unit_three * mlp_gain + mlp_bias).astype(BF16)
    hidden_pre = matmul(low_three, up_weight)
    hidden, slope = gelu_and_slope(hidden_pre)
    hidden_low = hidden.astype(BF16)
    block_output = (after_two + matmul(hidden_low, down_weight)).astype(BF16)

    grad_pre = (slope * right_product(out_grad, down_weight)).astype(BF16)
    down_grad = left_product(hidden_low, out_grad).astype(BF16)
    up_grad = left_product(low_three, grad_pre).astype(BF16)
    z_, y_, x_, c_ = 0, 1, 2, 3
    one_way = (c_, x_, y_, z_) if len(factors(count)) == 4 else (0,)
    other_way = (c_, y_, x_, z_) if len(factors(count)) == 4 else (0,)
    down_out = reduce_scatter(down_grad, one_way, BF16, count)
    up_out = reduce_scatter(up_grad, other_way, BF16, count)
    grad_three = right_product(grad_pre, up_weight)
    mlp_gain_grad = jnp.sum(grad_three * unit_three, axis=0)
    mlp_bias_grad = jnp.sum(grad_three, axis=0)
    grad_two = out_grad.astype(F32) + norm_back(grad_three, unit_three, scale_three, mlp_gain)
    grad_two_low = grad_two.astype(BF16)

    cross_output_grad = left_product(cross_att, grad_two_low).astype(BF16)
    grad_cross = right_product(grad_two_low, cross_output).astype(BF16)
    grad_cq, grad_tk, grad_tv = attend_backward(
        cross_q, text_keys, text_values, grad_cross, cross_att, cross_lse,
        query_code[None, :], text_code[:, :, None], no_numbers, False, (text,), text_ends,
    )
    own_text = reduce_scatter(jnp.concatenate([grad_tk, grad_tv], 1), one_way, BF16, count).astype(BF16)
    width = grad_tk.shape[1]
    caption_grad = right_product(own_text[:, :width], cross_key) + right_product(own_text[:, width:], cross_value)
    all_text = all_gather(own_text, one_way[::-1], count)
    share = width // count
    caption_part = lax.dynamic_slice_in_dim(caption_states, device * share, share, 1)
    text_weight_grads = left_product(caption_part, all_text)
    cross_key_grad = text_weight_grads[:, :width]
    cross_value_grad = text_weight_grads[:, width:]
    cross_query_grad = left_product(low_two, grad_cq).astype(BF16)
    grad_norm_two = right_product(grad_cq, cross_query)
    cross_gain_grad = jnp.sum(grad_norm_two * unit_two, axis=0)
    cross_bias_grad = jnp.sum(grad_norm_two, axis=0)
    grad_one = grad_two + norm_back(grad_norm_two, unit_two, scale_two, cross_gain)
    grad_one_low = grad_one.astype(BF16)

    output_weight_grad = left_product(self_att, grad_one_low).astype(BF16)
    middle = reduce_scatter(
        jnp.concatenate([cross_output_grad, cross_query_grad, output_weight_grad], 1), other_way, BF16, count
    )
    grad_self = right_product(grad_one_low, output_weight).astype(BF16)
    grad_q, grad_k, grad_v = attend_backward(
        queries, near_keys, near_values, grad_self, self_att, self_lse,
        own_ids[None, :], windows[:, :, None], numbers, True, self_sizes, self_ends,
    )
    grad_near = right_product(grad_k, key_weight) + right_product(grad_v, value_weight)
    grad_own = grad_near[REACH * rows :] + right_product(grad_q, query_weight)
    to_two = grad_near[:rows]
    to_one = grad_near[rows : REACH * rows].astype(BF16)
    from_swap = lax.ppermute(to_one, AXIS, swap).astype(F32)
    to_two = (to_two + jnp.where(odd, from_swap, 0.0)).astype(BF16)
    from_two = lax.ppermute(to_two, AXIS, behind).astype(F32)
    near_sum = jnp.concatenate([grad_near[: REACH * rows], grad_own], 0)
    attn_gain_grad = jnp.sum(near_sum * near_unit, axis=0)
    attn_bias_grad = jnp.sum(near_sum, axis=0)
    grad_norm_one = grad_own + from_two + jnp.where(odd, 0.0, from_swap)
    unit_one = near_unit[REACH * rows :]
    input_grad = grad_one + norm_back(grad_norm_one, unit_one, near_scale[REACH * rows :], attn_gain)
    query_grad = left_product(low_one, grad_q).astype(BF16)
    key_grad = left_product(near_low, grad_k).astype(BF16)
    value_grad = left_product(near_low, grad_v).astype(BF16)
    late = reduce_scatter(jnp.concatenate([query_grad, key_grad, value_grad], 1), one_way, BF16, count)
    vectors = jnp.stack(
        [attn_gain_grad, attn_bias_grad, cross_gain_grad, cross_bias_grad, mlp_gain_grad, mlp_bias_grad], 1
    )
    small = reduce_scatter(vectors, one_way, F32, count)
    return (
        block_output,
        input_grad,
        caption_grad,
        late[:, :width],
        late[:, width : 2 * width],
        late[:, 2 * width :],
        middle[:, 2 * width :],
        middle[:, width : 2 * width],
        cross_key_grad,
        cross_value_grad,
        middle[:, :width],
        up_out,
        down_out,
        small[:, 0],
        small[:, 1],
        small[:, 2],
        small[:, 3],
        small[:, 4],
        small[:, 5],
    )


def solution(mesh):
    split = P(AXIS, None)
    return jax.shard_map(
        body,
        mesh=mesh,
        in_specs=(split, split) + (P(),) * 21,
        out_specs=(split,) * 13 + (P(AXIS),) * 6,
        check_vma=False,
    )
```

time: 2060 us -> 668 us (0.32)
  waiting for transfers between devices: 1120 us -> 231 us
  matrix products: 589 us -> 131 us
  blocking collectives: 122 us -> 0 us
  Pallas kernels: 0 us -> 75.8 us
  local copies, waits for them, and re-layouts: 129 us -> 54 us
  starting transfers between devices: 22 us -> 77 us
  other arithmetic: 48.7 us -> 92.6 us
    reduce_scatter x10 -> x0, waiting for transfers between devices: 1070 us -> none  [the longest x1 187 us: body(): lax.psum_scatter(down_grad, 'seq', scatter_dimension=0, tiled=True)]
    dot_general x254 -> x29, matrix products: 589 us -> 131 us  [the longest x10 44.8 us: right_product(): return lax.dot_general(left, right, NT, preferred_element_type=F32)]
    ppermute x8 -> x46, waiting for transfers between devices: 58.2 us -> 231 us  [the longest x36 185 us: reduce_scatter(): arrived.append(lax.ppermute(sent, AXIS, peers_along(count, axis, step)))]
    psum x1 -> x0, blocking collectives: 122 us -> none  [body(): summed_tk, summed_tv = lax.psum((grad_tk, grad_tv), 'seq')]
    pallas_call x0 -> x4, Pallas kernels: none -> 75.8 us  [the longest x2 43.9 us: attend_backward(): pl.pallas_call(functools.partial(backward_kernel, causal, sizes, ends), g...]
    ppermute x8 -> x46, starting transfers between devices: 21.3 us -> 77 us  [the longest x36 69.2 us: reduce_scatter(): arrived.append(lax.ppermute(sent, AXIS, peers_along(count, axis, step)))]
    while x64 -> x0, local copies, waits for them, and re-layouts: 41.9 us -> none
    unnamed x127 -> x150, local copies, waits for them, and re-layouts: 46.1 us -> 8.42 us
  transfers between devices with their start and end apart: 18 -> 46, of which waited for: 9 -> 26; matrix products, arithmetic and copies ran while one was open for 17% -> 19% of each run, Pallas kernels for 0% -> 0%
where the time goes in v1:
time: 668 us; the launch traced here: 664 us
  waiting for transfers between devices  231 us (35%)
  matrix products  131 us (20%)
  other arithmetic  92.6 us (14%)
  starting transfers between devices  77 us (12%)
  Pallas kernels  75.8 us (11%)
  local copies, waits for them, and re-layouts  54 us (8%)
    ppermute x36, waiting for transfers between devices, reduce_scatter(): arrived.append(lax.ppermute(sent, AXIS, peers_along(count, axis, step)))  185 us
    ppermute x36, starting transfers between devices, reduce_scatter(): arrived.append(lax.ppermute(sent, AXIS, peers_along(count, axis, step)))  69.2 us
    dot_general x10, matrix products, right_product(): return lax.dot_general(left, right, NT, preferred_element_type=F32)  44.8 us
    pallas_call x2, Pallas kernels, attend_backward(): pl.pallas_call(functools.partial(backward_kernel, causal, sizes, ends), g...  43.9 us
    dot_general x9, matrix products, left_product(): return lax.dot_general(left, right, TN, preferred_element_type=F32)  43.8 us
    dot_general x10, matrix products, matmul(): return jnp.dot(left, right, preferred_element_type=F32)  42.1 us
    pallas_call x2, Pallas kernels, attend_forward(): pl.pallas_call(functools.partial(forward_kernel, causal, sizes, ends), gr...  32 us
    convert_element_type x15, other arithmetic, reduce_scatter(): sent = total([take(term, other, axis) for term in terms]).astype(kind)  28.4 us
  transfers between devices with their start and end apart: 46, of which 26 were waited for; matrix products, arithmetic and copies ran while one was open for 19% of the time, Pallas kernels for 0%

profile of v1, /device:TPU:0, one launch (start us, length us, event | category | flops | bytes accessed | tf_op | source)
XLA Modules:
  0.0 663.5 jit_solution(16665030575978234758)
XLA Ops:
  0.7 5.0 collective-permute-start
  9.2 19.2 %collective-permute-done = bf16[512,1024]{1,0:T(8,128)(2,1)S(1)} collective-permute-done((bf16[512,1024]{1,0:T(8,128)(2,1)}, bf16[512,1024]{1,0:T(8,128)(2,1)S(1)}, u32[]{:S(2)}, u32[]{:S(2)}) %collective-permute-start) | collective-permute-done | bytes 1048608 | tf_op jit(solution)/shard_map/ppermute | solution.py:349
  33.4 3.3 convolution_convert_fusion.13.k_ref
  40.4 4.0 fusion.2
  44.5 4.0 add_convert_fusion
  51.3 4.8 convolution_convert_fusion.2.v_ref
  56.0 4.8 convolution_convert_fusion.3.k_ref
  60.8 16.9 %shard_map.366 = (bf16[512,1024]{1,0:T(8,128)(2,1)S(1)}, f32[8,512,128]{2,1,0:T(8,128)S(1)}) custom-call(s32[2]{0:T(128)S(1)} %subtract_clamp_fusion.n_ref, s32[512,1]{1,0:T(8,128)S(1)} %copy-done.2, s32[2,1,1280]{2,1,0:T(1,128)S(1)} %broadcast_in_dim.37.kid_ref, bf16[512,1024]{1,0:T(8,128)(2,1)S(1)} %convolution_convert_fusion.15.q_ref, ...), custom_call_target="tpu_custom_call" | custom-call | flops 10737418240 | bytes 8388608 | tf_op jit(solution)/shard_map/pallas_call | solution.py:81
  77.7 3.7 fusion.52
  85.2 15.1 %shard_map.367 = (bf16[512,1024]{1,0:T(8,128)(2,1)S(1)}, f32[8,512,128]{2,1,0:T(8,128)}) custom-call(s32[2]{0:T(128)S(1)} %broadcast.194.n_ref, s32[512,1]{1,0:T(8,128)S(1)} %copy-done.1, s32[2,1,512]{2,1,0:T(1,128)S(1)} %broadcast_in_dim_broadcast_in_dim.4.kid_ref, bf16[512,1024]{1,0:T(8,128)(2,1)S(1)} %convolution_convert_fusion.14.q_ref, ...), custom_call_target="tpu_custom_call" | custom-call | flops 4294967296 | bytes 8388608 | tf_op jit(solution)/shard_map/pallas_call | solution.py:81
  102.4 10.6 %fusion.46 = f32[512,4096]{1,0:T(8,128)} fusion(bf16[1024,4096]{1,0:T(8,128)(2,1)} %param.34, f32[512,1024]{1,0:T(8,128)S(1)} %get-tuple-element.96, f32[1024]{0:T(1024)S(1)} %copy-done.58, f32[1024]{0:T(1024)S(1)} %copy-done.46, f32[512]{0:T(512)S(1)} %add_rsqrt_fusion.1, f32[512]{0:T(512)S(1)} %broadcast_multiply_fusion.7), kind=kOutput, calls=%fused_computation.209 | convolution fusion | flops 4297588736 | bytes 18886656 | tf_op jit(solution)/shard_map/dot_general | solution.py:293
  113.0 9.7 %add_convert_fusion.7 = bf16[512,1024]{1,0:T(8,128)(2,1)} fusion(f32[512,1024]{1,0:T(8,128)S(1)} %get-tuple-element.96, bf16[4096,1024]{1,0:T(8,128)(2,1)S(1)} %bitcast.123, f32[512,4096]{1,0:T(8,128)} %fusion.46), kind=kOutput, calls=%fused_computation.44 | convolution fusion | flops 4314890240 | bytes 19922944 | tf_op jit(solution)/shard_map/dot_general | solution.py:293
  122.7 14.5 %multiply_convert_fusion = bf16[512,4096]{1,0:T(8,128)(2,1)} fusion(f32[512,4096]{1,0:T(8,128)} %fusion.46, bf16[512,1024]{1,0:T(8,128)(2,1)S(1)} %copy-done.30, bf16[4096,1024]{1,0:T(8,128)(2,1)} %param.35), kind=kOutput, calls=%fused_computation | convolution fusion | flops 4332716032 | bytes 22020096 | tf_op jit(solution)/shard_map/dot_general | solution.py:301
  137.2 12.7 %convolution_convert_fusion = bf16[4096,1024]{1,0:T(8,128)(2,1)} fusion(bf16[512,1024]{1,0:T(8,128)(2,1)S(1)} %copy-done.30, f32[512,4096]{1,0:T(8,128)} %fusion.46), kind=kOutput, calls=%fused_computation.7 | convolution fusion | flops 4318035968 | bytes 17825792 | tf_op jit(solution)/shard_map/dot_general | solution.py:297
  149.9 9.3 %multiply_reduce_fusion = (f32[1024]{0:T(1024)S(1)}, f32[512]{0:T(512)S(1)}, f32[512]{0:T(512)S(1)}, f32[1024]{0:T(1024)S(1)}, f32[512,1024]{1,0:T(8,128)S(1)}) fusion(f32[512,1024]{1,0:T(8,128)S(1)} %get-tuple-element.96, f32[512]{0:T(512)S(1)} %add_rsqrt_fusion.1, f32[512]{0:T(512)S(1)} %broadcast_multiply_fusion.7, f32[1024]{0:T(1024)S(1)} %copy-done.46, ...), kind=kOutput, calls=%fused_computation.34 | convolution fusion | flops 4299682816 | bytes 16797696 | tf_op jit(solution)/shard_map/dot_general | solution.py:301
  165.7 7.2 %convolution_convert_fusion.1 = bf16[1024,4096]{1,0:T(8,128)(2,1)} fusion(bf16[512,4096]{1,0:T(8,128)(2,1)S(1)} %copy-done.62, f32[512,1024]{1,0:T(8,128)S(1)} %get-tuple-element.96, f32[1024]{0:T(1024)S(1)} %copy-done.58, f32[1024]{0:T(1024)S(1)} %copy-done.46, f32[512]{0:T(512)S(1)} %add_rsqrt_fusion.1, f32[512]{0:T(512)S(1)} %broadcast_multiply_fusion.7), kind=kOutput, calls=%fused_computation.8 | convolution fusion | flops 4301783040 | bytes 14692352 | tf_op jit(solution)/shard_map/dot_general | solution.py:297
  173.0 21.5 %shard_map.368 = (bf16[512,1024]{1,0:T(8,128)(2,1)S(1)}, bf16[512,1024]{1,0:T(8,128)(2,1)S(1)}, bf16[512,1024]{1,0:T(8,128)(2,1)S(1)}) custom-call(s32[2]{0:T(128)S(1)} %broadcast.194.n_ref, s32[1,512]{1,0:T(1,128)S(1)} %bitcast.83, s32[2,512,1]{2,1,0:T(8,128)S(1)} %broadcast_in_dim_broadcast_in_dim.5.kid_ref, ...), custom_call_target="tpu_custom_call" | custom-call | flops 10737418240 | bytes 12582912 | tf_op jit(solution)/shard_map/pallas_call | solution.py:188
  204.8 22.4 %shard_map.369 = (bf16[512,1024]{1,0:T(8,128)(2,1)S(1)}, bf16[1536,1024]{1,0:T(8,128)(2,1)}, bf16[1536,1024]{1,0:T(8,128)(2,1)}) custom-call(s32[2]{0:T(128)S(1)} %subtract_clamp_fusion.n_ref, s32[1,512]{1,0:T(1,128)S(1)} %bitcast.81, s32[2,1280,1]{2,1,0:T(8,128)S(1)} %copy.64.kid_ref, bf16[512,1024]{1,0:T(8,128)(2,1)S(1)} %convolution_convert_fusion.15.q_ref, ...), custom_call_target="tpu_custom_call" | custom-call | flops 26843545600 | bytes 12582912 | tf_op jit(solution)/shard_map/pallas_call | solution.py:188
  227.2 6.8 %convolution_convert_fusion.8 = bf16[1024,1024]{0,1:T(8,128)(2,1)} fusion(bf16[1536,1024]{1,0:T(8,128)(2,1)S(1)} %copy-done.25, bf16[1536,1024]{1,0:T(8,128)(2,1)} %get-tuple-element.34), kind=kOutput, calls=%fused_computation.56 | convolution fusion | flops 3222274048 | bytes 8388608 | tf_op jit(solution)/shard_map/dot_general | solution.py:297
  234.0 3.5 fusion.54
  237.5 5.0 convolution_convert_fusion.7
  245.1 3.5 convolution_add_fusion
  248.6 3.2 slice_add_fusion
  252.9 3.2 slice_reduce_fusion
  258.7 5.5 collective-permute-start.4
  264.2 13.6 %pad_maximum_fusion.1 = bf16[1024,3072]{0,1:T(8,128)(2,1)} fusion(bf16[1024,1024]{0,1:T(8,128)(2,1)S(1)} %copy-done.29, bf16[1024,1024]{0,1:T(8,128)(2,1)S(1)} %copy-done.28, bf16[1024,1024]{0,1:T(8,128)(2,1)S(1)} %copy-done.27), kind=kLoop, calls=%fused_computation.13 | loop fusion | flops 18874368 | bytes 12582912 | tf_op jit(solution)/shard_map/concatenate | solution.py:442
  277.8 8.6 %copy.66 = bf16[1024,3072]{1,0:T(8,128)(2,1)} copy(bf16[1024,3072]{0,1:T(8,128)(2,1)} %pad_maximum_fusion.1) | data formatting | bytes 12582912 | tf_op jit(solution)/shard_map/concatenate | solution.py:442
  286.4 6.0 pad_maximum_fusion
  292.4 8.6 %copy.65 = bf16[1024,3072]{1,0:T(8,128)(2,1)} copy(bf16[1024,3072]{0,1:T(8,128)(2,1)} %pad_maximum_fusion) | data formatting | bytes 12582912 | tf_op jit(solution)/shard_map/concatenate | solution.py:465
  302.4 3.9 constant_dynamic-slice_fusion.10
  307.3 6.9 %fusion.3 = (f32[1024]{0:T(1024)}, f32[1536,1024]{1,0:T(8,128)}) fusion(f32[512,1024]{1,0:T(8,128)} %slice_add_fusion, f32[1024,1024]{1,0:T(8,128)S(1)} %copy-done.13, f32[1536]{0:T(1024)S(1)} %copy-done.36, f32[1536]{0:T(1024)S(1)} %copy-done.34, bf16[512,1024]{1,0:T(8,128)(2,1)S(1)} %copy-done.9, bf16[512,1024]{1,0:T(8,128)(2,1)} %collective-permute-done.1, ...), kind=kLoop, calls=%fused_computation.15 | loop fusion | flops 17300480 | bytes 15745024 | tf_op jit(solution)/shard_map/reduce_sum | solution.py:457
  321.7 4.9 constant_dynamic-slice_fusion.23
  326.6 7.7 %collective-permute-done.5 = bf16[4,2,1,1,16,2048]{5,4,3,2,1,0:T(8,128)(2,1)S(1)} collective-permute-done((bf16[4,2,1,1,16,2048]{5,4,3,2,1,0:T(8,128)(2,1)S(1)}, bf16[4,2,1,1,16,2048]{5,4,3,2,1,0:T(8,128)(2,1)S(1)}, u32[]{:S(2)}, u32[]{:S(2)}) %collective-permute-start.5) | collective-permute-done | bytes 524320 | tf_op jit(solution)/shard_map/ppermute | solution.py:269
  335.6 10.6 %collective-permute-start.6 = (bf16[4,1,1,1,16,2048]{5,4,3,2,1,0:T(8,128)(2,1)S(1)}, bf16[4,1,1,1,16,2048]{5,4,3,2,1,0:T(8,128)(2,1)S(1)}, u32[]{:S(2)}, u32[]{:S(2)}) collective-permute-start(bf16[4,1,1,1,16,2048]{5,4,3,2,1,0:T(8,128)(2,1)S(1)} %add_convert_fusion.19), channel_id=1, source_target_pairs={{0,4},{1,5},{2,6},{3,7},{4,0},{5,1},{6,2},{7,3},{8,12},{9,13},{10,... | collective-permute-start | bytes 786440 | tf_op jit(solution)/shard_map/ppermute | solution.py:269
  353.6 3.5 collective-permute-start.7
  357.2 8.5 %collective-permute-start.9 = (bf16[1,1,1,1,16,2048]{5,4,3,2,1,0:T(8,128)(2,1)S(1)}, bf16[1,1,1,1,16,2048]{5,4,3,2,1,0:T(8,128)(2,1)S(1)}, u32[]{:S(2)}, u32[]{:S(2)}) collective-permute-start(bf16[1,1,1,1,16,2048]{5,4,3,2,1,0:T(8,128)(2,1)S(1)} %get-tuple-element.67), channel_id=1, source_target_pairs={{0,24},{1,25},{2,26},{3,27},{4,28},{5,29},{6,30},{7,31},{8,0},{9,1... | collective-permute-start | bytes 196616 | tf_op jit(solution)/shard_map/ppermute | solution.py:269
  371.1 18.2 %collective-permute-done.7 = bf16[1,1,1,1,16,2048]{5,4,3,2,1,0:T(8,128)(2,1)S(1)} collective-permute-done((bf16[1,1,1,1,16,2048]{5,4,3,2,1,0:T(8,128)(2,1)S(1)}, bf16[1,1,1,1,16,2048]{5,4,3,2,1,0:T(8,128)(2,1)S(1)}, u32[]{:S(2)}, u32[]{:S(2)}) %collective-permute-start.7) | collective-permute-done | bytes 65568 | tf_op jit(solution)/shard_map/ppermute | solution.py:269
  393.9 4.4 fusion.47
  399.9 3.2 convolution_add_fusion.2
  403.1 3.5 collective-permute-done.40
  406.6 6.2 collective-permute-done.22
  412.8 3.9 collective-permute-done.41
  416.7 5.2 collective-permute-done.23
  421.9 3.7 collective-permute-done.42
  425.6 4.2 collective-permute-done.24
  429.9 5.4 collective-permute-done.43
  435.4 3.5 collective-permute-done.45
  438.9 6.3 collective-permute-done.25
  445.3 4.5 collective-permute-done.44
  449.8 3.5 multiply_add_fusion
  453.5 5.4 collective-permute-done.26
  461.9 3.3 add_convert_fusion.4
  475.7 23.4 %collective-permute-done.17 = bf16[4,1,2,1,32,3072]{5,4,3,2,1,0:T(8,128)(2,1)S(1)} collective-permute-done((bf16[4,1,2,1,32,3072]{5,4,3,2,1,0:T(8,128)(2,1)S(1)}, bf16[4,1,2,1,32,3072]{5,4,3,2,1,0:T(8,128)(2,1)S(1)}, u32[]{:S(2)}, u32[]{:S(2)}) %collective-permute-start.17) | collective-permute-done | bytes 1572896 | tf_op jit(solution)/shard_map/ppermute | solution.py:269
  508.4 55.4 %collective-permute-done.18 = bf16[4,1,1,1,32,3072]{5,4,3,2,1,0:T(8,128)(2,1)S(1)} collective-permute-done((bf16[4,1,1,1,32,3072]{5,4,3,2,1,0:T(8,128)(2,1)S(1)}, bf16[4,1,1,1,32,3072]{5,4,3,2,1,0:T(8,128)(2,1)S(1)}, u32[]{:S(2)}, u32[]{:S(2)}) %collective-permute-start.18) | collective-permute-done | bytes 786464 | tf_op jit(solution)/shard_map/ppermute | solution.py:269
  565.6 3.8 collective-permute-start.21
  570.9 4.3 collective-permute-done.19
  577.1 3.1 collective-permute-start.15
  580.2 12.0 %collective-permute-done.20 = bf16[1,1,1,1,32,3072]{5,4,3,2,1,0:T(8,128)(2,1)S(1)} collective-permute-done((bf16[1,1,1,1,32,3072]{5,4,3,2,1,0:T(8,128)(2,1)S(1)}, bf16[1,1,1,1,32,3072]{5,4,3,2,1,0:T(8,128)(2,1)S(1)}, u32[]{:S(2)}, u32[]{:S(2)}) %collective-permute-start.20) | collective-permute-done | bytes 196640 | tf_op jit(solution)/shard_map/ppermute | solution.py:269
  602.9 12.8 %collective-permute-done.36 = bf16[4,1,1,1,128,1024]{5,4,3,2,1,0:T(8,128)(2,1)S(1)} collective-permute-done((bf16[4,1,1,1,128,1024]{5,4,3,2,1,0:T(8,128)(2,1)S(1)}, bf16[4,1,1,1,128,1024]{5,4,3,2,1,0:T(8,128)(2,1)S(1)}, u32[]{:S(2)}, u32[]{:S(2)}) %collective-permute-start.36) | collective-permute-done | bytes 1048608 | tf_op jit(solution)/shard_map/ppermute | solution.py:269
  617.5 3.8 collective-permute-start.39
  623.9 3.8 collective-permute-start.33
  628.8 11.9 %collective-permute-start.32 = (bf16[1,1,1,1,32,4096]{5,4,3,2,1,0:T(8,128)(2,1)S(1)}, bf16[1,1,1,1,32,4096]{5,4,3,2,1,0:T(8,128)(2,1)S(1)}, u32[]{:S(2)}, u32[]{:S(2)}) collective-permute-start(bf16[1,1,1,1,32,4096]{5,4,3,2,1,0:T(8,128)(2,1)S(1)} %get-tuple-element.57), channel_id=1, source_target_pairs={{0,16},{1,17},{2,18},{3,19},{4,20},{5,21},{6,22},{7,23},{8,24},{9,... | collective-permute-start | bytes 786440 | tf_op jit(solution)/shard_map/ppermute | solution.py:269
  641.4 11.7 %collective-permute-done.38 = bf16[1,1,1,1,128,1024]{5,4,3,2,1,0:T(8,128)(2,1)S(1)} collective-permute-done((bf16[1,1,1,1,128,1024]{5,4,3,2,1,0:T(8,128)(2,1)S(1)}, bf16[1,1,1,1,128,1024]{5,4,3,2,1,0:T(8,128)(2,1)S(1)}, u32[]{:S(2)}, u32[]{:S(2)}) %collective-permute-start.38) | collective-permute-done | bytes 262176 | tf_op jit(solution)/shard_map/ppermute | solution.py:269
  655.1 6.2 collective-permute-done.32
  (323 shorter events, 122.7 us)
Async XLA Ops:
  0.7 55.4 %copy-start = (bf16[1024,1024]{1,0:T(8,128)(2,1)S(1)}, bf16[1024,1024]{1,0:T(8,128)(2,1)}, u32[]{:S(2)}) copy-start(bf16[1024,1024]{1,0:T(8,128)(2,1)} %param.27) | copy-start | bytes 6291460
  0.7 27.7 %collective-permute-start = (bf16[512,1024]{1,0:T(8,128)(2,1)}, bf16[512,1024]{1,0:T(8,128)(2,1)S(1)}, u32[]{:S(2)}, u32[]{:S(2)}) collective-permute-start(bf16[512,1024]{1,0:T(8,128)(2,1)} %param.23), channel_id=1, source_target_pairs={{0,2},{1,3},{2,4},{3,5},{4,6},{5,7},{6,8},{7,9},{8,10},{9,11},{10,... | collective-permute-start | bytes 3145736 | tf_op jit(solution)/shard_map/ppermute | solution.py:349
  6.5 26.4 %copy-start.3 = (s32[512]{0:T(512)}, s32[512]{0:T(512)S(1)}, u32[]{:S(2)}) copy-start(s32[512]{0:T(512)S(1)} %pad_dynamic-slice_fusion.2) | copy-start | bytes 6148
  9.2 24.2 %copy-start.48 = (s32[4,128]{1,0:T(4,128)S(1)}, s32[4,128]{1,0:T(4,128)}, u32[]{:S(2)}) copy-start(s32[4,128]{1,0:T(4,128)} %param.43) | copy-start | bytes 6148
  31.1 7.0 %collective-permute-start.1 = (bf16[512,1024]{1,0:T(8,128)(2,1)}, bf16[512,1024]{1,0:T(8,128)(2,1)}, u32[]{:S(2)}, u32[]{:S(2)}) collective-permute-start(bf16[512,1024]{1,0:T(8,128)(2,1)} %broadcast_select_fusion), channel_id=1, source_target_pairs={{0,1},{1,0},{2,3},{3,2},{4,5},{5,4},{6,7},{7,6},{8,9},{9,8},{10,11... | collective-permute-start | bytes 3145736 | tf_op jit(solution)/shard_map/ppermute | solution.py:350
  38.0 47.2 %copy-start.6 = (bf16[512,1024]{1,0:T(8,128)(2,1)}, bf16[512,1024]{1,0:T(8,128)(2,1)S(1)}, u32[]{:S(2)}) copy-start(bf16[512,1024]{1,0:T(8,128)(2,1)S(1)} %convolution_convert_fusion.12.v_ref) | copy-start | bytes 3145732
  100.3 62.7 %copy-start.5 = (bf16[512,1024]{1,0:T(8,128)(2,1)}, bf16[512,1024]{1,0:T(8,128)(2,1)S(1)}, u32[]{:S(2)}) copy-start(bf16[512,1024]{1,0:T(8,128)(2,1)S(1)} %get-tuple-element.30.o_ref) | copy-start | bytes 3145732
  204.8 22.4 %copy-start.25 = (bf16[1536,1024]{1,0:T(8,128)(2,1)S(1)}, bf16[1536,1024]{1,0:T(8,128)(2,1)}, u32[]{:S(2)}) copy-start(bf16[1536,1024]{1,0:T(8,128)(2,1)} %copy-done.24) | copy-start | bytes 9437188
  258.7 59.6 %collective-permute-start.4 = (bf16[4,2,2,1,16,2048]{5,4,3,2,1,0:T(8,128)(2,1)}, bf16[4,2,2,1,16,2048]{5,4,3,2,1,0:T(8,128)(2,1)}, u32[]{:S(2)}, u32[]{:S(2)}) collective-permute-start(bf16[4,2,2,1,16,2048]{5,4,3,2,1,0:T(8,128)(2,1)} %constant_dynamic-slice_fusion.26), channel_id=1, source_target_pairs={{0,1},{1,0},{2,3},{3,2},{4,5},{5,4},{6,7},{7,6},{8,9},{9,8},{10,11... | collective-permute-start | bytes 3145736 | tf_op jit(solution)/shard_map/ppermute | solution.py:269
  301.1 45.2 %collective-permute-start.2 = (bf16[512,1024]{1,0:T(8,128)(2,1)}, bf16[512,1024]{1,0:T(8,128)(2,1)S(1)}, u32[]{:S(2)}, u32[]{:S(2)}) collective-permute-start(bf16[512,1024]{1,0:T(8,128)(2,1)} %slice.147), channel_id=1, source_target_pairs={{0,1},{1,0},{2,3},{3,2},{4,5},{5,4},{6,7},{7,6},{8,9},{9,8},{10,11... | collective-permute-start | bytes 3145736 | tf_op jit(solution)/shard_map/ppermute | solution.py:453
  306.4 152.7 %collective-permute-start.16 = (bf16[4,2,2,1,32,3072]{5,4,3,2,1,0:T(8,128)(2,1)}, bf16[4,2,2,1,32,3072]{5,4,3,2,1,0:T(8,128)(2,1)}, u32[]{:S(2)}, u32[]{:S(2)}) collective-permute-start(bf16[4,2,2,1,32,3072]{5,4,3,2,1,0:T(8,128)(2,1)} %constant_dynamic-slice_fusion.10), channel_id=1, source_target_pairs={{0,1},{1,0},{2,3},{3,2},{4,5},{5,4},{6,7},{7,6},{8,9},{9,8},{10,11... | collective-permute-start | bytes 9437192 | tf_op jit(solution)/shard_map/ppermute | solution.py:269
  318.2 49.0 %slice-start.6 = ((s8[8388608]{0:T(1024)(128)(4,1)}), s8[4194304]{0:T(1024)(128)(4,1)S(1)}, s32[]{:S(2)}) async-start(s8[8388608]{0:T(1024)(128)(4,1)} %bitcast.110), calls=%async_computation.6 | async-start | bytes 8388608
  319.7 14.5 %collective-permute-start.5 = (bf16[4,2,1,1,16,2048]{5,4,3,2,1,0:T(8,128)(2,1)S(1)}, bf16[4,2,1,1,16,2048]{5,4,3,2,1,0:T(8,128)(2,1)S(1)}, u32[]{:S(2)}, u32[]{:S(2)}) collective-permute-start(bf16[4,2,1,1,16,2048]{5,4,3,2,1,0:T(8,128)(2,1)S(1)} %add_convert_fusion.12), channel_id=1, source_target_pairs={{0,2},{1,3},{2,0},{3,1},{4,6},{5,7},{6,4},{7,5},{8,10},{9,11},{10,... | collective-permute-start | bytes 1572872 | tf_op jit(solution)/shard_map/ppermute | solution.py:269
  321.7 45.6 %slice-start.7 = ((s8[8388608]{0:T(1024)(128)(4,1)}), s8[4194304]{0:T(1024)(128)(4,1)S(1)}, s32[]{:S(2)}) async-start(s8[8388608]{0:T(1024)(128)(4,1)} %bitcast.110), calls=%async_computation.7 | async-start | bytes 8388608
  334.3 18.2 %copy-start.31 = (bf16[4,2,1,1,16,2048]{5,4,3,2,1,0:T(8,128)(2,1)}, bf16[4,2,1,1,16,2048]{5,4,3,2,1,0:T(8,128)(2,1)S(1)}, u32[]{:S(2)}) copy-start(bf16[4,2,1,1,16,2048]{5,4,3,2,1,0:T(8,128)(2,1)S(1)} %collective-permute-done.5) | copy-start | bytes 1572868
  335.6 16.8 %collective-permute-start.6 = (bf16[4,1,1,1,16,2048]{5,4,3,2,1,0:T(8,128)(2,1)S(1)}, bf16[4,1,1,1,16,2048]{5,4,3,2,1,0:T(8,128)(2,1)S(1)}, u32[]{:S(2)}, u32[]{:S(2)}) collective-permute-start(bf16[4,1,1,1,16,2048]{5,4,3,2,1,0:T(8,128)(2,1)S(1)} %add_convert_fusion.19), channel_id=1, source_target_pairs={{0,4},{1,5},{2,6},{3,7},{4,0},{5,1},{6,2},{7,3},{8,12},{9,13},{10,... | collective-permute-start | bytes 786440 | tf_op jit(solution)/shard_map/ppermute | solution.py:269
  349.2 44.6 %collective-permute-start.3 = (bf16[512,1024]{1,0:T(8,128)(2,1)}, bf16[512,1024]{1,0:T(8,128)(2,1)}, u32[]{:S(2)}, u32[]{:S(2)}) collective-permute-start(bf16[512,1024]{1,0:T(8,128)(2,1)} %fusion.5), channel_id=1, source_target_pairs={{2,0},{3,1},{4,2},{5,3},{6,4},{7,5},{8,6},{9,7},{10,8},{11,9},{12,... | collective-permute-start | bytes 3145736 | tf_op jit(solution)/shard_map/ppermute | solution.py:455
  352.4 17.3 %copy-start.32 = (bf16[4,1,1,1,16,2048]{5,4,3,2,1,0:T(8,128)(2,1)}, bf16[4,1,1,1,16,2048]{5,4,3,2,1,0:T(8,128)(2,1)S(1)}, u32[]{:S(2)}) copy-start(bf16[4,1,1,1,16,2048]{5,4,3,2,1,0:T(8,128)(2,1)S(1)} %collective-permute-done.6) | copy-start | bytes 786436
  353.6 35.6 %collective-permute-start.7 = (bf16[1,1,1,1,16,2048]{5,4,3,2,1,0:T(8,128)(2,1)S(1)}, bf16[1,1,1,1,16,2048]{5,4,3,2,1,0:T(8,128)(2,1)S(1)}, u32[]{:S(2)}, u32[]{:S(2)}) collective-permute-start(bf16[1,1,1,1,16,2048]{5,4,3,2,1,0:T(8,128)(2,1)S(1)} %get-tuple-element.66), channel_id=1, source_target_pairs={{0,8},{1,9},{2,10},{3,11},{4,12},{5,13},{6,14},{7,15},{8,16},{9,17... | collective-permute-start | bytes 196616 | tf_op jit(solution)/shard_map/ppermute | solution.py:269
  357.2 32.1 %collective-permute-start.9 = (bf16[1,1,1,1,16,2048]{5,4,3,2,1,0:T(8,128)(2,1)S(1)}, bf16[1,1,1,1,16,2048]{5,4,3,2,1,0:T(8,128)(2,1)S(1)}, u32[]{:S(2)}, u32[]{:S(2)}) collective-permute-start(bf16[1,1,1,1,16,2048]{5,4,3,2,1,0:T(8,128)(2,1)S(1)} %get-tuple-element.67), channel_id=1, source_target_pairs={{0,24},{1,25},{2,26},{3,27},{4,28},{5,29},{6,30},{7,31},{8,0},{9,1... | collective-permute-start | bytes 196616 | tf_op jit(solution)/shard_map/ppermute | solution.py:269
  365.7 24.1 %collective-permute-start.8 = (bf16[1,1,1,1,16,2048]{5,4,3,2,1,0:T(8,128)(2,1)S(1)}, bf16[1,1,1,1,16,2048]{5,4,3,2,1,0:T(8,128)(2,1)S(1)}, u32[]{:S(2)}, u32[]{:S(2)}) collective-permute-start(bf16[1,1,1,1,16,2048]{5,4,3,2,1,0:T(8,128)(2,1)S(1)} %get-tuple-element.68), channel_id=1, source_target_pairs={{0,16},{1,17},{2,18},{3,19},{4,20},{5,21},{6,22},{7,23},{8,24},{9,... | collective-permute-start | bytes 196616 | tf_op jit(solution)/shard_map/ppermute | solution.py:269
  371.1 22.8 %copy-start.15 = (f32[512,1024]{1,0:T(8,128)S(1)}, f32[512,1024]{1,0:T(8,128)}, u32[]{:S(2)}) copy-start(f32[512,1024]{1,0:T(8,128)} %slice_add_fusion) | copy-start | bytes 6291460
  371.1 22.8 %copy-start.40 = (f32[1024]{0:T(1024)S(1)}, f32[1024]{0:T(1024)}, u32[]{:S(2)}) copy-start(f32[1024]{0:T(1024)} %param.36) | copy-start | bytes 12292
  389.2 72.6 %collective-permute-start.10 = (bf16[4,2,2,1,32,3072]{5,4,3,2,1,0:T(8,128)(2,1)}, bf16[4,2,2,1,32,3072]{5,4,3,2,1,0:T(8,128)(2,1)}, u32[]{:S(2)}, u32[]{:S(2)}) collective-permute-start(bf16[4,2,2,1,32,3072]{5,4,3,2,1,0:T(8,128)(2,1)} %constant_dynamic-slice_fusion.20), channel_id=1, source_target_pairs={{0,1},{1,0},{2,3},{3,2},{4,5},{5,4},{6,7},{7,6},{8,9},{9,8},{10,11... | collective-permute-start | bytes 9437192 | tf_op jit(solution)/shard_map/ppermute | solution.py:269
  389.2 77.0 %collective-permute-start.34 = (bf16[4,2,2,1,128,1024]{5,4,3,2,1,0:T(8,128)(2,1)}, bf16[4,2,2,1,128,1024]{5,4,3,2,1,0:T(8,128)(2,1)}, u32[]{:S(2)}, u32[]{:S(2)}) collective-permute-start(bf16[4,2,2,1,128,1024]{5,4,3,2,1,0:T(8,128)(2,1)} %constant_dynamic-slice_fusion.3), channel_id=1, source_target_pairs={{0,1},{1,0},{2,3},{3,2},{4,5},{5,4},{6,7},{7,6},{8,9},{9,8},{10,11... | collective-permute-start | bytes 12582920 | tf_op jit(solution)/shard_map/ppermute | solution.py:269
  389.9 81.3 %collective-permute-start.28 = (bf16[4,2,2,1,32,4096]{5,4,3,2,1,0:T(8,128)(2,1)}, bf16[4,2,2,1,32,4096]{5,4,3,2,1,0:T(8,128)(2,1)}, u32[]{:S(2)}, u32[]{:S(2)}) collective-permute-start(bf16[4,2,2,1,32,4096]{5,4,3,2,1,0:T(8,128)(2,1)} %constant_dynamic-slice_fusion.23), channel_id=1, source_target_pairs={{0,1},{1,0},{2,3},{3,2},{4,5},{5,4},{6,7},{7,6},{8,9},{9,8},{10,11... | collective-permute-start | bytes 12582920 | tf_op jit(solution)/shard_map/ppermute | solution.py:269
  398.4 40.5 %copy-start.44 = (f32[512]{0:T(512)S(1)}, f32[512]{0:T(512)}, u32[]{:S(2)}) copy-start(f32[512]{0:T(512)} %get-tuple-element.47) | copy-start | bytes 6148
  399.3 39.6 %copy-start.43 = (f32[512]{0:T(512)S(1)}, f32[512]{0:T(512)}, u32[]{:S(2)}) copy-start(f32[512]{0:T(512)} %get-tuple-element.48) | copy-start | bytes 6148
  399.3 50.4 %copy-start.20 = (f32[512,1024]{1,0:T(8,128)S(1)}, f32[512,1024]{1,0:T(8,128)}, u32[]{:S(2)}) copy-start(f32[512,1024]{1,0:T(8,128)} %copy-done.19) | copy-start | bytes 6291460
  399.3 50.4 %copy-start.21 = (f32[512,1024]{1,0:T(8,128)S(1)}, f32[512,1024]{1,0:T(8,128)}, u32[]{:S(2)}) copy-start(f32[512,1024]{1,0:T(8,128)} %get-tuple-element.51) | copy-start | bytes 6291460
  399.3 50.4 %slice-start.10 = ((f32[1536]{0:T(1024)}), f32[512]{0:T(512)S(1)}, s32[]{:S(2)}) async-start(f32[1536]{0:T(1024)} %copy-done.35), calls=%async_computation.10 | async-start | bytes 4096 | tf_op jit(solution)/shard_map/slice | solution.py:461
  399.4 7.3 %collective-permute-start.40 = (f32[4,2,2,1,32,6]{4,5,3,2,1,0:T(8,128)S(1)}, f32[4,2,2,1,32,6]{4,5,3,2,1,0:T(8,128)S(1)}, u32[]{:S(2)}, u32[]{:S(2)}) collective-permute-start(f32[4,2,2,1,32,6]{4,5,3,2,1,0:T(8,128)S(1)} %constant_dynamic-slice_fusion.1), channel_id=1, source_target_pairs={{0,1},{1,0},{2,3},{3,2},{4,5},{5,4},{6,7},{7,6},{8,9},{9,8},{10,11... | collective-permute-start | bytes 36872 | tf_op jit(solution)/shard_map/ppermute | solution.py:269
  406.6 6.2 collective-permute-start.22
  412.8 3.9 collective-permute-start.41
  416.7 5.2 collective-permute-start.23
  421.9 3.7 collective-permute-start.42
  425.6 4.3 collective-permute-start.24
  429.9 5.4 collective-permute-start.43
  435.3 3.6 collective-permute-start.45
  435.3 26.5 %slice-start.2 = ((s8[6291456]{0:T(1024)(128)(4,1)}), s8[4194304]{0:T(1024)(128)(4,1)S(1)}, s32[]{:S(2)}) async-start(s8[6291456]{0:T(1024)(128)(4,1)} %bitcast.87), calls=%async_computation.2 | async-start | bytes 8388608
  438.9 6.4 collective-permute-start.25
  445.2 4.5 collective-permute-start.44
  449.8 9.2 %collective-permute-start.26 = (bf16[4,2,1,1,16,2048]{5,4,3,2,1,0:T(8,128)(2,1)S(1)}, bf16[4,2,1,1,16,2048]{5,4,3,2,1,0:T(8,128)(2,1)S(1)}, u32[]{:S(2)}, u32[]{:S(2)}) collective-permute-start(bf16[4,2,1,1,16,2048]{5,4,3,2,1,0:T(8,128)(2,1)S(1)} %constant_dynamic-update-slice_fusion.7), channel_id=1, source_target_pairs={{0,2},{1,3},{2,0},{3,1},{4,6},{5,7},{6,4},{7,5},{8,10},{9,11},{10,... | collective-permute-start | bytes 1572872 | tf_op jit(solution)/shard_map/ppermute | solution.py:285
  459.0 7.1 %collective-permute-start.27 = (bf16[4,2,2,1,16,2048]{5,4,3,2,1,0:T(8,128)(2,1)S(1)}, bf16[4,2,2,1,16,2048]{5,4,3,2,1,0:T(8,128)(2,1)S(1)}, u32[]{:S(2)}, u32[]{:S(2)}) collective-permute-start(bf16[4,2,2,1,16,2048]{5,4,3,2,1,0:T(8,128)(2,1)S(1)} %constant_dynamic-update-slice_fusion.5), channel_id=1, source_target_pairs={{0,1},{1,0},{2,3},{3,2},{4,5},{5,4},{6,7},{7,6},{8,9},{9,8},{10,11... | collective-permute-start | bytes 3145736 | tf_op jit(solution)/shard_map/ppermute | solution.py:285
  461.7 37.3 %collective-permute-start.17 = (bf16[4,1,2,1,32,3072]{5,4,3,2,1,0:T(8,128)(2,1)S(1)}, bf16[4,1,2,1,32,3072]{5,4,3,2,1,0:T(8,128)(2,1)S(1)}, u32[]{:S(2)}, u32[]{:S(2)}) collective-permute-start(bf16[4,1,2,1,32,3072]{5,4,3,2,1,0:T(8,128)(2,1)S(1)} %add_convert_fusion.3), channel_id=1, source_target_pairs={{0,4},{1,5},{2,6},{3,7},{4,0},{5,1},{6,2},{7,3},{8,12},{9,13},{10,... | collective-permute-start | bytes 4718600 | tf_op jit(solution)/shard_map/ppermute | solution.py:269
  465.2 37.4 %collective-permute-start.11 = (bf16[4,2,1,1,32,3072]{5,4,3,2,1,0:T(8,128)(2,1)}, bf16[4,2,1,1,32,3072]{5,4,3,2,1,0:T(8,128)(2,1)S(1)}, u32[]{:S(2)}, u32[]{:S(2)}) collective-permute-start(bf16[4,2,1,1,32,3072]{5,4,3,2,1,0:T(8,128)(2,1)} %add_convert_fusion.4), channel_id=1, source_target_pairs={{0,2},{1,3},{2,0},{3,1},{4,6},{5,7},{6,4},{7,5},{8,10},{9,11},{10,... | collective-permute-start | bytes 4718600 | tf_op jit(solution)/shard_map/ppermute | solution.py:269
  469.1 124.2 %collective-permute-start.35 = (bf16[4,2,1,1,128,1024]{5,4,3,2,1,0:T(8,128)(2,1)S(1)}, bf16[4,2,1,1,128,1024]{5,4,3,2,1,0:T(8,128)(2,1)S(1)}, u32[]{:S(2)}, u32[]{:S(2)}) collective-permute-start(bf16[4,2,1,1,128,1024]{5,4,3,2,1,0:T(8,128)(2,1)S(1)} %add_convert_fusion.1), channel_id=1, source_target_pairs={{0,2},{1,3},{2,0},{3,1},{4,6},{5,7},{6,4},{7,5},{8,10},{9,11},{10,... | collective-permute-start | bytes 6291464 | tf_op jit(solution)/shard_map/ppermute | solution.py:269
  473.6 123.5 %collective-permute-start.29 = (bf16[4,1,2,1,32,4096]{5,4,3,2,1,0:T(8,128)(2,1)S(1)}, bf16[4,1,2,1,32,4096]{5,4,3,2,1,0:T(8,128)(2,1)S(1)}, u32[]{:S(2)}, u32[]{:S(2)}) collective-permute-start(bf16[4,1,2,1,32,4096]{5,4,3,2,1,0:T(8,128)(2,1)S(1)} %add_convert_fusion.2), channel_id=1, source_target_pairs={{0,4},{1,5},{2,6},{3,7},{4,0},{5,1},{6,2},{7,3},{8,12},{9,13},{10,... | collective-permute-start | bytes 6291464 | tf_op jit(solution)/shard_map/ppermute | solution.py:269
  500.7 63.1 %collective-permute-start.18 = (bf16[4,1,1,1,32,3072]{5,4,3,2,1,0:T(8,128)(2,1)S(1)}, bf16[4,1,1,1,32,3072]{5,4,3,2,1,0:T(8,128)(2,1)S(1)}, u32[]{:S(2)}, u32[]{:S(2)}) collective-permute-start(bf16[4,1,1,1,32,3072]{5,4,3,2,1,0:T(8,128)(2,1)S(1)} %add_convert_fusion.10), channel_id=1, source_target_pairs={{0,2},{1,3},{2,0},{3,1},{4,6},{5,7},{6,4},{7,5},{8,10},{9,11},{10,... | collective-permute-start | bytes 2359304 | tf_op jit(solution)/shard_map/ppermute | solution.py:269
  504.1 65.3 %collective-permute-start.12 = (bf16[4,1,1,1,32,3072]{5,4,3,2,1,0:T(8,128)(2,1)S(1)}, bf16[4,1,1,1,32,3072]{5,4,3,2,1,0:T(8,128)(2,1)S(1)}, u32[]{:S(2)}, u32[]{:S(2)}) collective-permute-start(bf16[4,1,1,1,32,3072]{5,4,3,2,1,0:T(8,128)(2,1)S(1)} %add_convert_fusion.11), channel_id=1, source_target_pairs={{0,4},{1,5},{2,6},{3,7},{4,0},{5,1},{6,2},{7,3},{8,12},{9,13},{10,... | collective-permute-start | bytes 2359304 | tf_op jit(solution)/shard_map/ppermute | solution.py:269
  565.5 9.7 %collective-permute-start.19 = (bf16[1,1,1,1,32,3072]{5,4,3,2,1,0:T(8,128)(2,1)S(1)}, bf16[1,1,1,1,32,3072]{5,4,3,2,1,0:T(8,128)(2,1)S(1)}, u32[]{:S(2)}, u32[]{:S(2)}) collective-permute-start(bf16[1,1,1,1,32,3072]{5,4,3,2,1,0:T(8,128)(2,1)S(1)} %get-tuple-element.58), channel_id=1, source_target_pairs={{0,8},{1,9},{2,10},{3,11},{4,12},{5,13},{6,14},{7,15},{8,16},{9,17... | collective-permute-start | bytes 589832 | tf_op jit(solution)/shard_map/ppermute | solution.py:269
  565.6 11.5 %collective-permute-start.21 = (bf16[1,1,1,1,32,3072]{5,4,3,2,1,0:T(8,128)(2,1)S(1)}, bf16[1,1,1,1,32,3072]{5,4,3,2,1,0:T(8,128)(2,1)S(1)}, u32[]{:S(2)}, u32[]{:S(2)}) collective-permute-start(bf16[1,1,1,1,32,3072]{5,4,3,2,1,0:T(8,128)(2,1)S(1)} %get-tuple-element.59), channel_id=1, source_target_pairs={{0,24},{1,25},{2,26},{3,27},{4,28},{5,29},{6,30},{7,31},{8,0},{9,1... | collective-permute-start | bytes 589832 | tf_op jit(solution)/shard_map/ppermute | solution.py:269
  569.4 22.7 %collective-permute-start.20 = (bf16[1,1,1,1,32,3072]{5,4,3,2,1,0:T(8,128)(2,1)S(1)}, bf16[1,1,1,1,32,3072]{5,4,3,2,1,0:T(8,128)(2,1)S(1)}, u32[]{:S(2)}, u32[]{:S(2)}) collective-permute-start(bf16[1,1,1,1,32,3072]{5,4,3,2,1,0:T(8,128)(2,1)S(1)} %get-tuple-element.60), channel_id=1, source_target_pairs={{0,16},{1,17},{2,18},{3,19},{4,20},{5,21},{6,22},{7,23},{8,24},{9,... | collective-permute-start | bytes 589832 | tf_op jit(solution)/shard_map/ppermute | solution.py:269
  575.2 24.6 %collective-permute-start.13 = (bf16[1,1,1,1,32,3072]{5,4,3,2,1,0:T(8,128)(2,1)S(1)}, bf16[1,1,1,1,32,3072]{5,4,3,2,1,0:T(8,128)(2,1)S(1)}, u32[]{:S(2)}, u32[]{:S(2)}) collective-permute-start(bf16[1,1,1,1,32,3072]{5,4,3,2,1,0:T(8,128)(2,1)S(1)} %get-tuple-element.61), channel_id=1, source_target_pairs={{0,8},{1,9},{2,10},{3,11},{4,12},{5,13},{6,14},{7,15},{8,16},{9,17... | collective-permute-start | bytes 589832 | tf_op jit(solution)/shard_map/ppermute | solution.py:269
  577.1 22.7 %collective-permute-start.15 = (bf16[1,1,1,1,32,3072]{5,4,3,2,1,0:T(8,128)(2,1)S(1)}, bf16[1,1,1,1,32,3072]{5,4,3,2,1,0:T(8,128)(2,1)S(1)}, u32[]{:S(2)}, u32[]{:S(2)}) collective-permute-start(bf16[1,1,1,1,32,3072]{5,4,3,2,1,0:T(8,128)(2,1)S(1)} %get-tuple-element.62), channel_id=1, source_target_pairs={{0,24},{1,25},{2,26},{3,27},{4,28},{5,29},{6,30},{7,31},{8,0},{9,1... | collective-permute-start | bytes 589832 | tf_op jit(solution)/shard_map/ppermute | solution.py:269
  592.1 9.7 %collective-permute-start.14 = (bf16[1,1,1,1,32,3072]{5,4,3,2,1,0:T(8,128)(2,1)S(1)}, bf16[1,1,1,1,32,3072]{5,4,3,2,1,0:T(8,128)(2,1)S(1)}, u32[]{:S(2)}, u32[]{:S(2)}) collective-permute-start(bf16[1,1,1,1,32,3072]{5,4,3,2,1,0:T(8,128)(2,1)S(1)} %get-tuple-element.63), channel_id=1, source_target_pairs={{0,16},{1,17},{2,18},{3,19},{4,20},{5,21},{6,22},{7,23},{8,24},{9,... | collective-permute-start | bytes 589832 | tf_op jit(solution)/shard_map/ppermute | solution.py:269
  595.2 20.5 %collective-permute-start.36 = (bf16[4,1,1,1,128,1024]{5,4,3,2,1,0:T(8,128)(2,1)S(1)}, bf16[4,1,1,1,128,1024]{5,4,3,2,1,0:T(8,128)(2,1)S(1)}, u32[]{:S(2)}, u32[]{:S(2)}) collective-permute-start(bf16[4,1,1,1,128,1024]{5,4,3,2,1,0:T(8,128)(2,1)S(1)} %add_convert_fusion.5), channel_id=1, source_target_pairs={{0,4},{1,5},{2,6},{3,7},{4,0},{5,1},{6,2},{7,3},{8,12},{9,13},{10,... | collective-permute-start | bytes 3145736 | tf_op jit(solution)/shard_map/ppermute | solution.py:269
  598.8 23.4 %collective-permute-start.30 = (bf16[4,1,1,1,32,4096]{5,4,3,2,1,0:T(8,128)(2,1)S(1)}, bf16[4,1,1,1,32,4096]{5,4,3,2,1,0:T(8,128)(2,1)S(1)}, u32[]{:S(2)}, u32[]{:S(2)}) collective-permute-start(bf16[4,1,1,1,32,4096]{5,4,3,2,1,0:T(8,128)(2,1)S(1)} %add_convert_fusion.6), channel_id=1, source_target_pairs={{0,2},{1,3},{2,0},{3,1},{4,6},{5,7},{6,4},{7,5},{8,10},{9,11},{10,... | collective-permute-start | bytes 3145736 | tf_op jit(solution)/shard_map/ppermute | solution.py:269
  617.5 11.3 %collective-permute-start.37 = (bf16[1,1,1,1,128,1024]{5,4,3,2,1,0:T(8,128)(2,1)S(1)}, bf16[1,1,1,1,128,1024]{5,4,3,2,1,0:T(8,128)(2,1)S(1)}, u32[]{:S(2)}, u32[]{:S(2)}) collective-permute-start(bf16[1,1,1,1,128,1024]{5,4,3,2,1,0:T(8,128)(2,1)S(1)} %get-tuple-element.52), channel_id=1, source_target_pairs={{0,8},{1,9},{2,10},{3,11},{4,12},{5,13},{6,14},{7,15},{8,16},{9,17... | collective-permute-start | bytes 786440 | tf_op jit(solution)/shard_map/ppermute | solution.py:269
  617.5 23.9 %collective-permute-start.39 = (bf16[1,1,1,1,128,1024]{5,4,3,2,1,0:T(8,128)(2,1)S(1)}, bf16[1,1,1,1,128,1024]{5,4,3,2,1,0:T(8,128)(2,1)S(1)}, u32[]{:S(2)}, u32[]{:S(2)}) collective-permute-start(bf16[1,1,1,1,128,1024]{5,4,3,2,1,0:T(8,128)(2,1)S(1)} %get-tuple-element.53), channel_id=1, source_target_pairs={{0,24},{1,25},{2,26},{3,27},{4,28},{5,29},{6,30},{7,31},{8,0},{9,1... | collective-permute-start | bytes 786440 | tf_op jit(solution)/shard_map/ppermute | solution.py:269
  621.3 31.8 %collective-permute-start.38 = (bf16[1,1,1,1,128,1024]{5,4,3,2,1,0:T(8,128)(2,1)S(1)}, bf16[1,1,1,1,128,1024]{5,4,3,2,1,0:T(8,128)(2,1)S(1)}, u32[]{:S(2)}, u32[]{:S(2)}) collective-permute-start(bf16[1,1,1,1,128,1024]{5,4,3,2,1,0:T(8,128)(2,1)S(1)} %get-tuple-element.54), channel_id=1, source_target_pairs={{0,16},{1,17},{2,18},{3,19},{4,20},{5,21},{6,22},{7,23},{8,24},{9,... | collective-permute-start | bytes 786440 | tf_op jit(solution)/shard_map/ppermute | solution.py:269
  623.8 31.3 %collective-permute-start.31 = (bf16[1,1,1,1,32,4096]{5,4,3,2,1,0:T(8,128)(2,1)S(1)}, bf16[1,1,1,1,32,4096]{5,4,3,2,1,0:T(8,128)(2,1)S(1)}, u32[]{:S(2)}, u32[]{:S(2)}) collective-permute-start(bf16[1,1,1,1,32,4096]{5,4,3,2,1,0:T(8,128)(2,1)S(1)} %get-tuple-element.55), channel_id=1, source_target_pairs={{0,8},{1,9},{2,10},{3,11},{4,12},{5,13},{6,14},{7,15},{8,16},{9,17... | collective-permute-start | bytes 786440 | tf_op jit(solution)/shard_map/ppermute | solution.py:269
  623.9 31.2 %collective-permute-start.33 = (bf16[1,1,1,1,32,4096]{5,4,3,2,1,0:T(8,128)(2,1)S(1)}, bf16[1,1,1,1,32,4096]{5,4,3,2,1,0:T(8,128)(2,1)S(1)}, u32[]{:S(2)}, u32[]{:S(2)}) collective-permute-start(bf16[1,1,1,1,32,4096]{5,4,3,2,1,0:T(8,128)(2,1)S(1)} %get-tuple-element.56), channel_id=1, source_target_pairs={{0,24},{1,25},{2,26},{3,27},{4,28},{5,29},{6,30},{7,31},{8,0},{9,1... | collective-permute-start | bytes 786440 | tf_op jit(solution)/shard_map/ppermute | solution.py:269
  628.8 32.6 %collective-permute-start.32 = (bf16[1,1,1,1,32,4096]{5,4,3,2,1,0:T(8,128)(2,1)S(1)}, bf16[1,1,1,1,32,4096]{5,4,3,2,1,0:T(8,128)(2,1)S(1)}, u32[]{:S(2)}, u32[]{:S(2)}) collective-permute-start(bf16[1,1,1,1,32,4096]{5,4,3,2,1,0:T(8,128)(2,1)S(1)} %get-tuple-element.57), channel_id=1, source_target_pairs={{0,16},{1,17},{2,18},{3,19},{4,20},{5,21},{6,22},{7,23},{8,24},{9,... | collective-permute-start | bytes 786440 | tf_op jit(solution)/shard_map/ppermute | solution.py:269
  (58 other events, 309.5 us)

commit v2 on v1

--- a/solution.py
+++ b/solution.py
@@ -289,6 +289,185 @@
     return held.reshape(rows * count, width)
 
 
+MESH = pl.DeviceIdType.MESH
+BLOCK = 32
+WIDE = 1024
+
+
+def places32():
+    me = lax.axis_index(AXIS)
+    core = lax.rem(me, 2)
+    x = lax.rem(lax.div(me, 2), 2)
+    y = lax.rem(lax.div(me, 4), 2)
+    z = lax.div(me, 8)
+    return me, core, x, y, z
+
+
+def chunk_of(ref, first_row, first_col, y, x, core):
+    return ref.at[:, y, x, core, pl.ds(first_row, BLOCK), pl.ds(first_col, WIDE)]
+
+
+def reduce_kernel(chunks, n_in, n_out, *refs):
+    total = len(chunks)
+    ins = refs[:n_in]
+    vec_in = refs[n_in]
+    outs = refs[n_in + 1 : n_in + 1 + n_out]
+    vec_out = refs[n_in + 1 + n_out]
+    (own, r0, r1, r2, r3, v0, v1, v2, v3, own_sem, s0, d0, s1, d1, s2, d2, s3, d3, vs, vd) = refs[n_in + n_out + 2 :]
+    me, core, x, y, z = places32()
+    sibling = me + 1 - 2 * core
+    x_peer = me + 2 - 4 * x
+    y_peer = me + 4 - 8 * y
+    z_other = [lax.rem(z + m, 4) for m in range(1, 4)]
+    z_peers = [me + 8 * (o - z) for o in z_other]
+
+    barrier = pltpu.get_barrier_semaphore()
+    for peer in (sibling, x_peer, y_peer, *z_peers):
+        pl.semaphore_signal(barrier, inc=1, device_id=(peer,), device_id_type=MESH)
+    pl.semaphore_wait(barrier, 6)
+
+    def remote(src, dst, send, recv, peer):
+        return pltpu.make_async_remote_copy(
+            src_ref=src, dst_ref=dst, send_sem=send, recv_sem=recv, device_id=(peer,), device_id_type=MESH
+        )
+
+    vec = remote(vec_in.at[1 - core], v0, vs.at[0], vd.at[0], sibling)
+    vec.start()
+    for c, (number, row, col, *_) in enumerate(chunks):
+        for f in range(2):
+            for s in range(2):
+                yy, xx = (s, f) if c % 2 == 0 else (f, s)
+                remote(
+                    chunk_of(ins[number], row, col, yy, xx, 1 - core), r0.at[c, f, s], s0.at[c], d0.at[c], sibling
+                ).start()
+                pltpu.make_async_copy(
+                    chunk_of(ins[number], row, col, yy, xx, core), own.at[c, f, s], own_sem.at[c]
+                ).start()
+
+    def along(c):
+        even = lax.rem(c, 2) == 0
+        return (
+            jnp.where(even, x, y),
+            jnp.where(even, x_peer, y_peer),
+            jnp.where(even, y, x),
+            jnp.where(even, y_peer, x_peer),
+        )
+
+    def add_blocks(count, dst, src):
+        @pl.loop(0, count)
+        def _(i):
+            dst(i)[...] = dst(i)[...] + src(i)[...]
+
+    def first(c):
+        f, fp, _, _ = along(c)
+        pltpu.make_async_copy(own.at[c], own.at[c], own_sem.at[c]).wait()
+        remote(r0.at[c], r0.at[c], s0.at[c], d0.at[c], sibling).wait_recv()
+        add_blocks(
+            16, lambda i: r0.at[c, i // 8, (i // 4) % 2, i % 4], lambda i: own.at[c, i // 8, (i // 4) % 2, i % 4]
+        )
+        remote(r0.at[c, 1 - f], r1.at[c], s1.at[c], d1.at[c], fp).start()
+
+    def second(c):
+        f, fp, s, sp = along(c)
+        remote(r0.at[c, 1 - f], r1.at[c], s1.at[c], d1.at[c], fp).wait_recv()
+        add_blocks(8, lambda i: r1.at[c, i // 4, i % 4], lambda i: r0.at[c, f, i // 4, i % 4])
+        remote(r1.at[c, 1 - s], r2.at[c], s2.at[c], d2.at[c], sp).start()
+
+    def third(c):
+        _, _, s, sp = along(c)
+        remote(r1.at[c, 1 - s], r2.at[c], s2.at[c], d2.at[c], sp).wait_recv()
+        add_blocks(4, lambda i: r2.at[c, i], lambda i: r1.at[c, s, i])
+        for m in range(3):
+            remote(r2.at[c, z_other[m]], r3.at[c, m], s3.at[c, m], d3.at[c, m], z_peers[m]).start()
+
+    @pl.loop(0, total + 4)
+    def _(k):
+        @pl.when(k < total)
+        def _():
+            first(k)
+
+        @pl.when((k >= 2) & (k < total + 2))
+        def _():
+            second(k - 2)
+
+        @pl.when(k >= 4)
+        def _():
+            third(k - 4)
+
+    vec.wait()
+    v0[...] += vec_in[core]
+    step = remote(v0.at[1 - x], v1, vs.at[1], vd.at[1], x_peer)
+    step.start()
+    step.wait()
+    v1[...] += v0[x]
+    step = remote(v1.at[1 - y], v2, vs.at[2], vd.at[2], y_peer)
+    step.start()
+    step.wait()
+    v2[...] += v1[y]
+    steps = [remote(v2.at[z_other[m]], v3.at[m], vs.at[3 + m], vd.at[3 + m], z_peers[m]) for m in range(3)]
+    for step in steps:
+        step.start()
+    for step in steps:
+        step.wait()
+    vec_out[...] = v2[z] + v3[0] + v3[1] + v3[2]
+
+    for c, (_, _, _, number, rows, row, col) in enumerate(chunks):
+        for m in range(3):
+            remote(r2.at[c, z_other[m]], r3.at[c, m], s3.at[c, m], d3.at[c, m], z_peers[m]).wait()
+        summed = r2[c, z].astype(F32) + r3[c, 0].astype(F32) + r3[c, 1].astype(F32) + r3[c, 2].astype(F32)
+        outs[number][row : row + rows, col : col + WIDE] = summed[:rows]
+
+    @pl.loop(0, total)
+    def _(c):
+        f, fp, s, sp = along(c)
+        remote(r0.at[c], r0.at[c], s0.at[c], d0.at[c], sibling).wait_send()
+        remote(r0.at[c, 1 - f], r1.at[c], s1.at[c], d1.at[c], fp).wait_send()
+        remote(r1.at[c, 1 - s], r2.at[c], s2.at[c], d2.at[c], sp).wait_send()
+
+
+def reduce_all(arrays, vectors):
+    ins = []
+    chunks = []
+    shapes = []
+    for array, rows in arrays:
+        height = array.shape[0] // 32
+        cols = array.shape[1]
+        number = len(ins)
+        ins.append(array.reshape(4, 2, 2, 2, height, cols))
+        shapes.append((rows, cols))
+        for row in range(0, height, BLOCK):
+            for col in range(0, cols, WIDE):
+                chunks.append((number, row, col, number, min(BLOCK, rows - row), row, col))
+    total = len(chunks)
+    kinds = vectors.shape[0]
+    vec = jnp.pad(vectors.reshape(kinds, 32, 32).transpose(1, 0, 2), ((0, 0), (0, 8 - kinds), (0, LANES - 32)))
+    vec = vec.reshape(4, 2, 2, 2, 8, LANES).transpose(3, 2, 1, 0, 4, 5)
+    vmem = pl.BlockSpec(memory_space=pltpu.VMEM)
+    dma = pltpu.SemaphoreType.DMA
+    results = pl.pallas_call(
+        functools.partial(reduce_kernel, chunks, len(ins), len(ins)),
+        in_specs=[pl.BlockSpec(memory_space=pl.ANY)] * len(ins) + [vmem],
+        out_specs=[vmem] * (len(ins) + 1),
+        out_shape=[jax.ShapeDtypeStruct(shape, F32) for shape in shapes] + [jax.ShapeDtypeStruct((8, LANES), F32)],
+        scratch_shapes=[
+            pltpu.VMEM((total, 2, 2, 4, BLOCK, WIDE), BF16),
+            pltpu.VMEM((total, 2, 2, 4, BLOCK, WIDE), BF16),
+            pltpu.VMEM((total, 2, 4, BLOCK, WIDE), BF16),
+            pltpu.VMEM((total, 4, BLOCK, WIDE), BF16),
+            pltpu.VMEM((total, 3, BLOCK, WIDE), BF16),
+            pltpu.VMEM((2, 2, 4, 8, LANES), F32),
+            pltpu.VMEM((2, 4, 8, LANES), F32),
+            pltpu.VMEM((4, 8, LANES), F32),
+            pltpu.VMEM((3, 8, LANES), F32),
+            dma((total,)), dma((total,)), dma((total,)), dma((total,)), dma((total,)), dma((total,)), dma((total,)),
+            dma((total, 3)), dma((total, 3)), dma((6,)), dma((6,)),
+        ],
+        compiler_params=pltpu.CompilerParams(collective_id=0, has_side_effects=True, vmem_limit_bytes=62 << 20),
+        cost_estimate=pl.CostEstimate(flops=1 << 20, bytes_accessed=64 << 20, transcendentals=0),
+    )(*ins, vec)
+    return results[:-1], results[-1][:kinds, :32]
+
+
 def matmul(left, right):
     return jnp.dot(left, right, preferred_element_type=F32)
 
@@ -407,8 +586,7 @@
     z_, y_, x_, c_ = 0, 1, 2, 3
     one_way = (c_, x_, y_, z_) if len(factors(count)) == 4 else (0,)
     other_way = (c_, y_, x_, z_) if len(factors(count)) == 4 else (0,)
-    down_out = reduce_scatter(down_grad, one_way, BF16, count)
-    up_out = reduce_scatter(up_grad, other_way, BF16, count)
+    fused = count == 32
     grad_three = right_product(grad_pre, up_weight)
     mlp_gain_grad = jnp.sum(grad_three * unit_three, axis=0)
     mlp_bias_grad = jnp.sum(grad_three, axis=0)
@@ -421,15 +599,10 @@
         cross_q, text_keys, text_values, grad_cross, cross_att, cross_lse,
         query_code[None, :], text_code[:, :, None], no_numbers, False, (text,), text_ends,
     )
-    own_text = reduce_scatter(jnp.concatenate([grad_tk, grad_tv], 1), one_way, BF16, count).astype(BF16)
     width = grad_tk.shape[1]
-    caption_grad = right_product(own_text[:, :width], cross_key) + right_product(own_text[:, width:], cross_value)
-    all_text = all_gather(own_text, one_way[::-1], count)
-    share = width // count
-    caption_part = lax.dynamic_slice_in_dim(caption_states, device * share, share, 1)
-    text_weight_grads = left_product(caption_part, all_text)
-    cross_key_grad = text_weight_grads[:, :width]
-    cross_value_grad = text_weight_grads[:, width:]
+    cross_key_grad = left_product(caption_states, grad_tk).astype(BF16)
+    cross_value_grad = left_product(caption_states, grad_tv).astype(BF16)
+    caption_grad = (right_product(grad_tk, cross_key) + right_product(grad_tv, cross_value)).astype(BF16)
     cross_query_grad = left_product(low_two, grad_cq).astype(BF16)
     grad_norm_two = right_product(grad_cq, cross_query)
     cross_gain_grad = jnp.sum(grad_norm_two * unit_two, axis=0)
@@ -438,9 +611,6 @@
     grad_one_low = grad_one.astype(BF16)
 
     output_weight_grad = left_product(self_att, grad_one_low).astype(BF16)
-    middle = reduce_scatter(
-        jnp.concatenate([cross_output_grad, cross_query_grad, output_weight_grad], 1), other_way, BF16, count
-    )
     grad_self = right_product(grad_one_low, output_weight).astype(BF16)
     grad_q, grad_k, grad_v = attend_backward(
         queries, near_keys, near_values, grad_self, self_att, self_lse,
@@ -462,31 +632,33 @@
     query_grad = left_product(low_one, grad_q).astype(BF16)
     key_grad = left_product(near_low, grad_k).astype(BF16)
     value_grad = left_product(near_low, grad_v).astype(BF16)
-    late = reduce_scatter(jnp.concatenate([query_grad, key_grad, value_grad], 1), one_way, BF16, count)
+    grads = [
+        down_grad, up_grad, cross_output_grad, cross_query_grad, cross_key_grad, cross_value_grad,
+        output_weight_grad, query_grad, key_grad, value_grad,
+    ]
     vectors = jnp.stack(
-        [attn_gain_grad, attn_bias_grad, cross_gain_grad, cross_bias_grad, mlp_gain_grad, mlp_bias_grad], 1
-    )
-    small = reduce_scatter(vectors, one_way, F32, count)
+        [attn_gain_grad, attn_bias_grad, cross_gain_grad, cross_bias_grad, mlp_gain_grad, mlp_bias_grad]
+    )
+    if fused:
+        share = text // count
+        caption_blocks = jnp.pad(caption_grad.reshape(count, share, width), ((0, 0), (0, BLOCK - share), (0, 0)))
+        arrays = [(grad, grad.shape[0] // count) for grad in grads]
+        arrays.append((caption_blocks.reshape(count * BLOCK, width), share))
+        sums, small = reduce_all(arrays, vectors)
+    else:
+        sums = [
+            reduce_scatter(grad, one_way if i % 2 else other_way, BF16, count)
+            for i, grad in enumerate([*grads, caption_grad])
+        ]
+        small = reduce_scatter(vectors.T, one_way, F32, count).T
+    (down_out, up_out, cross_output_out, cross_query_out, cross_key_out, cross_value_out,
+     output_out, query_out, key_out, value_out, caption_out) = sums
     return (
-        block_output,
-        input_grad,
-        caption_grad,
-        late[:, :width],
-        late[:, width : 2 * width],
-        late[:, 2 * width :],
-        middle[:, 2 * width :],
-        middle[:, width : 2 * width],
-        cross_key_grad,
-        cross_value_grad,
-        middle[:, :width],
-        up_out,
-        down_out,
-        small[:, 0],
-        small[:, 1],
-        small[:, 2],
-        small[:, 3],
-        small[:, 4],
-        small[:, 5],
+        block_output, input_grad, caption_out,
+        query_out, key_out, value_out, output_out,
+        cross_query_out, cross_key_out, cross_value_out, cross_output_out,
+        up_out, down_out,
+        small[0], small[1], small[2], small[3], small[4], small[5],
     )
 
 

time: 668 us -> 515 us (0.77)
  waiting for transfers between devices: 231 us -> 38.6 us
  Pallas kernels: 75.8 us -> 262 us
  starting transfers between devices: 77 us -> 13.5 us
  other arithmetic: 92.6 us -> 34.1 us
  local copies, waits for them, and re-layouts: 54 us -> 24.3 us
    ppermute x42 -> x0, waiting for transfers between devices: 212 us -> none  [the longest x36 185 us: reduce_scatter(): arrived.append(lax.ppermute(sent, AXIS, peers_along(count, axis, step)))]
    pallas_call x0 -> x1, Pallas kernels: none -> 186 us  [reduce_all(): pl.pallas_call(functools.partial(reduce_kernel, chunks, len(ins), len(ins...]
    ppermute x42 -> x0, starting transfers between devices: 69.3 us -> none  [the longest x36 69.2 us: reduce_scatter(): arrived.append(lax.ppermute(sent, AXIS, peers_along(count, axis, step)))]
    convert_element_type x15 -> x0, other arithmetic: 28.4 us -> none  [reduce_scatter(): sent = total([take(term, other, axis) for term in terms]).astype(kind)]
    concatenate x3 -> x0, other arithmetic: 19.8 us -> none  [the longest x1 13.6 us: body(): jnp.concatenate([cross_output_grad, cross_query_grad, output_weight_grad]...]
    ppermute x1, waiting for transfers between devices: 0.01 us -> 19.4 us  [body(): from_two = lax.ppermute(to_two, AXIS, behind).astype(F32)]
    concatenate x2 -> x0, local copies, waits for them, and re-layouts: 17.3 us -> none  [the longest x1 8.64 us: body(): jnp.concatenate([query_grad, key_grad, value_grad], 1)]
    dynamic_slice x6 -> x0, local copies, waits for them, and re-layouts: 14.3 us -> none  [take(): return lax.dynamic_slice_in_dim(value, place, 1, axis)]
  transfers between devices with their start and end apart: 46 -> 4, of which waited for: 26 -> 2; matrix products, arithmetic and copies ran while one was open for 19% -> 6% of each run, Pallas kernels for 0% -> 0%
where the time goes in v2:
time: 515 us; the launch traced here: 509 us
  Pallas kernels  262 us (51%)
  matrix products  135 us (26%)
  waiting for transfers between devices  38.6 us (7%)
  other arithmetic  34.1 us (7%)
  local copies, waits for them, and re-layouts  24.3 us (5%)
  starting transfers between devices  13.5 us (3%)
    pallas_call x1, Pallas kernels, reduce_all(): pl.pallas_call(functools.partial(reduce_kernel, chunks, len(ins), len(ins...  186 us
    dot_general x10, matrix products, left_product(): return lax.dot_general(left, right, TN, preferred_element_type=F32)  47.6 us
    dot_general x10, matrix products, right_product(): return lax.dot_general(left, right, NT, preferred_element_type=F32)  45.1 us
    pallas_call x2, Pallas kernels, attend_backward(): pl.pallas_call(functools.partial(backward_kernel, causal, sizes, ends), g...  43.9 us
    dot_general x10, matrix products, matmul(): return jnp.dot(left, right, preferred_element_type=F32)  42.1 us
    pallas_call x2, Pallas kernels, attend_forward(): pl.pallas_call(functools.partial(forward_kernel, causal, sizes, ends), gr...  32 us
    ppermute x1, waiting for transfers between devices, body(): from_two = lax.ppermute(to_two, AXIS, behind).astype(F32)  19.4 us
    ppermute x1, waiting for transfers between devices, body(): block_two = lax.ppermute(tokens, AXIS, ahead)  19.2 us
  transfers between devices with their start and end apart: 4, of which 2 were waited for; matrix products, arithmetic and copies ran while one was open for 6% of the time, Pallas kernels for 0%

profile of v2, /device:TPU:0, one launch (start us, length us, event | category | flops | bytes accessed | tf_op | source)
XLA Modules:
  0.0 509.4 jit_solution(15650951719808952208)
XLA Ops:
  0.7 5.0 collective-permute-start
  5.7 0.8 pad_dynamic-slice_fusion.2
  6.6 0.8 pad_dynamic-slice_fusion.1
  7.5 0.8 pad_dynamic-slice_fusion.3
  9.2 19.2 %collective-permute-done = bf16[512,1024]{1,0:T(8,128)(2,1)S(1)} collective-permute-done((bf16[512,1024]{1,0:T(8,128)(2,1)}, bf16[512,1024]{1,0:T(8,128)(2,1)S(1)}, u32[]{:S(2)}, u32[]{:S(2)}) %collective-permute-start) | collective-permute-done | bytes 1048608 | tf_op jit(solution)/shard_map/ppermute | solution.py:528
  28.4 2.7 broadcast_select_fusion
  32.0 3.0 convolution_convert_fusion.15.k_ref
  35.0 1.3 convolution_convert_fusion.14.v_ref
  36.5 2.1 convert_reduce_fusion
  38.7 4.0 fusion.2
  42.7 4.0 add_convert_fusion
  46.8 1.3 convolution_convert_fusion.17.q_ref
  48.0 1.5 copy-done.52
  49.5 4.8 convolution_convert_fusion.2.v_ref
  54.3 4.8 convolution_convert_fusion.3.k_ref
  59.1 16.9 %shard_map.366 = (bf16[512,1024]{1,0:T(8,128)(2,1)S(1)}, f32[8,512,128]{2,1,0:T(8,128)S(1)}) custom-call(s32[2]{0:T(128)S(1)} %subtract_clamp_fusion.n_ref, s32[512,1]{1,0:T(8,128)S(1)} %copy.47.qid_ref, s32[2,1,1280]{2,1,0:T(1,128)S(1)} %broadcast_in_dim.29.kid_ref, bf16[512,1024]{1,0:T(8,128)(2,1)S(1)} %convolution_convert_fusion.17.q_ref, ...), custom_call_target="tpu_custom_call" | custom-call | flops 10737418240 | bytes 8388608 | tf_op jit(solution)/shard_map/pallas_call | solution.py:81
  76.0 1.4 fusion.24
  78.1 0.9 copy-done.46
  79.0 1.3 convolution_convert_fusion.16.q_ref
  80.4 15.1 %shard_map.367 = (bf16[512,1024]{1,0:T(8,128)(2,1)S(1)}, f32[8,512,128]{2,1,0:T(8,128)}) custom-call(s32[2]{0:T(128)S(1)} %broadcast.183.n_ref, s32[512,1]{1,0:T(8,128)S(1)} %copy.48.qid_ref, s32[2,1,512]{2,1,0:T(1,128)S(1)} %broadcast_in_dim_broadcast_in_dim.4.kid_ref, bf16[512,1024]{1,0:T(8,128)(2,1)S(1)} %convolution_convert_fusion.16.q_ref, ...), custom_call_target="tpu_custom_call" | custom-call | flops 4294967296 | bytes 8388608 | tf_op jit(solution)/shard_map/pallas_call | solution.py:81
  95.5 3.3 fusion.25
  99.6 11.3 %fusion.21 = f32[512,4096]{1,0:T(8,128)} fusion(bf16[1024,4096]{1,0:T(8,128)(2,1)} %param.34, f32[512,1024]{1,0:T(8,128)S(1)} %get-tuple-element.92, f32[1024]{0:T(1024)S(1)} %copy-done.59, f32[1024]{0:T(1024)S(1)} %copy-done.43, f32[512]{0:T(512)S(1)} %add_rsqrt_fusion.1, f32[512]{0:T(512)S(1)} %broadcast_multiply_fusion.7), kind=kOutput, calls=%fused_computation.117 | convolution fusion | flops 4297588736 | bytes 18886656 | tf_op jit(solution)/shard_map/dot_general | solution.py:472
  110.9 9.7 %add_convert_fusion.2 = bf16[512,1024]{1,0:T(8,128)(2,1)} fusion(f32[512,1024]{1,0:T(8,128)S(1)} %get-tuple-element.92, bf16[4096,1024]{1,0:T(8,128)(2,1)S(1)} %bitcast.109, f32[512,4096]{1,0:T(8,128)} %fusion.21), kind=kOutput, calls=%fused_computation.36 | convolution fusion | flops 4314890240 | bytes 19922944 | tf_op jit(solution)/shard_map/dot_general | solution.py:472
  120.6 14.6 %multiply_convert_fusion = bf16[512,4096]{1,0:T(8,128)(2,1)} fusion(f32[512,4096]{1,0:T(8,128)} %fusion.21, bf16[512,1024]{1,0:T(8,128)(2,1)S(1)} %copy-done.23, bf16[4096,1024]{1,0:T(8,128)(2,1)} %param.35), kind=kOutput, calls=%fused_computation | convolution fusion | flops 4332716032 | bytes 22020096 | tf_op jit(solution)/shard_map/dot_general | solution.py:480
  135.2 12.6 %convolution_convert_fusion.1 = bf16[4096,1024]{1,0:T(8,128)(2,1)} fusion(bf16[512,1024]{1,0:T(8,128)(2,1)S(1)} %copy-done.23, f32[512,4096]{1,0:T(8,128)} %fusion.21), kind=kOutput, calls=%fused_computation.8 | convolution fusion | flops 4318035968 | bytes 17825792 | tf_op jit(solution)/shard_map/dot_general | solution.py:476
  147.8 9.2 %multiply_reduce_fusion = (f32[1024]{0:T(1024)S(1)}, f32[512]{0:T(512)S(1)}, f32[512]{0:T(512)S(1)}, f32[1024]{0:T(1024)S(1)}, f32[512,1024]{1,0:T(8,128)S(1)}) fusion(f32[512,1024]{1,0:T(8,128)S(1)} %get-tuple-element.92, f32[512]{0:T(512)S(1)} %add_rsqrt_fusion.1, f32[512]{0:T(512)S(1)} %broadcast_multiply_fusion.7, f32[1024]{0:T(1024)S(1)} %copy-done.43, ...), kind=kOutput, calls=%fused_computation.27 | convolution fusion | flops 4299682816 | bytes 16797696 | tf_op jit(solution)/shard_map/dot_general | solution.py:480
  157.1 0.8 multiply_add_fusion.2
  157.9 0.8 copy-done.45
  158.7 2.3 convolution_convert_fusion.13.g_ref
  161.0 2.6 convolution_convert_fusion.11
  163.7 21.5 %shard_map.368 = (bf16[512,1024]{1,0:T(8,128)(2,1)S(1)}, bf16[512,1024]{1,0:T(8,128)(2,1)S(1)}, bf16[512,1024]{1,0:T(8,128)(2,1)S(1)}) custom-call(s32[2]{0:T(128)S(1)} %broadcast.183.n_ref, s32[1,512]{1,0:T(1,128)S(1)} %bitcast.92, s32[2,512,1]{2,1,0:T(8,128)S(1)} %broadcast_in_dim_broadcast_in_dim.5.kid_ref, ...), custom_call_target="tpu_custom_call" | custom-call | flops 10737418240 | bytes 12582912 | tf_op jit(solution)/shard_map/pallas_call | solution.py:188
  185.3 2.9 convolution_convert_fusion.10
  188.1 1.8 multiply_reduce_fusion.1
  189.9 0.7 multiply_add_fusion.1
  190.7 0.9 copy-done.49
  191.5 1.3 convolution_convert_fusion.12.g_ref
  192.8 2.6 convolution_convert_fusion.7
  195.5 22.4 %shard_map.369 = (bf16[512,1024]{1,0:T(8,128)(2,1)S(1)}, bf16[1536,1024]{1,0:T(8,128)(2,1)}, bf16[1536,1024]{1,0:T(8,128)(2,1)}) custom-call(s32[2]{0:T(128)S(1)} %subtract_clamp_fusion.n_ref, s32[1,512]{1,0:T(1,128)S(1)} %bitcast.90, s32[2,1280,1]{2,1,0:T(8,128)S(1)} %copy.49.kid_ref, bf16[512,1024]{1,0:T(8,128)(2,1)S(1)} %convolution_convert_fusion.17.q_ref, ...), custom_call_target="tpu_custom_call" | custom-call | flops 26843545600 | bytes 12582912 | tf_op jit(solution)/shard_map/pallas_call | solution.py:188
  217.9 7.0 %convolution_convert_fusion.5 = bf16[1024,1024]{1,0:T(8,128)(2,1)} fusion(bf16[1536,1024]{1,0:T(8,128)(2,1)S(1)} %copy-done.21, bf16[1536,1024]{1,0:T(8,128)(2,1)} %get-tuple-element.46), kind=kOutput, calls=%fused_computation.45 | convolution fusion | flops 3222274048 | bytes 8388608 | tf_op jit(solution)/shard_map/dot_general | solution.py:476
  224.9 3.5 fusion.26
  228.4 2.6 convolution_convert_fusion.6
  231.5 3.7 convolution_add_fusion
  235.3 3.1 slice_add_fusion
  238.4 1.2 slice.100
  239.5 2.6 slice_reduce_fusion
  242.5 3.0 fusion.27
  245.5 2.6 convolution_convert_fusion.8
  248.2 2.6 add_convert_fusion.1
  250.7 7.0 %collective-permute-start.2 = (bf16[512,1024]{1,0:T(8,128)(2,1)}, bf16[512,1024]{1,0:T(8,128)(2,1)S(1)}, u32[]{:S(2)}, u32[]{:S(2)}) collective-permute-start(bf16[512,1024]{1,0:T(8,128)(2,1)} %slice.100), channel_id=1, source_target_pairs={{0,1},{1,0},{2,3},{3,2},{4,5},{5,4},{6,7},{7,6},{8,9},{9,8},{10,11... | collective-permute-start | bytes 3145736 | tf_op jit(solution)/shard_map/ppermute | solution.py:623
  257.8 5.1 %fusion.3 = (f32[1024]{0:T(1024)S(1)}, f32[1536,1024]{1,0:T(8,128)}) fusion(f32[512,1024]{1,0:T(8,128)S(1)} %copy-done.15, f32[1024,1024]{1,0:T(8,128)S(1)} %copy-done.13, f32[1536]{0:T(1024)S(1)} %copy-done.37, f32[1536]{0:T(1024)S(1)} %copy-done.27, bf16[512,1024]{1,0:T(8,128)(2,1)S(1)} %copy-done.9, bf16[512,1024]{1,0:T(8,128)(2,1)} %collective-permute-done.1, ...), kind=kLoop, calls=%fused_computation.13 | loop fusion | flops 17300480 | bytes 15745024 | tf_op jit(solution)/shard_map/reduce_sum | solution.py:627
  263.0 2.8 pad.9
  265.9 2.6 convolution_convert_fusion.9
  268.5 1.0 copy-done.62
  269.5 4.7 convolution_convert_fusion.4
  274.2 2.1 fusion.5
  276.3 1.4 collective-permute-start.3
  277.8 7.4 %convolution_convert_fusion = bf16[1024,4096]{1,0:T(8,128)(2,1)} fusion(bf16[512,4096]{1,0:T(8,128)(2,1)S(1)} %copy-done.64, f32[512,1024]{1,0:T(8,128)S(1)} %copy-done.19, f32[1024]{0:T(1024)S(1)} %copy-done.60, f32[1024]{0:T(1024)S(1)} %copy-done.43, f32[512]{0:T(512)S(1)} %add_rsqrt_fusion.1, f32[512]{0:T(512)S(1)} %broadcast_multiply_fusion.7), kind=kOutput, calls=%fused_computation.7 | convolution fusion | flops 4301783040 | bytes 14692352 | tf_op jit(solution)/shard_map/dot_general | solution.py:476
  285.2 19.4 %collective-permute-done.3 = bf16[512,1024]{1,0:T(8,128)(2,1)S(1)} collective-permute-done((bf16[512,1024]{1,0:T(8,128)(2,1)S(1)}, bf16[512,1024]{1,0:T(8,128)(2,1)S(1)}, u32[]{:S(2)}, u32[]{:S(2)}) %collective-permute-start.3) | collective-permute-done | bytes 1048608 | tf_op jit(solution)/shard_map/ppermute | solution.py:625
  304.6 3.6 fusion.22
  309.1 186.2 %shard_map.370 = (f32[128,1024]{1,0:T(8,128)}, f32[32,4096]{1,0:T(8,128)}, f32[32,1024]{1,0:T(8,128)}, f32[32,1024]{1,0:T(8,128)}, f32[32,1024]{1,0:T(8,128)}, /...) custom-call(bf16[4,2,2,2,128,1024]{5,4,3,2,1,0:T(8,128)(2,1)} %bitca, ...), custom_call_target="tpu_custom_call" | custom-call | flops 1048576 | bytes 67108864 | tf_op jit(solution)/shard_map/pallas_call | solution.py:447
  495.4 1.4 slice_bitcast_fusion
  496.9 4.8 multiply_add_fusion
  507.6 0.8 copy.73
  508.3 0.8 copy.74
  (183 shorter events, 11.6 us)
Async XLA Ops:
  0.7 31.3 %copy-start = (bf16[512,1024]{1,0:T(8,128)(2,1)S(1)}, bf16[512,1024]{1,0:T(8,128)(2,1)}, u32[]{:S(2)}) copy-start(bf16[512,1024]{1,0:T(8,128)(2,1)} %param.25) | copy-start | bytes 3145732
  0.7 27.7 %collective-permute-start = (bf16[512,1024]{1,0:T(8,128)(2,1)}, bf16[512,1024]{1,0:T(8,128)(2,1)S(1)}, u32[]{:S(2)}, u32[]{:S(2)}) collective-permute-start(bf16[512,1024]{1,0:T(8,128)(2,1)} %param.23), channel_id=1, source_target_pairs={{0,2},{1,3},{2,4},{3,5},{4,6},{5,7},{6,8},{7,9},{8,10},{9,11},{10,... | collective-permute-start | bytes 3145736 | tf_op jit(solution)/shard_map/ppermute | solution.py:528
  9.2 22.8 %copy-start.44 = (s32[4,128]{1,0:T(4,128)S(1)}, s32[4,128]{1,0:T(4,128)}, u32[]{:S(2)}) copy-start(s32[4,128]{1,0:T(4,128)} %param.43) | copy-start | bytes 6148
  28.4 3.1 copy-start.10
  31.1 5.2 %collective-permute-start.1 = (bf16[512,1024]{1,0:T(8,128)(2,1)}, bf16[512,1024]{1,0:T(8,128)(2,1)}, u32[]{:S(2)}, u32[]{:S(2)}) collective-permute-start(bf16[512,1024]{1,0:T(8,128)(2,1)} %broadcast_select_fusion), channel_id=1, source_target_pairs={{0,1},{1,0},{2,3},{3,2},{4,5},{5,4},{6,7},{7,6},{8,9},{9,8},{10,11... | collective-permute-start | bytes 3145736 | tf_op jit(solution)/shard_map/ppermute | solution.py:529
  32.0 3.0 copy-start.56
  36.3 44.1 %copy-start.4 = (bf16[512,1024]{1,0:T(8,128)(2,1)}, bf16[512,1024]{1,0:T(8,128)(2,1)S(1)}, u32[]{:S(2)}) copy-start(bf16[512,1024]{1,0:T(8,128)(2,1)S(1)} %convolution_convert_fusion.14.v_ref) | copy-start | bytes 3145732
  38.6 4.1 copy-start.39
  38.6 4.1 copy-start.41
  38.7 8.1 %copy-start.26 = (f32[1536]{0:T(1024)}, f32[1536]{0:T(1024)S(1)}, u32[]{:S(2)}) copy-start(f32[1536]{0:T(1024)S(1)} %broadcast_multiply_fusion) | copy-start | bytes 18436
  42.7 4.1 copy-start.36
  42.7 4.0 copy-start.54
  46.7 7.5 %copy-start.20 = (bf16[1536,1024]{1,0:T(8,128)(2,1)}, bf16[1536,1024]{1,0:T(8,128)(2,1)S(1)}, u32[]{:S(2)}) copy-start(bf16[1536,1024]{1,0:T(8,128)(2,1)S(1)} %add_convert_fusion) | copy-start | bytes 9437188
  46.8 2.7 copy-start.52
  49.5 4.8 copy-start.50
  59.1 16.9 %copy-start.48 = (bf16[1024,1024]{1,0:T(8,128)(2,1)S(1)}, bf16[1024,1024]{1,0:T(8,128)(2,1)}, u32[]{:S(2)}) copy-start(bf16[1024,1024]{1,0:T(8,128)(2,1)} %param.29) | copy-start | bytes 6291460
  77.4 1.6 copy-start.46
  95.5 65.5 %copy-start.3 = (bf16[512,1024]{1,0:T(8,128)(2,1)}, bf16[512,1024]{1,0:T(8,128)(2,1)S(1)}, u32[]{:S(2)}) copy-start(bf16[512,1024]{1,0:T(8,128)(2,1)S(1)} %get-tuple-element.42.o_ref) | copy-start | bytes 3145732
  98.8 58.3 %copy-start.18 = (f32[512,1024]{1,0:T(8,128)}, f32[512,1024]{1,0:T(8,128)S(1)}, u32[]{:S(2)}) copy-start(f32[512,1024]{1,0:T(8,128)S(1)} %get-tuple-element.92) | copy-start | bytes 6291460
  98.9 12.0 %slice-start.1 = ((s8[8388608]{0:T(1024)(128)(4,1)}), s8[4194304]{0:T(1024)(128)(4,1)S(1)}, s32[]{:S(2)}) async-start(s8[8388608]{0:T(1024)(128)(4,1)} %bitcast.108), calls=%async_computation.1 | async-start | bytes 8388608
  99.6 11.3 %slice-start.2 = ((s8[8388608]{0:T(1024)(128)(4,1)}), s8[4194304]{0:T(1024)(128)(4,1)S(1)}, s32[]{:S(2)}) async-start(s8[8388608]{0:T(1024)(128)(4,1)} %bitcast.108), calls=%async_computation.2 | async-start | bytes 8388608
  110.9 9.7 %copy-start.23 = (bf16[512,1024]{1,0:T(8,128)(2,1)S(1)}, bf16[512,1024]{1,0:T(8,128)(2,1)}, u32[]{:S(2)}) copy-start(bf16[512,1024]{1,0:T(8,128)(2,1)} %param.24) | copy-start | bytes 3145732
  157.1 1.6 copy-start.45
  185.2 2.9 copy-start.1
  185.2 2.9 copy-start.5
  185.3 2.9 copy-start.47
  189.9 1.6 copy-start.49
  195.5 22.4 %copy-start.21 = (bf16[1536,1024]{1,0:T(8,128)(2,1)S(1)}, bf16[1536,1024]{1,0:T(8,128)(2,1)}, u32[]{:S(2)}) copy-start(bf16[1536,1024]{1,0:T(8,128)(2,1)} %copy-done.20) | copy-start | bytes 9437188
  217.9 7.0 %copy-start.51 = (bf16[1024,1024]{1,0:T(8,128)(2,1)S(1)}, bf16[1024,1024]{1,0:T(8,128)(2,1)}, u32[]{:S(2)}) copy-start(bf16[1024,1024]{1,0:T(8,128)(2,1)} %param.27) | copy-start | bytes 6291460
  217.9 7.0 %copy-start.63 = (bf16[1536,1024]{1,0:T(8,128)(2,1)S(1)}, bf16[1536,1024]{1,0:T(8,128)(2,1)}, u32[]{:S(2)}) copy-start(bf16[1536,1024]{1,0:T(8,128)(2,1)} %get-tuple-element.46) | copy-start | bytes 9437188
  228.4 2.6 copy-start.53
  228.4 3.1 copy-start.61
  231.5 3.7 copy-start.55
  235.2 4.3 copy-start.14
  239.5 2.9 copy-start.6
  242.5 3.0 copy-start.2
  245.5 2.7 copy-start.57
  245.5 12.3 %copy-start.15 = (f32[512,1024]{1,0:T(8,128)S(1)}, f32[512,1024]{1,0:T(8,128)}, u32[]{:S(2)}) copy-start(f32[512,1024]{1,0:T(8,128)} %slice_add_fusion) | copy-start | bytes 6291460
  248.1 9.6 %copy-start.9 = (bf16[512,1024]{1,0:T(8,128)(2,1)S(1)}, bf16[512,1024]{1,0:T(8,128)(2,1)}, u32[]{:S(2)}) copy-start(bf16[512,1024]{1,0:T(8,128)(2,1)} %param.23) | copy-start | bytes 3145732
  248.1 9.6 %copy-start.12 = (bf16[512,1024]{1,0:T(8,128)(2,1)S(1)}, bf16[512,1024]{1,0:T(8,128)(2,1)}, u32[]{:S(2)}) copy-start(bf16[512,1024]{1,0:T(8,128)(2,1)} %copy-done.10) | copy-start | bytes 3145732
  248.1 9.6 %copy-start.13 = (f32[1024,1024]{1,0:T(8,128)S(1)}, f32[1024,1024]{1,0:T(8,128)}, u32[]{:S(2)}) copy-start(f32[1024,1024]{1,0:T(8,128)} %get-tuple-element.75) | copy-start | bytes 12582916
  248.1 9.6 %copy-start.27 = (f32[1536]{0:T(1024)S(1)}, f32[1536]{0:T(1024)}, u32[]{:S(2)}) copy-start(f32[1536]{0:T(1024)} %copy-done.26) | copy-start | bytes 18436
  248.2 9.6 %copy-start.37 = (f32[1536]{0:T(1024)S(1)}, f32[1536]{0:T(1024)}, u32[]{:S(2)}) copy-start(f32[1536]{0:T(1024)} %copy-done.36) | copy-start | bytes 18436
  250.7 23.5 %collective-permute-start.2 = (bf16[512,1024]{1,0:T(8,128)(2,1)}, bf16[512,1024]{1,0:T(8,128)(2,1)S(1)}, u32[]{:S(2)}, u32[]{:S(2)}) collective-permute-start(bf16[512,1024]{1,0:T(8,128)(2,1)} %slice.100), channel_id=1, source_target_pairs={{0,1},{1,0},{2,3},{3,2},{4,5},{5,4},{6,7},{7,6},{8,9},{9,8},{10,11... | collective-permute-start | bytes 3145736 | tf_op jit(solution)/shard_map/ppermute | solution.py:623
  265.9 2.6 copy-start.22
  265.9 3.6 copy-start.62
  269.5 8.2 %copy-start.64 = (bf16[512,4096]{1,0:T(8,128)(2,1)S(1)}, bf16[512,4096]{1,0:T(8,128)(2,1)}, u32[]{:S(2)}) copy-start(bf16[512,4096]{1,0:T(8,128)(2,1)} %multiply_convert_fusion) | copy-start | bytes 12582916
  274.2 3.6 copy-start.19
  274.2 3.6 copy-start.60
  276.3 28.4 %copy-start.16 = (f32[512,1024]{1,0:T(8,128)S(1)}, f32[512,1024]{1,0:T(8,128)}, u32[]{:S(2)}) copy-start(f32[512,1024]{1,0:T(8,128)} %slice_add_fusion) | copy-start | bytes 6291460
  276.3 28.3 %copy-start.40 = (f32[1024]{0:T(1024)S(1)}, f32[1024]{0:T(1024)}, u32[]{:S(2)}) copy-start(f32[1024]{0:T(1024)} %param.36) | copy-start | bytes 12292
  276.3 28.3 %collective-permute-start.3 = (bf16[512,1024]{1,0:T(8,128)(2,1)S(1)}, bf16[512,1024]{1,0:T(8,128)(2,1)S(1)}, u32[]{:S(2)}, u32[]{:S(2)}) collective-permute-start(bf16[512,1024]{1,0:T(8,128)(2,1)S(1)} %fusion.5), channel_id=1, source_target_pairs={{2,0},{3,1},{4,2},{5,3},{6,4},{7,5},{8,6},{9,7},{10,8},{11,9},{12,... | collective-permute-start | bytes 3145736 | tf_op jit(solution)/shard_map/ppermute | solution.py:625
  309.1 187.7 %slice-start = ((f32[1536]{0:T(1024)}), f32[512]{0:T(512)S(1)}, s32[]{:S(2)}) async-start(f32[1536]{0:T(1024)} %copy-done.36), calls=%async_computation | async-start | bytes 4096 | tf_op jit(solution)/shard_map/slice | solution.py:631
  496.8 4.8 copy-start.38
  496.8 5.5 %copy-start.35 = (f32[32,1024]{1,0:T(8,128)S(1)}, f32[32,1024]{1,0:T(8,128)}, u32[]{:S(2)}) copy-start(f32[32,1024]{1,0:T(8,128)} %get-tuple-element.119) | copy-start | bytes 393220
  496.8 6.1 %copy-start.34 = (f32[32,1024]{1,0:T(8,128)S(1)}, f32[32,1024]{1,0:T(8,128)}, u32[]{:S(2)}) copy-start(f32[32,1024]{1,0:T(8,128)} %get-tuple-element.120) | copy-start | bytes 393220
  496.8 6.8 %copy-start.33 = (f32[32,1024]{1,0:T(8,128)S(1)}, f32[32,1024]{1,0:T(8,128)}, u32[]{:S(2)}) copy-start(f32[32,1024]{1,0:T(8,128)} %get-tuple-element.121) | copy-start | bytes 393220
  496.8 7.4 %copy-start.32 = (f32[32,1024]{1,0:T(8,128)S(1)}, f32[32,1024]{1,0:T(8,128)}, u32[]{:S(2)}) copy-start(f32[32,1024]{1,0:T(8,128)} %get-tuple-element.122) | copy-start | bytes 393220
  496.9 8.1 %copy-start.31 = (f32[32,1024]{1,0:T(8,128)S(1)}, f32[32,1024]{1,0:T(8,128)}, u32[]{:S(2)}) copy-start(f32[32,1024]{1,0:T(8,128)} %get-tuple-element.123) | copy-start | bytes 393220
  496.9 8.7 %copy-start.30 = (f32[32,1024]{1,0:T(8,128)S(1)}, f32[32,1024]{1,0:T(8,128)}, u32[]{:S(2)}) copy-start(f32[32,1024]{1,0:T(8,128)} %get-tuple-element.124) | copy-start | bytes 393220
  496.9 9.4 %copy-start.29 = (f32[32,1024]{1,0:T(8,128)S(1)}, f32[32,1024]{1,0:T(8,128)}, u32[]{:S(2)}) copy-start(f32[32,1024]{1,0:T(8,128)} %get-tuple-element.125) | copy-start | bytes 393220
  496.9 10.0 %copy-start.28 = (f32[32,1024]{1,0:T(8,128)S(1)}, f32[32,1024]{1,0:T(8,128)}, u32[]{:S(2)}) copy-start(f32[32,1024]{1,0:T(8,128)} %get-tuple-element.126) | copy-start | bytes 393220
  501.6 5.9 %copy-start.25 = (f32[32,4096]{1,0:T(8,128)S(1)}, f32[32,4096]{1,0:T(8,128)}, u32[]{:S(2)}) copy-start(f32[32,4096]{1,0:T(8,128)} %get-tuple-element.127) | copy-start | bytes 1572868
  501.6 6.7 %copy-start.24 = (f32[128,1024]{1,0:T(8,128)S(1)}, f32[128,1024]{1,0:T(8,128)}, u32[]{:S(2)}) copy-start(f32[128,1024]{1,0:T(8,128)} %get-tuple-element.128) | copy-start | bytes 1572868
  (8 other events, 9.3 us)

commit v3 on v2

--- a/solution.py
+++ b/solution.py
@@ -61,7 +61,8 @@
             lses.append(row_max + jnp.log(summed))
         lane = lax.broadcasted_iota(jnp.int32, (TILE, LANES), 1)
         o_ref[...] = jnp.where(lane < LANES // 2, outs[0], outs[1]).astype(BF16)
-        lse_ref[0] = jnp.where(lane < LANES // 2, lses[0], lses[1])
+        for half in range(2):
+            lse_ref[0, half : half + 1, :] = jnp.transpose(jnp.broadcast_to(lses[half], (TILE, LANES)))[:1]
 
     if len(sizes) == 1:
         run(sizes[0])
@@ -92,13 +93,13 @@
             ],
             out_specs=[
                 pl.BlockSpec((TILE, LANES), lambda h, t, n: (t, h)),
-                pl.BlockSpec((1, TILE, LANES), lambda h, t, n: (h, t, 0)),
+                pl.BlockSpec((1, 2, TILE), lambda h, t, n: (h, 0, t)),
             ],
             scratch_shapes=[pltpu.VMEM((tiles, TILE, span), F32)],
         ),
         out_shape=[
             jax.ShapeDtypeStruct((rows, width), BF16),
-            jax.ShapeDtypeStruct((pairs, rows, LANES), F32),
+            jax.ShapeDtypeStruct((pairs, 2, rows), F32),
         ],
         compiler_params=pltpu.CompilerParams(vmem_limit_bytes=48 << 20),
         cost_estimate=pl.CostEstimate(flops=4 * flops, bytes_accessed=8 << 20, transcendentals=rows * span * HEADS),
@@ -137,7 +138,6 @@
         query = q_ref[...] * jnp.asarray(0.125, BF16)
         grad = g_ref[...]
         inner = grad.astype(F32) * o_ref[...].astype(F32)
-        lse_rows = jnp.transpose(lse_ref[0])
         inner_rows = jnp.transpose(inner)
         half_lanes = LANES // 2
         parts_dq = []
@@ -146,7 +146,7 @@
         for half in range(2):
             head_q = head_lanes(query, half)
             head_g = head_lanes(grad, half)
-            lse = lse_rows[half * half_lanes : half * half_lanes + 1, :]
+            lse = lse_ref[0, half : half + 1, :]
             delta = jnp.sum(inner_rows[half * half_lanes : (half + 1) * half_lanes, :], axis=0, keepdims=True)
             scores = lax.dot_general(keys, head_q, NT, preferred_element_type=F32)
             probs = jnp.exp(scores + bias_ref[tile, span - size :, :] - lse)
@@ -198,7 +198,7 @@
                 wide,
                 near,
                 near,
-                pl.BlockSpec((1, TILE, LANES), lambda h, t, n: (h, t, 0)),
+                pl.BlockSpec((1, 2, TILE), lambda h, t, n: (h, 0, t)),
             ],
             out_specs=[near, wide, wide],
             scratch_shapes=[
@@ -303,46 +303,97 @@
     return me, core, x, y, z
 
 
+SLOTS = 2
+LANDINGS = 9
+HALF = LANES // 2
+
+
 def chunk_of(ref, first_row, first_col, y, x, core):
     return ref.at[:, y, x, core, pl.ds(first_row, BLOCK), pl.ds(first_col, WIDE)]
 
 
-def reduce_kernel(chunks, n_in, n_out, *refs):
+def normalise_rows(value):
+    mean = jnp.mean(value, axis=-1, keepdims=True)
+    centred = value - mean
+    scale = lax.rsqrt(jnp.mean(centred * centred, axis=-1, keepdims=True) + EPS)
+    return centred * scale, scale
+
+
+IN_HBM = (
+    "queries", "near_keys", "near_values", "self_att", "grad_self", "near_low", "near_tokens", "grad_one",
+    "query_weight", "key_weight", "value_weight",
+)
+IN_VMEM = ("vectors", "starts", "self_lse", "attn_gain")
+SCRATCH = (
+    "arena", "sums", "accum_k", "accum_v", "back_one", "back_two", "vec", "vec_in",
+    "tiles", "r0", "r1", "r2", "r3",
+    "load", "own_sem", "s0", "d0", "s1", "d1", "s2", "d2", "s3", "d3", "vs", "vd", "bs", "bd", "credit",
+)
+
+
+def layer_kernel(chunks, rows, n_in, n_out, *refs):
     total = len(chunks)
+    made = total - 3
     ins = refs[:n_in]
-    vec_in = refs[n_in]
-    outs = refs[n_in + 1 : n_in + 1 + n_out]
-    vec_out = refs[n_in + 1 + n_out]
-    (own, r0, r1, r2, r3, v0, v1, v2, v3, own_sem, s0, d0, s1, d1, s2, d2, s3, d3, vs, vd) = refs[n_in + n_out + 2 :]
+    refs = refs[n_in:]
+    hbm = dict(zip(IN_HBM, refs))
+    refs = refs[len(IN_HBM) :]
+    near = dict(zip(IN_VMEM, refs))
+    refs = refs[len(IN_VMEM) :]
+    outs = refs[:n_out]
+    vec_out, input_grad = refs[n_out : n_out + 2]
+    held = dict(zip(SCRATCH, refs[n_out + 2 :]))
+    arena, tiles = held["arena"], held["tiles"]
+    r0, r1, r2, r3 = held["r0"], held["r1"], held["r2"], held["r3"]
+    s0, d0, s1, d1, s2, d2, s3, d3 = (held[name] for name in ("s0", "d0", "s1", "d1", "s2", "d2", "s3", "d3"))
+    own_sem, credit, load = held["own_sem"], held["credit"], held["load"]
+    sums = held["sums"]
+    vec = held["vec"]
+
     me, core, x, y, z = places32()
     sibling = me + 1 - 2 * core
     x_peer = me + 2 - 4 * x
     y_peer = me + 4 - 8 * y
     z_other = [lax.rem(z + m, 4) for m in range(1, 4)]
     z_peers = [me + 8 * (o - z) for o in z_other]
+    has_before = me >= 2
+    has_after = me < 30
 
     barrier = pltpu.get_barrier_semaphore()
     for peer in (sibling, x_peer, y_peer, *z_peers):
         pl.semaphore_signal(barrier, inc=1, device_id=(peer,), device_id_type=MESH)
-    pl.semaphore_wait(barrier, 6)
+
+    @pl.when(has_before)
+    def _():
+        pl.semaphore_signal(barrier, inc=1, device_id=(me - 2,), device_id_type=MESH)
+
+    @pl.when(has_after)
+    def _():
+        pl.semaphore_signal(barrier, inc=1, device_id=(me + 2,), device_id_type=MESH)
+
+    def fetch(name, place, number, at=None, dst=None):
+        source = hbm[name] if at is None else at
+        target = arena.at[pl.ds(place, source.shape[0])] if dst is None else dst
+        return pltpu.make_async_copy(source, target, load.at[number])
+
+    q_at, k_at, v_at, g_at, o_at = 0, rows, 4 * rows, 7 * rows, 8 * rows
+    low_at = 9 * rows
+    wq_at, wk_at, wv_at = 12 * rows, 14 * rows, 7 * rows
+
+    first_loads = [
+        fetch("queries", q_at, 0), fetch("near_keys", k_at, 1), fetch("near_values", v_at, 2),
+        fetch("grad_self", g_at, 3), fetch("self_att", o_at, 4), fetch("near_low", low_at, 5),
+        fetch("query_weight", wq_at, 6), fetch("key_weight", wk_at, 7),
+    ]
+    for copy in first_loads:
+        copy.start()
+
+    pl.semaphore_wait(barrier, 6 + jnp.where(has_before, 1, 0) + jnp.where(has_after, 1, 0))
 
     def remote(src, dst, send, recv, peer):
         return pltpu.make_async_remote_copy(
             src_ref=src, dst_ref=dst, send_sem=send, recv_sem=recv, device_id=(peer,), device_id_type=MESH
         )
-
-    vec = remote(vec_in.at[1 - core], v0, vs.at[0], vd.at[0], sibling)
-    vec.start()
-    for c, (number, row, col, *_) in enumerate(chunks):
-        for f in range(2):
-            for s in range(2):
-                yy, xx = (s, f) if c % 2 == 0 else (f, s)
-                remote(
-                    chunk_of(ins[number], row, col, yy, xx, 1 - core), r0.at[c, f, s], s0.at[c], d0.at[c], sibling
-                ).start()
-                pltpu.make_async_copy(
-                    chunk_of(ins[number], row, col, yy, xx, core), own.at[c, f, s], own_sem.at[c]
-                ).start()
 
     def along(c):
         even = lax.rem(c, 2) == 0
@@ -358,114 +409,358 @@
         def _(i):
             dst(i)[...] = dst(i)[...] + src(i)[...]
 
+    def take_credit(c):
+        if c >= LANDINGS:
+            pl.semaphore_wait(credit, 1)
+
+    def stage(c):
+        number, row, col = chunks[c][:3]
+        take_credit(c)
+        for f in range(2):
+            for s in range(2):
+                yy, xx = (s, f) if c % 2 == 0 else (f, s)
+                remote(
+                    chunk_of(ins[number], row, col, yy, xx, 1 - core), r0.at[c % LANDINGS, f, s], s0.at[c], d0.at[c],
+                    sibling,
+                ).start()
+                pltpu.make_async_copy(
+                    chunk_of(ins[number], row, col, yy, xx, core), tiles.at[c % SLOTS, core, f, s], own_sem.at[c]
+                ).start()
+
+    def make(c, left_at, right_at, depth):
+        take_credit(c)
+
+        @pl.loop(0, 4)
+        def _(zz):
+            left = arena[pl.ds(left_at, depth), pl.ds(pl.multiple_of(zz * TILE, TILE), TILE)]
+            for part in range(2):
+                cols = slice(part * (WIDE // 2), (part + 1) * (WIDE // 2))
+                result = lax.dot_general(left, arena[pl.ds(right_at, depth), cols], TN, preferred_element_type=F32)
+                result = result.astype(BF16)
+                for block in range(8):
+                    yy, xx, cc = block // 4, (block // 2) % 2, block % 2
+                    f, s = (xx, yy) if c % 2 == 0 else (yy, xx)
+                    tiles[c % SLOTS, cc, f, s, zz, :, cols] = result[block * BLOCK : (block + 1) * BLOCK]
+
+        remote(tiles.at[c % SLOTS, 1 - core], r0.at[c % LANDINGS], s0.at[c], d0.at[c], sibling).start()
+
     def first(c):
         f, fp, _, _ = along(c)
-        pltpu.make_async_copy(own.at[c], own.at[c], own_sem.at[c]).wait()
-        remote(r0.at[c], r0.at[c], s0.at[c], d0.at[c], sibling).wait_recv()
+        slot, place = c % SLOTS, c % LANDINGS
+        if c < made:
+            pltpu.make_async_copy(tiles.at[slot, core], tiles.at[slot, core], own_sem.at[c]).wait()
+        copy = remote(tiles.at[slot, 1 - core], r0.at[place], s0.at[c], d0.at[c], sibling)
+        copy.wait_recv()
         add_blocks(
-            16, lambda i: r0.at[c, i // 8, (i // 4) % 2, i % 4], lambda i: own.at[c, i // 8, (i // 4) % 2, i % 4]
+            16,
+            lambda i: r0.at[place, i // 8, (i // 4) % 2, i % 4],
+            lambda i: tiles.at[slot, core, i // 8, (i // 4) % 2, i % 4],
         )
-        remote(r0.at[c, 1 - f], r1.at[c], s1.at[c], d1.at[c], fp).start()
+        remote(r0.at[place, 1 - f], r1.at[c], s1.at[c], d1.at[c], fp).start()
+        copy.wait_send()
 
     def second(c):
         f, fp, s, sp = along(c)
-        remote(r0.at[c, 1 - f], r1.at[c], s1.at[c], d1.at[c], fp).wait_recv()
-        add_blocks(8, lambda i: r1.at[c, i // 4, i % 4], lambda i: r0.at[c, f, i // 4, i % 4])
+        place = lax.rem(c, LANDINGS)
+        copy = remote(r0.at[place, 1 - f], r1.at[c], s1.at[c], d1.at[c], fp)
+        copy.wait_recv()
+        add_blocks(8, lambda i: r1.at[c, i // 4, i % 4], lambda i: r0.at[place, f, i // 4, i % 4])
         remote(r1.at[c, 1 - s], r2.at[c], s2.at[c], d2.at[c], sp).start()
+        copy.wait_send()
+
+        @pl.when(c < total - LANDINGS)
+        def _():
+            pl.semaphore_signal(credit, inc=1, device_id=(sibling,), device_id_type=MESH)
 
     def third(c):
         _, _, s, sp = along(c)
-        remote(r1.at[c, 1 - s], r2.at[c], s2.at[c], d2.at[c], sp).wait_recv()
+        copy = remote(r1.at[c, 1 - s], r2.at[c], s2.at[c], d2.at[c], sp)
+        copy.wait_recv()
         add_blocks(4, lambda i: r2.at[c, i], lambda i: r1.at[c, s, i])
         for m in range(3):
             remote(r2.at[c, z_other[m]], r3.at[c, m], s3.at[c, m], d3.at[c, m], z_peers[m]).start()
-
-    @pl.loop(0, total + 4)
-    def _(k):
-        @pl.when(k < total)
-        def _():
-            first(k)
-
-        @pl.when((k >= 2) & (k < total + 2))
-        def _():
-            second(k - 2)
-
-        @pl.when(k >= 4)
-        def _():
-            third(k - 4)
-
-    vec.wait()
-    v0[...] += vec_in[core]
-    step = remote(v0.at[1 - x], v1, vs.at[1], vd.at[1], x_peer)
-    step.start()
-    step.wait()
-    v1[...] += v0[x]
-    step = remote(v1.at[1 - y], v2, vs.at[2], vd.at[2], y_peer)
-    step.start()
-    step.wait()
-    v2[...] += v1[y]
-    steps = [remote(v2.at[z_other[m]], v3.at[m], vs.at[3 + m], vd.at[3 + m], z_peers[m]) for m in range(3)]
-    for step in steps:
-        step.start()
-    for step in steps:
-        step.wait()
-    vec_out[...] = v2[z] + v3[0] + v3[1] + v3[2]
-
-    for c, (_, _, _, number, rows, row, col) in enumerate(chunks):
+        copy.wait_send()
+
+    def last(c):
+        number, height, row, col = chunks[c][3:]
         for m in range(3):
             remote(r2.at[c, z_other[m]], r3.at[c, m], s3.at[c, m], d3.at[c, m], z_peers[m]).wait()
         summed = r2[c, z].astype(F32) + r3[c, 0].astype(F32) + r3[c, 1].astype(F32) + r3[c, 2].astype(F32)
-        outs[number][row : row + rows, col : col + WIDE] = summed[:rows]
-
-    @pl.loop(0, total)
-    def _(c):
-        f, fp, s, sp = along(c)
-        remote(r0.at[c], r0.at[c], s0.at[c], d0.at[c], sibling).wait_send()
-        remote(r0.at[c, 1 - f], r1.at[c], s1.at[c], d1.at[c], fp).wait_send()
-        remote(r1.at[c, 1 - s], r2.at[c], s2.at[c], d2.at[c], sp).wait_send()
-
-
-def reduce_all(arrays, vectors):
+        outs[number][row : row + height, col : col + WIDE] = summed[:height]
+
+    stage(0)
+    stage(1)
+    for c in range(made):
+        first(c)
+        if c >= 5:
+            second(c - 5)
+        if c + SLOTS < made:
+            stage(c + SLOTS)
+
+    for copy in first_loads[:5]:
+        copy.wait()
+    half_lanes = LANES // 2
+    span = 2 * rows + TILE
+
+    def self_step(i):
+        h, t = lax.div(i, 2), lax.rem(i, 2)
+        lanes = pl.ds(pl.multiple_of(h * LANES, LANES), LANES)
+        own = pl.multiple_of(t * TILE, TILE)
+        mine = pl.ds(q_at + own, TILE)
+        keys = arena[pl.ds(k_at + own, span), lanes]
+        values = arena[pl.ds(v_at + own, span), lanes]
+        query = arena[mine, lanes] * jnp.asarray(0.125, BF16)
+        grad = arena[pl.ds(g_at + own, TILE), lanes]
+        inner = jnp.transpose(grad.astype(F32) * arena[pl.ds(o_at + own, TILE), lanes].astype(F32))
+        kpos = lax.broadcasted_iota(jnp.int32, (span, TILE), 0)
+        qpos = lax.broadcasted_iota(jnp.int32, (TILE, TILE), 1)
+        dpos = lax.broadcasted_iota(jnp.int32, (TILE, TILE), 0)
+        start = near["starts"][:, pl.ds(own, TILE)] - own
+        allowed = kpos >= start
+        allowed = jnp.concatenate([allowed[: span - TILE], allowed[span - TILE :] & (dpos <= qpos)], 0)
+
+        @pl.when(t == 0)
+        def _():
+            held["accum_k"][span:] = jnp.zeros((3 * rows - span, LANES), F32)
+            held["accum_v"][span:] = jnp.zeros((3 * rows - span, LANES), F32)
+            held["accum_k"][:span] = jnp.zeros((span, LANES), F32)
+            held["accum_v"][:span] = jnp.zeros((span, LANES), F32)
+
+        parts = []
+        dk = None
+        dv = None
+        for half in range(2):
+            head_q = head_lanes(query, half)
+            head_g = head_lanes(grad, half)
+            lse = near["self_lse"][h, half : half + 1, pl.ds(own, TILE)]
+            delta = jnp.sum(inner[half * half_lanes : (half + 1) * half_lanes], axis=0, keepdims=True)
+            scores = lax.dot_general(keys, head_q, NT, preferred_element_type=F32)
+            probs = jnp.where(allowed, jnp.exp(jnp.where(allowed, scores - lse, 0.0)), 0.0)
+            grad_probs = lax.dot_general(values, head_g, NT, preferred_element_type=F32)
+            grad_scores = (probs * (grad_probs - delta)).astype(BF16)
+            probs = probs.astype(BF16)
+            part_k = jnp.dot(grad_scores, head_q, preferred_element_type=F32)
+            part_v = jnp.dot(probs, head_g, preferred_element_type=F32)
+            dk = part_k if dk is None else dk + part_k
+            dv = part_v if dv is None else dv + part_v
+            parts.append(lax.dot_general(grad_scores, keys, TN, preferred_element_type=F32))
+        lane = lax.broadcasted_iota(jnp.int32, (TILE, LANES), 1)
+        arena[mine, lanes] = (jnp.where(lane < half_lanes, parts[0], parts[1]) * 0.125).astype(BF16)
+        window = pl.ds(own, span)
+        held["accum_k"][window] += dk
+        held["accum_v"][window] += dv
+
+        @pl.when(t == 1)
+        def _():
+            arena[pl.ds(k_at, 3 * rows), lanes] = held["accum_k"][...].astype(BF16)
+            arena[pl.ds(v_at, 3 * rows), lanes] = held["accum_v"][...].astype(BF16)
+
+    @pl.loop(0, 16)
+    def _(i):
+        self_step(i)
+        step = lax.div(i, 2)
+
+        @pl.when(lax.rem(i, 2) == 0)
+        def _():
+            third(step)
+
+        @pl.when((lax.rem(i, 2) == 1) & (step + made - 5 < made))
+        def _():
+            second(step + made - 5)
+
+    value_weight = fetch("value_weight", wv_at, 3)
+    value_weight.start()
+    for copy in first_loads[5:]:
+        copy.wait()
+    own_low = low_at + 2 * rows
+    make(made, own_low, q_at, rows)
+
+    def norm_grad(j):
+        @pl.loop(0, 4)
+        def _(n):
+            cols = pl.ds(pl.multiple_of(n * TILE, TILE), TILE)
+            result = lax.dot_general(
+                arena[pl.ds(k_at + j * rows, rows), :], arena[pl.ds(wk_at + n * TILE, TILE), :], NT,
+                preferred_element_type=F32,
+            )
+            result += lax.dot_general(
+                arena[pl.ds(v_at + j * rows, rows), :], arena[pl.ds(wv_at + n * TILE, TILE), :], NT,
+                preferred_element_type=F32,
+            )
+            if j == 2:
+                result += lax.dot_general(
+                    arena[pl.ds(q_at, rows), :], arena[pl.ds(wq_at + n * TILE, TILE), :], NT,
+                    preferred_element_type=F32,
+                )
+            sums[0, :, cols] = result
+
+    vec[...] = near["vectors"][...]
+
+    STEP = 64
+
+    def gains(j, token_at):
+        @pl.loop(0, rows // STEP)
+        def _(i):
+            here = pl.ds(pl.multiple_of(i * STEP, STEP), STEP)
+            unit, _ = normalise_rows(arena[pl.ds(token_at + i * STEP, STEP), :].astype(F32))
+            grad = sums[0, here, :]
+            vec[0:1] += jnp.sum(grad * unit, axis=0, keepdims=True)
+            vec[1:2] += jnp.sum(grad, axis=0, keepdims=True)
+
+    value_weight.wait()
+    norm_grad(1)
+    first(made)
+    make(made + 1, low_at, k_at, 3 * rows)
+    third(8)
+    first(made + 1)
+    make(made + 2, low_at, v_at, 3 * rows)
+    third(9)
+    first(made + 2)
+    token_copy = fetch("near_tokens", low_at, 5)
+    token_copy.start()
+    grad_copy = pltpu.make_async_copy(hbm["grad_one"], sums.at[1], load.at[0])
+    grad_copy.start()
+    token_copy.wait()
+    back_one, back_two = held["back_one"], held["back_two"]
+    bs, bd = held["bs"], held["bd"]
+    gains(1, low_at + rows)
+
+    def as_low(dst, extra):
+        @pl.loop(0, rows // STEP)
+        def _(i):
+            here = pl.ds(pl.multiple_of(i * STEP, STEP), STEP)
+            value = sums[0, here, :]
+            if extra is not None:
+                value = value + jnp.where(core == 1, extra[here, :].astype(F32), 0.0)
+            dst[here, :] = value.astype(BF16)
+
+    as_low(back_one.at[0], None)
+    swap = remote(back_one.at[0], back_one.at[1], bs.at[0], bd.at[0], sibling)
+    swap.start()
+    norm_grad(0)
+    gains(0, low_at)
+    swap.wait()
+    as_low(back_two.at[0], back_one.at[1])
+    send_back = remote(back_two.at[0], back_two.at[1], bs.at[1], bd.at[1], me - 2)
+
+    @pl.when(has_before)
+    def _():
+        send_back.start()
+
+    norm_grad(2)
+    gains(2, low_at + 2 * rows)
+
+    vs, vd = held["vs"], held["vd"]
+    vec_in = held["vec_in"]
+
+    def vec_step(number, peer, slot):
+        step = remote(vec, vec_in.at[slot], vs.at[number], vd.at[number], peer)
+        step.start()
+        return step
+
+    step = vec_step(0, sibling, 0)
+    step.wait()
+    vec[...] += vec_in[0]
+    step = vec_step(1, x_peer, 1)
+    for c in range(10, made):
+        third(c)
+    step.wait()
+    vec[...] += vec_in[1]
+    step = vec_step(2, y_peer, 2)
+    for c in range(made, total):
+        second(c)
+    step.wait()
+    vec[...] += vec_in[2]
+    steps = [vec_step(3 + m, z_peers[m], 3 + m) for m in range(3)]
+
+    grad_copy.wait()
+
+    @pl.when(has_before)
+    def _():
+        send_back.wait_send()
+
+    @pl.when(has_after)
+    def _():
+        send_back.wait_recv()
+
+    gain = near["attn_gain"][...]
+
+    @pl.loop(0, rows // STEP)
+    def _(i):
+        here = pl.ds(pl.multiple_of(i * STEP, STEP), STEP)
+        unit, scale = normalise_rows(arena[pl.ds(low_at + 2 * rows + i * STEP, STEP), :].astype(F32))
+        grad = sums[0, here, :]
+        grad = grad + jnp.where(core == 0, back_one[1, here, :].astype(F32), 0.0)
+        grad = grad + jnp.where(has_after, back_two[1, here, :].astype(F32), 0.0)
+        scaled = grad * gain
+        back = scale * (
+            scaled - jnp.mean(scaled, axis=-1, keepdims=True) - unit * jnp.mean(scaled * unit, axis=-1, keepdims=True)
+        )
+        sums[1, here, :] += back
+
+    out_copy = pltpu.make_async_copy(sums.at[1], input_grad, load.at[0])
+    out_copy.start()
+
+    for c in range(made, total):
+        third(c)
+    for step in steps:
+        step.wait()
+    vec_out[...] = vec[...] + vec_in[3] + vec_in[4] + vec_in[5]
+    for c in range(total):
+        last(c)
+    out_copy.wait()
+
+
+def layer_tail(arrays, hbm, vmem, rows):
     ins = []
     chunks = []
     shapes = []
-    for array, rows in arrays:
+    for array, height_out in arrays:
         height = array.shape[0] // 32
         cols = array.shape[1]
         number = len(ins)
         ins.append(array.reshape(4, 2, 2, 2, height, cols))
-        shapes.append((rows, cols))
+        shapes.append((height_out, cols))
         for row in range(0, height, BLOCK):
             for col in range(0, cols, WIDE):
-                chunks.append((number, row, col, number, min(BLOCK, rows - row), row, col))
+                chunks.append((number, row, col, number, min(BLOCK, height_out - row), row, col))
+    for i in range(3):
+        chunks.append((None, 0, 0, len(shapes), BLOCK, 0, 0))
+        shapes.append((BLOCK, WIDE))
     total = len(chunks)
-    kinds = vectors.shape[0]
-    vec = jnp.pad(vectors.reshape(kinds, 32, 32).transpose(1, 0, 2), ((0, 0), (0, 8 - kinds), (0, LANES - 32)))
-    vec = vec.reshape(4, 2, 2, 2, 8, LANES).transpose(3, 2, 1, 0, 4, 5)
-    vmem = pl.BlockSpec(memory_space=pltpu.VMEM)
+    local = pl.BlockSpec(memory_space=pltpu.VMEM)
+    anywhere = pl.BlockSpec(memory_space=pl.ANY)
     dma = pltpu.SemaphoreType.DMA
+    width = hbm["queries"].shape[1]
+    scratch = dict(
+        arena=pltpu.VMEM((16 * rows, width), BF16),
+        sums=pltpu.VMEM((2, rows, width), F32),
+        accum_k=pltpu.VMEM((3 * rows, LANES), F32),
+        accum_v=pltpu.VMEM((3 * rows, LANES), F32),
+        back_one=pltpu.VMEM((2, rows, width), BF16),
+        back_two=pltpu.VMEM((2, rows, width), BF16),
+        vec=pltpu.VMEM((8, width), F32),
+        vec_in=pltpu.VMEM((6, 8, width), F32),
+        tiles=pltpu.VMEM((SLOTS, 2, 2, 2, 4, BLOCK, WIDE), BF16),
+        r0=pltpu.VMEM((LANDINGS, 2, 2, 4, BLOCK, WIDE), BF16),
+        r1=pltpu.VMEM((total, 2, 4, BLOCK, WIDE), BF16),
+        r2=pltpu.VMEM((total, 4, BLOCK, WIDE), BF16),
+        r3=pltpu.VMEM((total, 3, BLOCK, WIDE), BF16),
+        load=dma((8,)), own_sem=dma((total,)), s0=dma((total,)), d0=dma((total,)), s1=dma((total,)), d1=dma((total,)),
+        s2=dma((total,)), d2=dma((total,)), s3=dma((total, 3)), d3=dma((total, 3)), vs=dma((6,)), vd=dma((6,)),
+        bs=dma((2,)), bd=dma((2,)), credit=pltpu.SemaphoreType.REGULAR,
+    )
     results = pl.pallas_call(
-        functools.partial(reduce_kernel, chunks, len(ins), len(ins)),
-        in_specs=[pl.BlockSpec(memory_space=pl.ANY)] * len(ins) + [vmem],
-        out_specs=[vmem] * (len(ins) + 1),
-        out_shape=[jax.ShapeDtypeStruct(shape, F32) for shape in shapes] + [jax.ShapeDtypeStruct((8, LANES), F32)],
-        scratch_shapes=[
-            pltpu.VMEM((total, 2, 2, 4, BLOCK, WIDE), BF16),
-            pltpu.VMEM((total, 2, 2, 4, BLOCK, WIDE), BF16),
-            pltpu.VMEM((total, 2, 4, BLOCK, WIDE), BF16),
-            pltpu.VMEM((total, 4, BLOCK, WIDE), BF16),
-            pltpu.VMEM((total, 3, BLOCK, WIDE), BF16),
-            pltpu.VMEM((2, 2, 4, 8, LANES), F32),
-            pltpu.VMEM((2, 4, 8, LANES), F32),
-            pltpu.VMEM((4, 8, LANES), F32),
-            pltpu.VMEM((3, 8, LANES), F32),
-            dma((total,)), dma((total,)), dma((total,)), dma((total,)), dma((total,)), dma((total,)), dma((total,)),
-            dma((total, 3)), dma((total, 3)), dma((6,)), dma((6,)),
-        ],
-        compiler_params=pltpu.CompilerParams(collective_id=0, has_side_effects=True, vmem_limit_bytes=62 << 20),
-        cost_estimate=pl.CostEstimate(flops=1 << 20, bytes_accessed=64 << 20, transcendentals=0),
-    )(*ins, vec)
-    return results[:-1], results[-1][:kinds, :32]
+        functools.partial(layer_kernel, chunks, rows, len(ins), len(shapes)),
+        in_specs=[anywhere] * (len(ins) + len(IN_HBM)) + [local] * len(IN_VMEM),
+        out_specs=[local] * (len(shapes) + 1) + [anywhere],
+        out_shape=[jax.ShapeDtypeStruct(shape, F32) for shape in shapes]
+        + [jax.ShapeDtypeStruct((8, width), F32), jax.ShapeDtypeStruct((rows, width), F32)],
+        scratch_shapes=[scratch[name] for name in SCRATCH],
+        compiler_params=pltpu.CompilerParams(collective_id=0, has_side_effects=True, vmem_limit_bytes=63 << 20),
+        cost_estimate=pl.CostEstimate(flops=1 << 34, bytes_accessed=64 << 20, transcendentals=0),
+    )(*ins, *[hbm[name] for name in IN_HBM], *[vmem[name] for name in IN_VMEM])
+    return results[:-2], results[-2], results[-1]
 
 
 def matmul(left, right):
@@ -612,47 +907,59 @@
 
     output_weight_grad = left_product(self_att, grad_one_low).astype(BF16)
     grad_self = right_product(grad_one_low, output_weight).astype(BF16)
-    grad_q, grad_k, grad_v = attend_backward(
-        queries, near_keys, near_values, grad_self, self_att, self_lse,
-        own_ids[None, :], windows[:, :, None], numbers, True, self_sizes, self_ends,
-    )
-    grad_near = right_product(grad_k, key_weight) + right_product(grad_v, value_weight)
-    grad_own = grad_near[REACH * rows :] + right_product(grad_q, query_weight)
-    to_two = grad_near[:rows]
-    to_one = grad_near[rows : REACH * rows].astype(BF16)
-    from_swap = lax.ppermute(to_one, AXIS, swap).astype(F32)
-    to_two = (to_two + jnp.where(odd, from_swap, 0.0)).astype(BF16)
-    from_two = lax.ppermute(to_two, AXIS, behind).astype(F32)
-    near_sum = jnp.concatenate([grad_near[: REACH * rows], grad_own], 0)
-    attn_gain_grad = jnp.sum(near_sum * near_unit, axis=0)
-    attn_bias_grad = jnp.sum(near_sum, axis=0)
-    grad_norm_one = grad_own + from_two + jnp.where(odd, 0.0, from_swap)
-    unit_one = near_unit[REACH * rows :]
-    input_grad = grad_one + norm_back(grad_norm_one, unit_one, near_scale[REACH * rows :], attn_gain)
-    query_grad = left_product(low_one, grad_q).astype(BF16)
-    key_grad = left_product(near_low, grad_k).astype(BF16)
-    value_grad = left_product(near_low, grad_v).astype(BF16)
     grads = [
-        down_grad, up_grad, cross_output_grad, cross_query_grad, cross_key_grad, cross_value_grad,
-        output_weight_grad, query_grad, key_grad, value_grad,
+        down_grad, up_grad, cross_output_grad, cross_query_grad, cross_key_grad, cross_value_grad, output_weight_grad,
     ]
-    vectors = jnp.stack(
-        [attn_gain_grad, attn_bias_grad, cross_gain_grad, cross_bias_grad, mlp_gain_grad, mlp_bias_grad]
-    )
+    none = jnp.zeros_like(attn_gain)
+    vectors = jnp.stack([none, none, cross_gain_grad, cross_bias_grad, mlp_gain_grad, mlp_bias_grad, none, none])
     if fused:
         share = text // count
         caption_blocks = jnp.pad(caption_grad.reshape(count, share, width), ((0, 0), (0, BLOCK - share), (0, 0)))
         arrays = [(grad, grad.shape[0] // count) for grad in grads]
         arrays.append((caption_blocks.reshape(count * BLOCK, width), share))
-        sums, small = reduce_all(arrays, vectors)
+        starts = jnp.sum((near_ids[None, :] < own_ids[:, None]).astype(jnp.int32), axis=1)
+        sums, small, input_grad = layer_tail(
+            arrays,
+            dict(
+                queries=queries, near_keys=near_keys, near_values=near_values, self_att=self_att, grad_self=grad_self,
+                near_low=near_low, near_tokens=near_tokens, grad_one=grad_one,
+                query_weight=query_weight, key_weight=key_weight, value_weight=value_weight,
+            ),
+            dict(vectors=vectors, starts=starts[None, :], self_lse=self_lse, attn_gain=attn_gain[None, :]),
+            rows,
+        )
+        (down_out, up_out, cross_output_out, cross_query_out, cross_key_out, cross_value_out,
+         output_out, caption_out, query_out, key_out, value_out) = sums
+        small = lax.dynamic_slice_in_dim(small, device * (width // count), width // count, 1)
     else:
+        grad_q, grad_k, grad_v = attend_backward(
+            queries, near_keys, near_values, grad_self, self_att, self_lse,
+            own_ids[None, :], windows[:, :, None], numbers, True, self_sizes, self_ends,
+        )
+        grad_near = right_product(grad_k, key_weight) + right_product(grad_v, value_weight)
+        grad_own = grad_near[REACH * rows :] + right_product(grad_q, query_weight)
+        to_two = grad_near[:rows]
+        to_one = grad_near[rows : REACH * rows].astype(BF16)
+        from_swap = lax.ppermute(to_one, AXIS, swap).astype(F32)
+        to_two = (to_two + jnp.where(odd, from_swap, 0.0)).astype(BF16)
+        from_two = lax.ppermute(to_two, AXIS, behind).astype(F32)
+        near_sum = jnp.concatenate([grad_near[: REACH * rows], grad_own], 0)
+        attn_gain_grad = jnp.sum(near_sum * near_unit, axis=0)
+        attn_bias_grad = jnp.sum(near_sum, axis=0)
+        grad_norm_one = grad_own + from_two + jnp.where(odd, 0.0, from_swap)
+        unit_one = near_unit[REACH * rows :]
+        input_grad = grad_one + norm_back(grad_norm_one, unit_one, near_scale[REACH * rows :], attn_gain)
+        query_grad = left_product(low_one, grad_q).astype(BF16)
+        key_grad = left_product(near_low, grad_k).astype(BF16)
+        value_grad = left_product(near_low, grad_v).astype(BF16)
+        vectors = vectors.at[0].set(attn_gain_grad).at[1].set(attn_bias_grad)
         sums = [
             reduce_scatter(grad, one_way if i % 2 else other_way, BF16, count)
-            for i, grad in enumerate([*grads, caption_grad])
+            for i, grad in enumerate([*grads, query_grad, key_grad, value_grad, caption_grad])
         ]
         small = reduce_scatter(vectors.T, one_way, F32, count).T
-    (down_out, up_out, cross_output_out, cross_query_out, cross_key_out, cross_value_out,
-     output_out, query_out, key_out, value_out, caption_out) = sums
+        (down_out, up_out, cross_output_out, cross_query_out, cross_key_out, cross_value_out,
+         output_out, query_out, key_out, value_out, caption_out) = sums
     return (
         block_output, input_grad, caption_out,
         query_out, key_out, value_out, output_out,

time: 515 us -> 456 us (0.89)
  matrix products: 135 us -> 102 us
  Pallas kernels: 262 us -> 291 us
  other arithmetic: 34.1 us -> 9.28 us
  waiting for transfers between devices: 38.6 us -> 18.8 us
  starting transfers between devices: 13.5 us -> 4.98 us
    pallas_call x1, Pallas kernels: 186 us -> 233 us  [layer_tail(): pl.pallas_call(functools.partial(layer_kernel, chunks, rows, len(ins), le...]
    pallas_call x2 -> x1, Pallas kernels: 43.9 us -> 21.7 us  [attend_backward(): pl.pallas_call(functools.partial(backward_kernel, causal, sizes, ends), g...]
    ppermute x2 -> x0, waiting for transfers between devices: 19.4 us -> none  [the longest x1 19.4 us: body(): from_two = lax.ppermute(to_two, AXIS, behind).astype(F32)]
    dot_general x10 -> x7, matrix products: 47.6 us -> 33.2 us  [left_product(): return lax.dot_general(left, right, TN, preferred_element_type=F32)]
    dot_general x10 -> x7, matrix products: 45.1 us -> 32.4 us  [right_product(): return lax.dot_general(left, right, NT, preferred_element_type=F32)]
    reduce_sum x4 -> x1, other arithmetic: 11.3 us -> 1.09 us  [body(): jnp.sum((near_ids[None, :] < own_ids[:, None]).astype(jnp.int32), axis=1)]
    ppermute x2 -> x0, starting transfers between devices: 8.47 us -> none  [the longest x1 7.04 us: body(): from_swap = lax.ppermute(to_one, AXIS, swap).astype(F32)]
    dot_general x10, matrix products: 42.1 us -> 36.5 us  [matmul(): return jnp.dot(left, right, preferred_element_type=F32)]
  transfers between devices with their start and end apart: 4 -> 2, of which waited for: 2 -> 1; matrix products, arithmetic and copies ran while one was open for 6% -> 2% of each run, Pallas kernels for 0% -> 0%
where the time goes in v3:
time: 456 us; the launch traced here: 451 us
  Pallas kernels  291 us (64%)
  matrix products  102 us (22%)
  local copies, waits for them, and re-layouts  23.3 us (5%)
  waiting for transfers between devices  18.8 us (4%)
  other arithmetic  9.28 us (2%)
  starting transfers between devices  4.98 us (1%)
    pallas_call x1, Pallas kernels, layer_tail(): pl.pallas_call(functools.partial(layer_kernel, chunks, rows, len(ins), le...  233 us
    pallas_call x2, Pallas kernels, attend_forward(): pl.pallas_call(functools.partial(forward_kernel, causal, sizes, ends), gr...  37 us
    dot_general x10, matrix products, matmul(): return jnp.dot(left, right, preferred_element_type=F32)  36.5 us
    dot_general x7, matrix products, left_product(): return lax.dot_general(left, right, TN, preferred_element_type=F32)  33.2 us
    dot_general x7, matrix products, right_product(): return lax.dot_general(left, right, NT, preferred_element_type=F32)  32.4 us
    pallas_call x1, Pallas kernels, attend_backward(): pl.pallas_call(functools.partial(backward_kernel, causal, sizes, ends), g...  21.7 us
    ppermute x1, waiting for transfers between devices, body(): block_two = lax.ppermute(tokens, AXIS, ahead)  18.8 us
    unnamed x105, local copies, waits for them, and re-layouts  16.8 us
  transfers between devices with their start and end apart: 2, of which 1 were waited for; matrix products, arithmetic and copies ran while one was open for 2% of the time, Pallas kernels for 0%

profile of v3, /device:TPU:0, one launch (start us, length us, event | category | flops | bytes accessed | tf_op | source)
XLA Modules:
  0.0 451.2 jit_solution(9929736622335219741)
XLA Ops:
  0.7 4.9 %collective-permute-start = (bf16[512,1024]{1,0:T(8,128)(2,1)}, bf16[512,1024]{1,0:T(8,128)(2,1)S(1)}, u32[]{:S(2)}, u32[]{:S(2)}) collective-permute-start(bf16[512,1024]{1,0:T(8,128)(2,1)} %param.23), channel_id=1, source_target_pairs={{0,2},{1,3},{2,4},{3,5},{4,6},{5,7},{6,8},{7,9},{8,10},{9,11},{10,... | collective-permute-start | bytes 3145736 | tf_op jit(solution)/shard_map/ppermute | solution.py:823
  5.6 0.9 pad_dynamic-slice_fusion.1
  6.4 0.8 pad_dynamic-slice_fusion.2
  7.3 0.7 multiply_add_fusion.2
  8.4 0.8 pad_dynamic-slice_fusion.3
  9.5 18.8 %collective-permute-done = bf16[512,1024]{1,0:T(8,128)(2,1)S(1)} collective-permute-done((bf16[512,1024]{1,0:T(8,128)(2,1)}, bf16[512,1024]{1,0:T(8,128)(2,1)S(1)}, u32[]{:S(2)}, u32[]{:S(2)}) %collective-permute-start) | collective-permute-done | bytes 1048608 | tf_op jit(solution)/shard_map/ppermute | solution.py:823
  28.2 1.7 broadcast_select_fusion
  30.0 1.1 convert_reduce_fusion.1
  31.2 1.3 convolution_convert_fusion.12.k_ref
  32.4 0.3 copy-done.34
  32.8 1.2 convolution_convert_fusion.11.v_ref
  34.1 1.5 copy-done.7
  35.7 0.5 convert_reduce_fusion
  36.2 1.0 fusion.2
  37.3 1.7 fusion.5.refs_13_
  39.1 1.3 convolution_convert_fusion.14.q_ref.refs_8_
  40.4 1.5 copy-done.38
  41.8 4.7 %convolution_convert_fusion.2.v_ref.refs_10_ = bf16[1536,1024]{1,0:T(8,128)(2,1)} fusion(bf16[1536,1024]{1,0:T(8,128)(2,1)S(1)} %fusion.5.refs_13_, bf16[1024,1024]{1,0:T(8,128)(2,1)S(1)} %copy-done.38), kind=kOutput, calls=%fused_computation.15 | convolution fusion | flops 3222798336 | bytes 8388608 | tf_op jit(solution)/shard_map/dot_general | solution.py:767
  46.6 3.6 convolution_convert_fusion.3.k_ref.refs_9_
  50.3 19.5 %shard_map.366 = (bf16[512,1024]{1,0:T(8,128)(2,1)S(1)}, f32[8,2,512]{2,1,0:T(2,128)S(1)}) custom-call(s32[2]{0:T(128)S(1)} %subtract_clamp_fusion.n_ref, s32[512,1]{1,0:T(8,128)S(1)} %copy.44.qid_ref, s32[2,1,1280]{2,1,0:T(1,128)S(1)} %broadcast_in_dim.25.kid_ref, bf16[512,1024]{1,0:T(8,128)(2,1)S(1)} %convolution_convert_fusion.14.q_ref.refs_8_, ...), custom_call_target="tpu_custom_call" | custom-call | flops 10737418240 | bytes 8388608 | tf_op jit(solution)/shard_map/pallas_call | solution.py:82
  69.8 1.4 fusion.18
  71.2 0.3 multiply_reduce_fusion.5
  71.9 0.9 copy-done.28
  72.8 1.3 convolution_convert_fusion.13.q_ref
  74.2 17.5 %shard_map.367 = (bf16[512,1024]{1,0:T(8,128)(2,1)S(1)}, f32[8,2,512]{2,1,0:T(2,128)S(1)}) custom-call(s32[2]{0:T(128)S(1)} %broadcast.159.n_ref, s32[512,1]{1,0:T(8,128)S(1)} %copy.45.qid_ref, s32[2,1,512]{2,1,0:T(1,128)S(1)} %broadcast_in_dim_broadcast_in_dim.4.kid_ref, bf16[512,1024]{1,0:T(8,128)(2,1)S(1)} %convolution_convert_fusion.13.q_ref, ...), custom_call_target="tpu_custom_call" | custom-call | flops 4294967296 | bytes 8388608 | tf_op jit(solution)/shard_map/pallas_call | solution.py:82
  91.7 1.4 fusion.19
  93.1 0.3 multiply_reduce_fusion.4
  93.8 10.6 %fusion.17 = f32[512,4096]{1,0:T(8,128)} fusion(bf16[1024,4096]{1,0:T(8,128)(2,1)} %param.34, f32[512,1024]{1,0:T(8,128)S(1)} %get-tuple-element.80, f32[1024]{0:T(1024)S(1)} %copy-done.41, f32[1024]{0:T(1024)S(1)} %copy-done.23, f32[512]{0:T(512)S(1)} %add_rsqrt_fusion.1, f32[512]{0:T(512)S(1)} %broadcast_multiply_fusion.5), kind=kOutput, calls=%fused_computation.101 | convolution fusion | flops 4297588736 | bytes 18886656 | tf_op jit(solution)/shard_map/dot_general | solution.py:767
  104.4 9.7 %add_convert_fusion.1 = bf16[512,1024]{1,0:T(8,128)(2,1)} fusion(f32[512,1024]{1,0:T(8,128)S(1)} %get-tuple-element.80, bf16[4096,1024]{1,0:T(8,128)(2,1)S(1)} %bitcast.85, f32[512,4096]{1,0:T(8,128)} %fusion.17), kind=kOutput, calls=%fused_computation.25 | convolution fusion | flops 4314890240 | bytes 19922944 | tf_op jit(solution)/shard_map/dot_general | solution.py:767
  114.1 14.5 %multiply_convert_fusion = bf16[512,4096]{1,0:T(8,128)(2,1)} fusion(f32[512,4096]{1,0:T(8,128)} %fusion.17, bf16[512,1024]{1,0:T(8,128)(2,1)S(1)} %copy-done.10, bf16[4096,1024]{1,0:T(8,128)(2,1)} %param.35), kind=kOutput, calls=%fused_computation | convolution fusion | flops 4332716032 | bytes 22020096 | tf_op jit(solution)/shard_map/dot_general | solution.py:775
  128.6 12.6 %convolution_convert_fusion.1 = bf16[4096,1024]{1,0:T(8,128)(2,1)} fusion(bf16[512,1024]{1,0:T(8,128)(2,1)S(1)} %copy-done.10, f32[512,4096]{1,0:T(8,128)} %fusion.17), kind=kOutput, calls=%fused_computation.8 | convolution fusion | flops 4318035968 | bytes 17825792 | tf_op jit(solution)/shard_map/dot_general | solution.py:771
  141.1 9.0 %multiply_reduce_fusion = (f32[1024]{0:T(1024)S(1)}, f32[512]{0:T(512)S(1)}, f32[512]{0:T(512)S(1)}, f32[1024]{0:T(1024)S(1)}, f32[512,1024]{1,0:T(8,128)S(1)}) fusion(f32[512,1024]{1,0:T(8,128)S(1)} %get-tuple-element.80, f32[512]{0:T(512)S(1)} %add_rsqrt_fusion.1, f32[512]{0:T(512)S(1)} %broadcast_multiply_fusion.5, f32[1024]{0:T(1024)S(1)} %copy-done.23, ...), kind=kOutput, calls=%fused_computation.18 | convolution fusion | flops 4299682816 | bytes 16797696 | tf_op jit(solution)/shard_map/dot_general | solution.py:775
  150.1 0.8 multiply_add_fusion.1
  150.9 2.3 convolution_convert_fusion.10.g_ref
  153.2 2.6 convolution_convert_fusion.8
  155.9 7.2 %convolution_convert_fusion = bf16[1024,4096]{1,0:T(8,128)(2,1)} fusion(bf16[512,4096]{1,0:T(8,128)(2,1)S(1)} %copy-done.43, f32[512,1024]{1,0:T(8,128)S(1)} %get-tuple-element.80, f32[1024]{0:T(1024)S(1)} %copy-done.41, f32[1024]{0:T(1024)S(1)} %copy-done.23, f32[512]{0:T(512)S(1)} %add_rsqrt_fusion.1, f32[512]{0:T(512)S(1)} %broadcast_multiply_fusion.5), kind=kOutput, calls=%fused_computation.7 | convolution fusion | flops 4301783040 | bytes 14692352 | tf_op jit(solution)/shard_map/dot_general | solution.py:771
  163.2 21.7 %shard_map.368 = (bf16[512,1024]{1,0:T(8,128)(2,1)S(1)}, bf16[512,1024]{1,0:T(8,128)(2,1)S(1)}, bf16[512,1024]{1,0:T(8,128)(2,1)S(1)}) custom-call(s32[2]{0:T(128)S(1)} %broadcast.159.n_ref, s32[1,512]{1,0:T(1,128)S(1)} %bitcast.74, s32[2,512,1]{2,1,0:T(8,128)S(1)} %broadcast_in_dim_broadcast_in_dim.5.kid_ref, ...), custom_call_target="tpu_custom_call" | custom-call | flops 10737418240 | bytes 12582912 | tf_op jit(solution)/shard_map/pallas_call | solution.py:188
  184.9 2.8 convolution_convert_fusion.7
  187.8 1.8 multiply_reduce_fusion.1
  189.6 0.7 multiply_add_fusion.refs_15_
  190.3 0.9 copy-done.31
  191.2 2.3 convolution_convert_fusion.9.refs_12_
  193.5 2.7 convolution_convert_fusion.4
  196.1 1.3 fusion.20
  197.5 2.6 convolution_convert_fusion.6
  200.1 2.6 convolution_convert_fusion.5
  202.7 1.3 add_convert_fusion
  204.0 1.6 pad.5
  205.6 0.7 stack.31.refs_19_
  206.3 232.6 %shard_map.369 = (f32[128,1024]{1,0:T(8,128)}, f32[32,4096]{1,0:T(8,128)}, f32[32,1024]{1,0:T(8,128)}, f32[32,1024]{1,0:T(8,128)}, f32[32,1024]{1,0:T(8,128)}, /...) custom-call(bf16[4,2,2,2,128,1024]{5,4,3,2,1,0:T(8,128)(2,1)} %bitca, ...), custom_call_target="tpu_custom_call" | custom-call | flops 17179869184 | bytes 67108864 | tf_op jit(solution)/shard_map/pallas_call | solution.py:753
  438.8 0.8 constant_dynamic-slice_fusion
  439.6 0.5 slice_bitcast_fusion
  440.2 3.3 copy.60
  443.5 0.6 copy.61
  444.1 0.7 copy.62
  444.8 0.7 copy.63
  445.4 0.7 copy.64
  446.1 0.7 copy.65
  446.7 0.7 copy.66
  447.4 0.7 copy.67
  448.1 0.7 copy.68
  448.7 0.7 copy.69
  449.4 0.8 copy.70
  450.2 0.8 copy.71
  (116 shorter events, 2.0 us)
Async XLA Ops:
  0.7 27.6 %collective-permute-start = (bf16[512,1024]{1,0:T(8,128)(2,1)}, bf16[512,1024]{1,0:T(8,128)(2,1)S(1)}, u32[]{:S(2)}, u32[]{:S(2)}) collective-permute-start(bf16[512,1024]{1,0:T(8,128)(2,1)} %param.23), channel_id=1, source_target_pairs={{0,2},{1,3},{2,4},{3,5},{4,6},{5,7},{6,8},{7,9},{8,10},{9,11},{10,... | collective-permute-start | bytes 3145736 | tf_op jit(solution)/shard_map/ppermute | solution.py:823
  9.4 21.7 %copy-start.26 = (s32[4,128]{1,0:T(4,128)S(1)}, s32[4,128]{1,0:T(4,128)}, u32[]{:S(2)}) copy-start(s32[4,128]{1,0:T(4,128)} %param.43) | copy-start | bytes 6148
  9.4 21.7 %copy-start.32 = (bf16[1024,1024]{1,0:T(8,128)(2,1)S(1)}, bf16[1024,1024]{1,0:T(8,128)(2,1)}, u32[]{:S(2)}) copy-start(bf16[1024,1024]{1,0:T(8,128)(2,1)} %param.31) | copy-start | bytes 6291460
  9.5 21.7 %copy-start.39 = (bf16[512,1024]{1,0:T(8,128)(2,1)S(1)}, bf16[512,1024]{1,0:T(8,128)(2,1)}, u32[]{:S(2)}) copy-start(bf16[512,1024]{1,0:T(8,128)(2,1)} %param.25) | copy-start | bytes 3145732
  30.0 4.1 collective-permute-start.1
  31.2 1.6 copy-start.34
  34.0 40.2 %copy-start.3 = (bf16[512,1024]{1,0:T(8,128)(2,1)}, bf16[512,1024]{1,0:T(8,128)(2,1)S(1)}, u32[]{:S(2)}) copy-start(bf16[512,1024]{1,0:T(8,128)(2,1)S(1)} %convolution_convert_fusion.11.v_ref) | copy-start | bytes 3145732
  34.0 1.6 copy-start.7
  35.7 1.6 copy-start.6
  36.2 1.1 copy-start.22
  36.2 1.1 copy-start.25
  37.3 1.8 copy-start.36
  39.1 7.5 %copy-start.8 = (bf16[1536,1024]{1,0:T(8,128)(2,1)}, bf16[1536,1024]{1,0:T(8,128)(2,1)S(1)}, u32[]{:S(2)}) copy-start(bf16[1536,1024]{1,0:T(8,128)(2,1)S(1)} %fusion.5.refs_13_) | copy-start | bytes 9437188
  39.1 2.7 copy-start.38
  41.8 8.4 %copy-start.2 = (bf16[512,1024]{1,0:T(8,128)(2,1)}, bf16[512,1024]{1,0:T(8,128)(2,1)S(1)}, u32[]{:S(2)}) copy-start(bf16[512,1024]{1,0:T(8,128)(2,1)S(1)} %convolution_convert_fusion.14.q_ref.refs_8_) | copy-start | bytes 3145732
  41.8 4.8 %copy-start.37 = (bf16[1024,1024]{1,0:T(8,128)(2,1)S(1)}, bf16[1024,1024]{1,0:T(8,128)(2,1)}, u32[]{:S(2)}) copy-start(bf16[1024,1024]{1,0:T(8,128)(2,1)} %refs_17_.1) | copy-start | bytes 6291460
  50.2 19.5 %copy-start.4 = (bf16[1536,1024]{1,0:T(8,128)(2,1)}, bf16[1536,1024]{1,0:T(8,128)(2,1)S(1)}, u32[]{:S(2)}) copy-start(bf16[1536,1024]{1,0:T(8,128)(2,1)S(1)} %convolution_convert_fusion.3.k_ref.refs_9_) | copy-start | bytes 9437188
  50.2 19.5 %copy-start.30 = (bf16[1024,1024]{1,0:T(8,128)(2,1)S(1)}, bf16[1024,1024]{1,0:T(8,128)(2,1)}, u32[]{:S(2)}) copy-start(bf16[1024,1024]{1,0:T(8,128)(2,1)} %param.29) | copy-start | bytes 6291460
  69.8 1.4 copy-start.5
  69.8 123.7 %copy-start = (bf16[512,1024]{1,0:T(8,128)(2,1)}, bf16[512,1024]{1,0:T(8,128)(2,1)S(1)}, u32[]{:S(2)}) copy-start(bf16[512,1024]{1,0:T(8,128)(2,1)S(1)} %get-tuple-element.39.refs_11_) | copy-start | bytes 3145732
  71.2 0.7 copy-start.24
  71.2 1.6 copy-start.28
  71.2 1.6 copy-start.42
  74.2 17.5 %copy-start.27 = (bf16[1024,1024]{1,0:T(8,128)(2,1)S(1)}, bf16[1024,1024]{1,0:T(8,128)(2,1)}, u32[]{:S(2)}) copy-start(bf16[1024,1024]{1,0:T(8,128)(2,1)} %param.33) | copy-start | bytes 6291460
  91.7 61.5 %copy-start.1 = (bf16[512,1024]{1,0:T(8,128)(2,1)}, bf16[512,1024]{1,0:T(8,128)(2,1)S(1)}, u32[]{:S(2)}) copy-start(bf16[512,1024]{1,0:T(8,128)(2,1)S(1)} %get-tuple-element.40.o_ref) | copy-start | bytes 3145732
  93.1 0.7 copy-start.23
  93.1 0.7 copy-start.41
  93.1 11.2 %slice-start = ((s8[8388608]{0:T(1024)(128)(4,1)}), s8[4194304]{0:T(1024)(128)(4,1)S(1)}, s32[]{:S(2)}) async-start(s8[8388608]{0:T(1024)(128)(4,1)} %bitcast.84), calls=%async_computation | async-start | bytes 8388608
  93.8 10.6 %slice-start.1 = ((s8[8388608]{0:T(1024)(128)(4,1)}), s8[4194304]{0:T(1024)(128)(4,1)S(1)}, s32[]{:S(2)}) async-start(s8[8388608]{0:T(1024)(128)(4,1)} %bitcast.84), calls=%async_computation.1 | async-start | bytes 8388608
  104.4 9.7 %copy-start.10 = (bf16[512,1024]{1,0:T(8,128)(2,1)S(1)}, bf16[512,1024]{1,0:T(8,128)(2,1)}, u32[]{:S(2)}) copy-start(bf16[512,1024]{1,0:T(8,128)(2,1)} %param.24) | copy-start | bytes 3145732
  153.2 2.6 copy-start.43
  184.9 2.9 copy-start.29
  189.6 1.6 copy-start.31
  191.2 2.3 copy-start.9
  193.5 2.7 copy-start.33
  196.1 1.3 copy-start.40
  200.1 2.6 copy-start.35
  440.1 3.3 copy-start.21
  440.1 4.0 copy-start.20
  440.1 4.6 %copy-start.19 = (f32[32,1024]{1,0:T(8,128)S(1)}, f32[32,1024]{1,0:T(8,128)}, u32[]{:S(2)}) copy-start(f32[32,1024]{1,0:T(8,128)} %get-tuple-element.108) | copy-start | bytes 393220
  440.2 5.3 %copy-start.18 = (f32[32,1024]{1,0:T(8,128)S(1)}, f32[32,1024]{1,0:T(8,128)}, u32[]{:S(2)}) copy-start(f32[32,1024]{1,0:T(8,128)} %get-tuple-element.109) | copy-start | bytes 393220
  440.2 5.9 %copy-start.17 = (f32[32,1024]{1,0:T(8,128)S(1)}, f32[32,1024]{1,0:T(8,128)}, u32[]{:S(2)}) copy-start(f32[32,1024]{1,0:T(8,128)} %get-tuple-element.110) | copy-start | bytes 393220
  440.2 6.6 %copy-start.16 = (f32[32,1024]{1,0:T(8,128)S(1)}, f32[32,1024]{1,0:T(8,128)}, u32[]{:S(2)}) copy-start(f32[32,1024]{1,0:T(8,128)} %get-tuple-element.111) | copy-start | bytes 393220
  440.2 7.2 %copy-start.15 = (f32[32,1024]{1,0:T(8,128)S(1)}, f32[32,1024]{1,0:T(8,128)}, u32[]{:S(2)}) copy-start(f32[32,1024]{1,0:T(8,128)} %get-tuple-element.112) | copy-start | bytes 393220
  440.2 7.9 %copy-start.14 = (f32[32,1024]{1,0:T(8,128)S(1)}, f32[32,1024]{1,0:T(8,128)}, u32[]{:S(2)}) copy-start(f32[32,1024]{1,0:T(8,128)} %get-tuple-element.113) | copy-start | bytes 393220
  440.2 8.5 %copy-start.13 = (f32[32,1024]{1,0:T(8,128)S(1)}, f32[32,1024]{1,0:T(8,128)}, u32[]{:S(2)}) copy-start(f32[32,1024]{1,0:T(8,128)} %get-tuple-element.114) | copy-start | bytes 393220
  443.5 5.9 %copy-start.12 = (f32[32,4096]{1,0:T(8,128)S(1)}, f32[32,4096]{1,0:T(8,128)}, u32[]{:S(2)}) copy-start(f32[32,4096]{1,0:T(8,128)} %get-tuple-element.115) | copy-start | bytes 1572868
  443.5 6.7 %copy-start.11 = (f32[128,1024]{1,0:T(8,128)S(1)}, f32[128,1024]{1,0:T(8,128)}, u32[]{:S(2)}) copy-start(f32[128,1024]{1,0:T(8,128)} %get-tuple-element.116) | copy-start | bytes 1572868

commit v4 on v1

--- a/solution.py
+++ b/solution.py
@@ -1,4 +1,5 @@
 import functools
+from typing import Any, NamedTuple
 
 import jax
 import jax.numpy as jnp
@@ -61,7 +62,8 @@
             lses.append(row_max + jnp.log(summed))
         lane = lax.broadcasted_iota(jnp.int32, (TILE, LANES), 1)
         o_ref[...] = jnp.where(lane < LANES // 2, outs[0], outs[1]).astype(BF16)
-        lse_ref[0] = jnp.where(lane < LANES // 2, lses[0], lses[1])
+        for half in range(2):
+            lse_ref[0, half : half + 1, :] = jnp.transpose(jnp.broadcast_to(lses[half], (TILE, LANES)))[:1]
 
     if len(sizes) == 1:
         run(sizes[0])
@@ -92,13 +94,13 @@
             ],
             out_specs=[
                 pl.BlockSpec((TILE, LANES), lambda h, t, n: (t, h)),
-                pl.BlockSpec((1, TILE, LANES), lambda h, t, n: (h, t, 0)),
+                pl.BlockSpec((1, 2, TILE), lambda h, t, n: (h, 0, t)),
             ],
             scratch_shapes=[pltpu.VMEM((tiles, TILE, span), F32)],
         ),
         out_shape=[
             jax.ShapeDtypeStruct((rows, width), BF16),
-            jax.ShapeDtypeStruct((pairs, rows, LANES), F32),
+            jax.ShapeDtypeStruct((pairs, 2, rows), F32),
         ],
         compiler_params=pltpu.CompilerParams(vmem_limit_bytes=48 << 20),
         cost_estimate=pl.CostEstimate(flops=4 * flops, bytes_accessed=8 << 20, transcendentals=rows * span * HEADS),
@@ -137,7 +139,6 @@
         query = q_ref[...] * jnp.asarray(0.125, BF16)
         grad = g_ref[...]
         inner = grad.astype(F32) * o_ref[...].astype(F32)
-        lse_rows = jnp.transpose(lse_ref[0])
         inner_rows = jnp.transpose(inner)
         half_lanes = LANES // 2
         parts_dq = []
@@ -146,7 +147,7 @@
         for half in range(2):
             head_q = head_lanes(query, half)
             head_g = head_lanes(grad, half)
-            lse = lse_rows[half * half_lanes : half * half_lanes + 1, :]
+            lse = lse_ref[0, half : half + 1, :]
             delta = jnp.sum(inner_rows[half * half_lanes : (half + 1) * half_lanes, :], axis=0, keepdims=True)
             scores = lax.dot_general(keys, head_q, NT, preferred_element_type=F32)
             probs = jnp.exp(scores + bias_ref[tile, span - size :, :] - lse)
@@ -198,7 +199,7 @@
                 wide,
                 near,
                 near,
-                pl.BlockSpec((1, TILE, LANES), lambda h, t, n: (h, t, 0)),
+                pl.BlockSpec((1, 2, TILE), lambda h, t, n: (h, 0, t)),
             ],
             out_specs=[near, wide, wide],
             scratch_shapes=[
@@ -289,6 +290,790 @@
     return held.reshape(rows * count, width)
 
 
+MESH = pl.DeviceIdType.MESH
+BLOCK = 32
+WIDE = 1024
+
+
+def places32():
+    me = lax.axis_index(AXIS)
+    core = lax.rem(me, 2)
+    x = lax.rem(lax.div(me, 2), 2)
+    y = lax.rem(lax.div(me, 4), 2)
+    z = lax.div(me, 8)
+    return me, core, x, y, z
+
+
+GELU_A = 0.7978845608028654
+GELU_B = 0.044715
+
+
+def gelu_and_slope(value):
+    square = value * value
+    bend = jnp.tanh(GELU_A * (value + GELU_B * value * square))
+    gate = 0.5 * (1.0 + bend)
+    slope = gate + value * 0.5 * (1.0 - bend * bend) * (GELU_A * (1.0 + 3.0 * GELU_B * square))
+    return value * gate, slope
+
+
+def normalise_rows(value):
+    mean = jnp.mean(value, axis=-1, keepdims=True)
+    centred = value - mean
+    scale = lax.rsqrt(jnp.mean(centred * centred, axis=-1, keepdims=True) + EPS)
+    return centred * scale, scale
+
+
+class Far(NamedTuple):
+    low_three: Any
+    out_grad: Any
+    after_two: Any
+    up_weight: Any
+    down_weight: Any
+    cross_att: Any
+    cross_q: Any
+    text_keys: Any
+    text_values: Any
+    low_two: Any
+    after_one: Any
+    captions: Any
+    cross_output: Any
+    cross_key: Any
+    cross_value: Any
+    cross_query: Any
+    output_weight: Any
+    queries: Any
+    near_keys: Any
+    near_values: Any
+    self_att: Any
+    near_low: Any
+    near_tokens: Any
+    query_weight: Any
+    key_weight: Any
+    value_weight: Any
+
+
+class Near(NamedTuple):
+    starts: Any
+    self_lse: Any
+    query_code: Any
+    key_code: Any
+    cross_lse: Any
+    gains: Any
+
+
+class Sums(NamedTuple):
+    up: Any
+    down: Any
+    cross_output: Any
+    cross_key: Any
+    cross_value: Any
+    caption: Any
+    cross_query: Any
+    output: Any
+    query: Any
+    key: Any
+    value: Any
+
+
+class Scratch(NamedTuple):
+    arena: Any
+    sums: Any
+    accum_k: Any
+    accum_v: Any
+    back_one: Any
+    back_two: Any
+    vec: Any
+    vec_in: Any
+    tiles: Any
+    r0: Any
+    r1: Any
+    r2: Any
+    r3: Any
+    load: Any
+    s0: Any
+    d0: Any
+    s1: Any
+    d1: Any
+    s2: Any
+    d2: Any
+    s3: Any
+    d3: Any
+    vs: Any
+    vd: Any
+    bs: Any
+    bd: Any
+    credit: Any
+
+
+UP, DOWN, CROSS_OUTPUT, CROSS_KEY, CROSS_VALUE, CAPTION, CROSS_QUERY, OUTPUT, QUERY, KEY, VALUE = range(11)
+PIECES = (
+    (UP, 0), (UP, 1), (UP, 2), (UP, 3), (DOWN, 0), (DOWN, 1), (DOWN, 2), (DOWN, 3),
+    (CROSS_OUTPUT, 0), (CROSS_KEY, 0), (CROSS_VALUE, 0), (CAPTION, 0), (CROSS_QUERY, 0), (OUTPUT, 0),
+    (QUERY, 0), (KEY, 0), (VALUE, 0),
+)
+PLAN = (
+    (), (), (), (), ((2, 0),), (), ((2, 1),), ((2, 2),), (), ((2, 3),), (), (), (), ((3, 0), (2, 4)), (), (), (),
+    (), ((3, 1),), (), (), (), ((2, 5),), (), (), (), (), ((3, 2), (2, 6)), (), (), (), ((3, 3),), (), ((2, 7),),
+    (), (), ((3, 4), (2, 8)), ((3, 6), (3, 5)), ((1, 13),), ((3, 7),), (), ((2, 9),), (), (), ((2, 10),), (), (),
+    ((2, 11),), (), ((3, 8), (2, 12)), (), (), ((3, 9),), (), ((2, 13), (3, 11)), ((3, 10),), ((3, 12),), (),
+    ((2, 14),), ((3, 13),),
+)
+LANDINGS = 9
+SLOTS = 2
+HALF = LANES // 2
+STEP = 64
+LOADS = 48
+
+
+def layer_kernel(rows, *refs):
+    total = len(PIECES)
+    n_far, n_near, n_sums = len(Far._fields), len(Near._fields), len(Sums._fields)
+    far = Far(*refs[:n_far])
+    near = Near(*refs[n_far : n_far + n_near])
+    refs = refs[n_far + n_near :]
+    outs = Sums(*refs[:n_sums])
+    vec_out, block_output, input_grad = refs[n_sums : n_sums + 3]
+    held = Scratch(*refs[n_sums + 3 :])
+    (arena, sums, accum_k, accum_v, back_one, back_two, vec, vec_in, tiles, r0, r1, r2, r3,
+     load, s0, d0, s1, d1, s2, d2, s3, d3, vs, vd, bs, bd, credit) = held
+
+    me, core, x, y, z = places32()
+    sibling = me + 1 - 2 * core
+    x_peer = me + 2 - 4 * x
+    y_peer = me + 4 - 8 * y
+    z_other = [lax.rem(z + m, 4) for m in range(1, 4)]
+    z_peers = [me + 8 * (o - z) for o in z_other]
+    has_before = me >= 2
+    has_after = me < 30
+
+    barrier = pltpu.get_barrier_semaphore()
+    for peer in (sibling, x_peer, y_peer, *z_peers):
+        pl.semaphore_signal(barrier, inc=1, device_id=(peer,), device_id_type=MESH)
+
+    @pl.when(has_before)
+    def _():
+        pl.semaphore_signal(barrier, inc=1, device_id=(me - 2,), device_id_type=MESH)
+
+    @pl.when(has_after)
+    def _():
+        pl.semaphore_signal(barrier, inc=1, device_id=(me + 2,), device_id_type=MESH)
+
+    numbers = iter(range(LOADS))
+
+    def fetch(source, slot):
+        return start_copy(source, arena.at[pl.ds(slot * rows, source.shape[0])])
+
+    def start_copy(source, target):
+        copy = pltpu.make_async_copy(source, target, load.at[next(numbers)])
+        copy.start()
+        return copy
+
+    def at(slot, count=1):
+        return pl.ds(slot * rows, count * rows)
+
+    def up_part(part):
+        return far.up_weight.at[:, pl.ds(part * WIDE, WIDE)]
+
+    def down_part(part):
+        return far.down_weight.at[pl.ds(part * WIDE, WIDE)]
+
+    ONE, TWO, THREE = 12, 14, 10
+    low_three_load = fetch(far.low_three, 8)
+    up_loads = [fetch(up_part(0), THREE)]
+    out_grad_load = fetch(far.out_grad, 9)
+    down_loads = [fetch(down_part(0), ONE)]
+    up_loads.append(fetch(up_part(1), TWO))
+    after_load = start_copy(far.after_two, sums.at[2])
+
+    pl.semaphore_wait(barrier, 6 + jnp.where(has_before, 1, 0) + jnp.where(has_after, 1, 0))
+
+    def remote(src, dst, send, recv, peer):
+        return pltpu.make_async_remote_copy(
+            src_ref=src, dst_ref=dst, send_sem=send, recv_sem=recv, device_id=(peer,), device_id_type=MESH
+        )
+
+    def along(c):
+        even = lax.rem(c, 2) == 0
+        return (
+            jnp.where(even, x, y),
+            jnp.where(even, x_peer, y_peer),
+            jnp.where(even, y, x),
+            jnp.where(even, y_peer, x_peer),
+        )
+
+    def add_blocks(count, dst, src):
+        @pl.loop(0, count, unroll=4)
+        def _(i):
+            dst(i)[...] = dst(i)[...] + src(i)[...]
+
+    def take_credit(c):
+        if c >= LANDINGS:
+            pl.semaphore_wait(credit, 1)
+
+    def give(c):
+        take_credit(c)
+        remote(tiles.at[c % SLOTS, 1 - core], r0.at[c % LANDINGS], s0.at[c], d0.at[c], sibling).start()
+
+    def make(c, left_at, right_at, depth):
+        @pl.loop(0, 4)
+        def _(zz):
+            left = arena[pl.ds(left_at * rows, depth), pl.ds(pl.multiple_of(zz * TILE, TILE), TILE)]
+            for part in range(2):
+                cols = slice(part * (WIDE // 2), (part + 1) * (WIDE // 2))
+                result = lax.dot_general(
+                    left, arena[pl.ds(right_at * rows, depth), cols], TN, preferred_element_type=F32
+                ).astype(BF16)
+                for block in range(8):
+                    yy, xx, cc = block // 4, (block // 2) % 2, block % 2
+                    f, s = (xx, yy) if c % 2 == 0 else (yy, xx)
+                    tiles[c % SLOTS, cc, f, s, zz, :, cols] = result[block * BLOCK : (block + 1) * BLOCK]
+
+        give(c)
+
+    def make_down(c, part):
+        @pl.loop(0, 4)
+        def _(zz):
+            for quarter in range(4):
+                yy, xx = quarter // 2, quarter % 2
+                f, s = (xx, yy) if c % 2 == 0 else (yy, xx)
+                left = arena[
+                    pl.ds(pl.multiple_of(zz * rows, rows), rows), quarter * TILE : (quarter + 1) * TILE
+                ]
+                result = lax.dot_general(
+                    left, arena[at(9), part * TILE : (part + 1) * TILE], TN, preferred_element_type=F32
+                ).astype(BF16)
+                for cc in range(2):
+                    for group in range(4):
+                        top = cc * 128 + group * BLOCK
+                        tiles[c % SLOTS, cc, f, s, zz, :, group * TILE : (group + 1) * TILE] = result[top : top + BLOCK]
+
+        give(c)
+
+    def first(c):
+        f, fp, _, _ = along(c)
+        slot, place = c % SLOTS, c % LANDINGS
+        copy = remote(tiles.at[slot, 1 - core], r0.at[place], s0.at[c], d0.at[c], sibling)
+        copy.wait_recv()
+        add_blocks(
+            16,
+            lambda i: r0.at[place, i // 8, (i // 4) % 2, i % 4],
+            lambda i: tiles.at[slot, core, i // 8, (i // 4) % 2, i % 4],
+        )
+        remote(r0.at[place, 1 - f], r1.at[c], s1.at[c], d1.at[c], fp).start()
+        copy.wait_send()
+
+    def second(c):
+        f, fp, s, sp = along(c)
+        place = c % LANDINGS
+        copy = remote(r0.at[place, 1 - f], r1.at[c], s1.at[c], d1.at[c], fp)
+        copy.wait_recv()
+        add_blocks(8, lambda i: r1.at[c, i // 4, i % 4], lambda i: r0.at[place, f, i // 4, i % 4])
+        remote(r1.at[c, 1 - s], r2.at[c], s2.at[c], d2.at[c], sp).start()
+        copy.wait_send()
+        if c < total - LANDINGS:
+            pl.semaphore_signal(credit, inc=1, device_id=(sibling,), device_id_type=MESH)
+
+    def third(c):
+        _, _, s, sp = along(c)
+        copy = remote(r1.at[c, 1 - s], r2.at[c], s2.at[c], d2.at[c], sp)
+        copy.wait_recv()
+        add_blocks(4, lambda i: r2.at[c, i], lambda i: r1.at[c, s, i])
+        for m in range(3):
+            remote(r2.at[c, z_other[m]], r3.at[c, m], s3.at[c, m], d3.at[c, m], z_peers[m]).start()
+        copy.wait_send()
+
+    def last(c):
+        number, part = PIECES[c]
+        for m in range(3):
+            remote(r2.at[c, z_other[m]], r3.at[c, m], s3.at[c, m], d3.at[c, m], z_peers[m]).wait()
+        summed = r2[c, z].astype(F32) + r3[c, 0].astype(F32) + r3[c, 1].astype(F32) + r3[c, 2].astype(F32)
+        out = outs[number]
+        if number == DOWN:
+            for group in range(4):
+                out[group * BLOCK : (group + 1) * BLOCK, part * TILE : (part + 1) * TILE] = summed[
+                    :, group * TILE : (group + 1) * TILE
+                ]
+        else:
+            out[:, part * WIDE : (part + 1) * WIDE] = summed[: out.shape[0]]
+
+    def each_tile(run):
+        @pl.loop(0, WIDE // TILE, unroll=2)
+        def _(n):
+            run(pl.multiple_of(n * TILE, TILE))
+
+    def product(pairs, add=False):
+        def run(n):
+            result = None
+            for slot, weight in pairs:
+                term = lax.dot_general(
+                    arena[at(slot), :], arena[pl.ds(weight * rows + n, TILE), :], NT, preferred_element_type=F32
+                )
+                result = term if result is None else result + term
+            if add:
+                result += sums[0, :, pl.ds(n, TILE)]
+            sums[0, :, pl.ds(n, TILE)] = result
+
+        each_tile(run)
+
+    def plain_product(slot, weight, add):
+        def run(n):
+            result = jnp.dot(arena[at(slot), :], arena[at(weight, 2), pl.ds(n, TILE)], preferred_element_type=F32)
+            if add:
+                result += sums[0, :, pl.ds(n, TILE)]
+            sums[0, :, pl.ds(n, TILE)] = result
+
+        each_tile(run)
+
+    def low_product(slot, weight, target):
+        def run(n):
+            result = lax.dot_general(
+                arena[at(slot), :], arena[pl.ds(weight * rows + n, TILE), :], NT, preferred_element_type=F32
+            )
+            arena[at(target), pl.ds(n, TILE)] = result.astype(BF16)
+
+        each_tile(run)
+
+    def each_step(run):
+        @pl.loop(0, rows // STEP)
+        def _(i):
+            run(pl.multiple_of(i * STEP, STEP))
+
+    vec[...] = jnp.zeros_like(vec)
+
+    def add_gains(row, grad, unit):
+        vec[row : row + 1] += jnp.sum(grad * unit, axis=0, keepdims=True)
+        vec[row + 1 : row + 2] += jnp.sum(grad, axis=0, keepdims=True)
+
+    def norm_back_rows(grad, unit, scale, gain):
+        scaled = grad * gain
+        return scale * (
+            scaled - jnp.mean(scaled, axis=-1, keepdims=True) - unit * jnp.mean(scaled * unit, axis=-1, keepdims=True)
+        )
+
+    def attend_step(keys, values, query, grad, out, lse, allowed):
+        query = query * jnp.asarray(0.125, BF16)
+        inner = jnp.transpose(grad.astype(F32) * out.astype(F32))
+        turned_keys = jnp.transpose(keys)
+        parts = []
+        dk = None
+        dv = None
+        for half in range(2):
+            head_q = head_lanes(query, half)
+            head_g = head_lanes(grad, half)
+            delta = jnp.sum(inner[half * HALF : (half + 1) * HALF], axis=0, keepdims=True)
+            scores = lax.dot_general(keys, head_q, NT, preferred_element_type=F32)
+            probs = jnp.exp(jnp.where(allowed, scores - lse[half], NEG))
+            grad_probs = lax.dot_general(values, head_g, NT, preferred_element_type=F32)
+            grad_scores = (probs * (grad_probs - delta)).astype(BF16)
+            part_k = jnp.dot(grad_scores, head_q, preferred_element_type=F32)
+            part_v = jnp.dot(probs.astype(BF16), head_g, preferred_element_type=F32)
+            dk = part_k if dk is None else dk + part_k
+            dv = part_v if dv is None else dv + part_v
+            parts.append(jnp.dot(turned_keys, grad_scores, preferred_element_type=F32))
+        dq = jnp.concatenate([parts[0][:HALF], parts[1][HALF:]], 0)
+        return (jnp.transpose(dq) * 0.125).astype(BF16), dk, dv
+
+    position = [0]
+
+    def take_steps(steps):
+        for kind, c in steps:
+            (first, second, third)[kind - 1](c)
+
+    def tick():
+        take_steps(PLAN[position[0]])
+        position[0] += 1
+
+    def loop_tick(base, i):
+        for number, steps in enumerate(PLAN[base : base + 16]):
+            if steps:
+                pl.when(i == number)(functools.partial(take_steps, steps))
+
+    def activate(part, up_at, down_at):
+        def run(n):
+            cols = pl.ds(n, TILE)
+            pre = jnp.dot(arena[at(8), :], arena[at(up_at, 2), cols], preferred_element_type=F32)
+            grad = lax.dot_general(
+                arena[at(9), :], arena[pl.ds(down_at * rows + n, TILE), :], NT, preferred_element_type=F32
+            )
+            hidden, slope = gelu_and_slope(pre)
+            arena[at(part), cols] = hidden.astype(BF16)
+            arena[at(4 + part), cols] = (slope * grad).astype(BF16)
+
+        each_tile(run)
+
+    low_three_load.wait()
+    out_grad_load.wait()
+    places = ((THREE, ONE), (TWO, THREE), (ONE, TWO), (THREE, ONE))
+    for part in range(4):
+        up_loads[part].wait()
+        down_loads[part].wait()
+        activate(part, *places[part])
+        if part == 0:
+            down_loads.append(fetch(down_part(1), THREE))
+            up_loads.append(fetch(up_part(2), ONE))
+        if part == 1:
+            down_loads.append(fetch(down_part(2), TWO))
+            up_loads.append(fetch(up_part(3), THREE))
+        if part == 2:
+            down_loads.append(fetch(down_part(3), ONE))
+            weight_two = fetch(up_part(1), TWO)
+        if part == 3:
+            weight_one = fetch(up_part(0), ONE)
+        make(part, 8, 4 + part, rows)
+        if part > 0:
+            first(part - 1)
+        tick()
+    places = (ONE, TWO, THREE, ONE)
+    loads = [weight_one, weight_two, fetch(up_part(2), THREE)]
+    for part in range(4):
+        make_down(4 + part, part)
+        loads[part].wait()
+        product([(4 + part, places[part])], add=part > 0)
+        if part == 0:
+            loads.append(fetch(up_part(3), ONE))
+        first(3 + part)
+        tick()
+    weight_two = fetch(far.cross_output, TWO)
+    weight_three = fetch(down_part(0), THREE)
+    weight_one = fetch(down_part(1), ONE)
+    low_two_load = fetch(far.low_two, 4)
+    captions_load = fetch(far.captions, 5)
+    cross_att_load = fetch(far.cross_att, 6)
+    cross_q_load = fetch(far.cross_q, 7)
+    after_load.wait()
+    gains = near.gains
+
+    def norm_three(n):
+        here = pl.ds(n, STEP)
+        unit, scale = normalise_rows(sums[2, here, :])
+        grad = sums[0, here, :]
+        add_gains(4, grad, unit)
+        value = arena[pl.ds(9 * rows + n, STEP), :].astype(F32) + norm_back_rows(grad, unit, scale, gains[2:3])
+        sums[1, here, :] = value
+        arena[pl.ds(9 * rows + n, STEP), :] = value.astype(BF16)
+
+    each_step(norm_three)
+    first(7)
+    tick()
+
+    weight_two.wait()
+    low_product(9, TWO, 8)
+    weight_two = fetch(down_part(2), TWO)
+    cross_att_load.wait()
+    make(8, 6, 9, rows)
+    tick()
+    weight_three.wait()
+    plain_product(0, THREE, False)
+    weight_three = fetch(down_part(3), THREE)
+    tick()
+    weight_one.wait()
+    plain_product(1, ONE, True)
+    weight_one = fetch(far.cross_key, ONE)
+    first(8)
+    tick()
+    weight_two.wait()
+    plain_product(2, TWO, True)
+    weight_two = fetch(far.cross_value, TWO)
+    keys_load = fetch(far.text_keys, 2)
+    tick()
+    weight_three.wait()
+    plain_product(3, THREE, True)
+    weight_three = fetch(far.cross_query, THREE)
+    values_load = fetch(far.text_values, 3)
+    tick()
+
+    def finish_block(n):
+        here = pl.ds(n, STEP)
+        arena[pl.ds(n, STEP), :] = (sums[2, here, :] + sums[0, here, :]).astype(BF16)
+
+    each_step(finish_block)
+    tick()
+    loop_base = position[0]
+    position[0] += 16
+    block_copy = start_copy(arena.at[at(0)], block_output)
+    after_load = start_copy(far.after_one, sums.at[2])
+
+    text = far.text_keys.shape[0]
+    cross_q_load.wait()
+    keys_load.wait()
+    values_load.wait()
+
+    @pl.loop(0, 16)
+    def _(i):
+        h, t = lax.div(i, 2), lax.rem(i, 2)
+        lanes = pl.ds(pl.multiple_of(h * LANES, LANES), LANES)
+        own = pl.multiple_of(t * TILE, TILE)
+        mine = pl.ds(7 * rows + own, TILE)
+        allowed = near.key_code[...] == near.query_code[:, pl.ds(own, TILE)]
+        lse = [near.cross_lse[h, half : half + 1, pl.ds(own, TILE)] for half in range(2)]
+        dq, dk, dv = attend_step(
+            arena[at(2), lanes], arena[at(3), lanes], arena[mine, lanes],
+            arena[pl.ds(8 * rows + own, TILE), lanes], arena[pl.ds(6 * rows + own, TILE), lanes], lse, allowed,
+        )
+        arena[mine, lanes] = dq
+
+        @pl.when(t == 0)
+        def _():
+            accum_k[:text] = dk
+            accum_v[:text] = dv
+
+        @pl.when(t == 1)
+        def _():
+            arena[at(2), lanes] = (accum_k[:text] + dk).astype(BF16)
+            arena[at(3), lanes] = (accum_v[:text] + dv).astype(BF16)
+
+        loop_tick(loop_base, i)
+
+    block_copy.wait()
+    self_att_load = fetch(far.self_att, 8)
+    captions_load.wait()
+    make(9, 5, 2, rows)
+    tick()
+    weight_one.wait()
+    weight_two.wait()
+    product([(2, ONE), (3, TWO)])
+    weight_one = fetch(far.output_weight, ONE)
+    make(10, 5, 3, rows)
+    first(9)
+    tick()
+
+    c = 11
+    for zz in range(4):
+        for block in range(8):
+            yy, xx, cc = block // 4, (block // 2) % 2, block % 2
+            f, s = (xx, yy) if c % 2 == 0 else (yy, xx)
+            top = (zz * 8 + block) * 16
+            tiles[c % SLOTS, cc, f, s, zz, :16, :] = sums[0, top : top + 16, :].astype(BF16)
+            tiles[c % SLOTS, cc, f, s, zz, 16:, :] = jnp.zeros((16, WIDE), BF16)
+    give(c)
+    tick()
+    keys_load = fetch(far.near_keys, 1)
+    weight_three.wait()
+    product([(7, THREE)])
+    near_low_load = fetch(far.near_low, 9)
+    first(10)
+    tick()
+    low_two_load.wait()
+    make(12, 4, 7, rows)
+    values_load = fetch(far.near_values, 4)
+    queries_load = fetch(far.queries, 0)
+    first(11)
+    tick()
+    after_load.wait()
+
+    def norm_two(n):
+        here = pl.ds(n, STEP)
+        unit, scale = normalise_rows(sums[2, here, :])
+        grad = sums[0, here, :]
+        add_gains(2, grad, unit)
+        value = sums[1, here, :] + norm_back_rows(grad, unit, scale, gains[1:2])
+        sums[1, here, :] = value
+        arena[pl.ds(14 * rows + n, STEP), :] = value.astype(BF16)
+
+    each_step(norm_two)
+    first(12)
+    tick()
+
+    weight_one.wait()
+    low_product(14, ONE, 7)
+    weight_one = fetch(far.value_weight, ONE)
+    self_att_load.wait()
+    make(13, 8, 14, rows)
+    tick()
+    loop_base = position[0]
+    position[0] += 16
+    weight_two = fetch(far.key_weight, TWO)
+    queries_load.wait()
+    keys_load.wait()
+    values_load.wait()
+
+    span = 2 * rows + TILE
+
+    @pl.loop(0, 16)
+    def _(i):
+        h, t = lax.div(i, 2), lax.rem(i, 2)
+        lanes = pl.ds(pl.multiple_of(h * LANES, LANES), LANES)
+        own = pl.multiple_of(t * TILE, TILE)
+        mine = pl.ds(own, TILE)
+        kpos = lax.broadcasted_iota(jnp.int32, (span, TILE), 0)
+        qpos = lax.broadcasted_iota(jnp.int32, (TILE, TILE), 1)
+        dpos = lax.broadcasted_iota(jnp.int32, (TILE, TILE), 0)
+        allowed = kpos >= near.starts[:, mine] - own
+        allowed = jnp.concatenate([allowed[: span - TILE], allowed[span - TILE :] & (dpos <= qpos)], 0)
+        lse = [near.self_lse[h, half : half + 1, mine] for half in range(2)]
+        dq, dk, dv = attend_step(
+            arena[pl.ds(rows + own, span), lanes], arena[pl.ds(4 * rows + own, span), lanes], arena[mine, lanes],
+            arena[pl.ds(7 * rows + own, TILE), lanes], arena[pl.ds(8 * rows + own, TILE), lanes], lse, allowed,
+        )
+        arena[mine, lanes] = dq
+
+        @pl.when(t == 0)
+        def _():
+            accum_k[:span] = dk
+            accum_v[:span] = dv
+
+        @pl.when(t == 1)
+        def _():
+            for target, accum, part in ((1, accum_k, dk), (4, accum_v, dv)):
+                arena[pl.ds(target * rows, TILE), lanes] = accum[:TILE].astype(BF16)
+                arena[pl.ds(target * rows + TILE, span - TILE), lanes] = (accum[TILE:span] + part[: span - TILE]).astype(BF16)
+                arena[pl.ds(target * rows + span, TILE), lanes] = part[span - TILE :].astype(BF16)
+
+        loop_tick(loop_base, i)
+
+    near_low_load.wait()
+    make(14, 11, 0, rows)
+    weight_two.wait()
+    weight_one.wait()
+    product([(2, TWO), (5, ONE)])
+
+    def as_low(slot, extra):
+        def run(n):
+            value = sums[0, pl.ds(n, STEP), :]
+            if extra is not None:
+                value = value + jnp.where(core == 1, extra[pl.ds(n, STEP), :].astype(F32), 0.0)
+            arena[pl.ds(slot * rows + n, STEP), :] = value.astype(BF16)
+
+        each_step(run)
+
+    as_low(7, None)
+    swap = remote(arena.at[at(7)], back_one, bs.at[0], bd.at[0], sibling)
+    swap.start()
+    first(14)
+    tick()
+    product([(1, TWO), (4, ONE)])
+    swap.wait()
+    as_low(8, back_one)
+    send_back = remote(arena.at[at(8)], back_two, bs.at[1], bd.at[1], me - 2)
+
+    @pl.when(has_before)
+    def _():
+        send_back.start()
+
+    tick()
+    make(15, 9, 1, 3 * rows)
+    tick()
+    query_weight_load = fetch(far.query_weight, 1)
+    make(16, 9, 4, 3 * rows)
+    token_load = fetch(far.near_tokens, 9)
+    first(15)
+    tick()
+
+    def block_gains(slot, grad_slot, factor):
+        def run(n):
+            unit, _ = normalise_rows(arena[pl.ds(slot * rows + n, STEP), :].astype(F32))
+            if grad_slot is None:
+                grad = sums[0, pl.ds(n, STEP), :]
+            else:
+                grad = arena[pl.ds(grad_slot * rows + n, STEP), :].astype(F32)
+            if factor is not None:
+                grad = grad * factor
+            add_gains(0, grad, unit)
+
+        each_step(run)
+
+    token_load.wait()
+    block_gains(9, 8, None)
+    block_gains(10, 7, jnp.where(core == 1, 1.0, 0.0))
+    first(16)
+    tick()
+    query_weight_load.wait()
+    product([(0, 1), (3, TWO), (6, ONE)])
+    tick()
+    block_gains(11, None, None)
+
+    def vec_step(number, peer):
+        step = remote(vec, vec_in.at[number], vs.at[number], vd.at[number], peer)
+        step.start()
+        return step
+
+    def norm_one(n):
+        here = pl.ds(n, STEP)
+        unit, scale = normalise_rows(arena[pl.ds(11 * rows + n, STEP), :].astype(F32))
+        grad = sums[0, here, :]
+        grad = grad + jnp.where(core == 0, back_one[here, :].astype(F32), 0.0)
+        grad = grad + jnp.where(has_after, back_two[here, :].astype(F32), 0.0)
+        sums[1, here, :] += norm_back_rows(grad, unit, scale, gains[0:1])
+
+    step = vec_step(0, sibling)
+    step.wait()
+    vec[...] += vec_in[0]
+    step = vec_step(1, x_peer)
+    second(15)
+
+    @pl.when(has_before)
+    def _():
+        send_back.wait_send()
+
+    @pl.when(has_after)
+    def _():
+        send_back.wait_recv()
+
+    each_step(norm_one)
+    out_copy = start_copy(sums.at[1], input_grad)
+    step.wait()
+    vec[...] += vec_in[1]
+    step = vec_step(2, y_peer)
+    third(14)
+    second(16)
+    step.wait()
+    vec[...] += vec_in[2]
+    steps = [vec_step(3 + m, z_peers[m]) for m in range(3)]
+    for c in range(total - 3):
+        last(c)
+    third(15)
+    third(16)
+    for step in steps:
+        step.wait()
+    vec_out[...] = vec[...] + vec_in[3] + vec_in[4] + vec_in[5]
+    for c in range(total - 3, total):
+        last(c)
+    out_copy.wait()
+
+
+def layer_tail(far, near):
+    rows, width = far.queries.shape
+    count = 32
+    sizes = {UP: (BLOCK, 4 * WIDE), DOWN: (4 * BLOCK, WIDE), CAPTION: (far.captions.shape[0] // count, WIDE)}
+    total = len(PIECES)
+    local = pl.BlockSpec(memory_space=pltpu.VMEM)
+    anywhere = pl.BlockSpec(memory_space=pl.ANY)
+    dma = pltpu.SemaphoreType.DMA
+    scratch = Scratch(
+        arena=pltpu.VMEM((16 * rows, width), BF16),
+        sums=pltpu.VMEM((3, rows, width), F32),
+        accum_k=pltpu.VMEM((3 * rows, LANES), F32),
+        accum_v=pltpu.VMEM((3 * rows, LANES), F32),
+        back_one=pltpu.VMEM((rows, width), BF16),
+        back_two=pltpu.VMEM((rows, width), BF16),
+        vec=pltpu.VMEM((8, width), F32),
+        vec_in=pltpu.VMEM((6, 8, width), F32),
+        tiles=pltpu.VMEM((SLOTS, 2, 2, 2, 4, BLOCK, WIDE), BF16),
+        r0=pltpu.VMEM((LANDINGS, 2, 2, 4, BLOCK, WIDE), BF16),
+        r1=pltpu.VMEM((total, 2, 4, BLOCK, WIDE), BF16),
+        r2=pltpu.VMEM((total, 4, BLOCK, WIDE), BF16),
+        r3=pltpu.VMEM((total, 3, BLOCK, WIDE), BF16),
+        load=dma((LOADS,)), s0=dma((total,)), d0=dma((total,)), s1=dma((total,)), d1=dma((total,)),
+        s2=dma((total,)), d2=dma((total,)), s3=dma((total, 3)), d3=dma((total, 3)), vs=dma((6,)), vd=dma((6,)),
+        bs=dma((2,)), bd=dma((2,)), credit=pltpu.SemaphoreType.REGULAR,
+    )
+    results = pl.pallas_call(
+        functools.partial(layer_kernel, rows),
+        in_specs=[anywhere] * len(far) + [local] * len(near),
+        out_specs=[local] * (len(Sums._fields) + 1) + [anywhere] * 2,
+        out_shape=[jax.ShapeDtypeStruct(sizes.get(number, (BLOCK, WIDE)), F32) for number in range(len(Sums._fields))]
+        + [
+            jax.ShapeDtypeStruct((8, width), F32),
+            jax.ShapeDtypeStruct((rows, width), BF16),
+            jax.ShapeDtypeStruct((rows, width), F32),
+        ],
+        scratch_shapes=list(scratch),
+        compiler_params=pltpu.CompilerParams(collective_id=0, has_side_effects=True, vmem_limit_bytes=63 << 20),
+        cost_estimate=pl.CostEstimate(flops=1 << 34, bytes_accessed=64 << 20, transcendentals=0),
+    )(*far, *near)
+    return Sums(*results[: len(Sums._fields)]), *results[len(Sums._fields) :]
+
+
 def matmul(left, right):
     return jnp.dot(left, right, preferred_element_type=F32)
 
@@ -315,18 +1100,6 @@
         - jnp.mean(scaled, axis=-1, keepdims=True)
         - unit * jnp.mean(scaled * unit, axis=-1, keepdims=True)
     )
-
-
-GELU_A = 0.7978845608028654
-GELU_B = 0.044715
-
-
-def gelu_and_slope(value):
-    square = value * value
-    bend = jnp.tanh(GELU_A * (value + GELU_B * value * square))
-    gate = 0.5 * (1.0 + bend)
-    slope = gate + value * 0.5 * (1.0 - bend * bend) * (GELU_A * (1.0 + 3.0 * GELU_B * square))
-    return value * gate, slope
 
 
 def body(
@@ -396,97 +1169,108 @@
     after_two = after_one + matmul(cross_att, cross_output)
     unit_three, scale_three = normalise(after_two)
     low_three = (unit_three * mlp_gain + mlp_bias).astype(BF16)
-    hidden_pre = matmul(low_three, up_weight)
-    hidden, slope = gelu_and_slope(hidden_pre)
-    hidden_low = hidden.astype(BF16)
-    block_output = (after_two + matmul(hidden_low, down_weight)).astype(BF16)
-
-    grad_pre = (slope * right_product(out_grad, down_weight)).astype(BF16)
-    down_grad = left_product(hidden_low, out_grad).astype(BF16)
-    up_grad = left_product(low_three, grad_pre).astype(BF16)
-    z_, y_, x_, c_ = 0, 1, 2, 3
-    one_way = (c_, x_, y_, z_) if len(factors(count)) == 4 else (0,)
-    other_way = (c_, y_, x_, z_) if len(factors(count)) == 4 else (0,)
-    down_out = reduce_scatter(down_grad, one_way, BF16, count)
-    up_out = reduce_scatter(up_grad, other_way, BF16, count)
-    grad_three = right_product(grad_pre, up_weight)
-    mlp_gain_grad = jnp.sum(grad_three * unit_three, axis=0)
-    mlp_bias_grad = jnp.sum(grad_three, axis=0)
-    grad_two = out_grad.astype(F32) + norm_back(grad_three, unit_three, scale_three, mlp_gain)
-    grad_two_low = grad_two.astype(BF16)
-
-    cross_output_grad = left_product(cross_att, grad_two_low).astype(BF16)
-    grad_cross = right_product(grad_two_low, cross_output).astype(BF16)
-    grad_cq, grad_tk, grad_tv = attend_backward(
-        cross_q, text_keys, text_values, grad_cross, cross_att, cross_lse,
-        query_code[None, :], text_code[:, :, None], no_numbers, False, (text,), text_ends,
-    )
-    own_text = reduce_scatter(jnp.concatenate([grad_tk, grad_tv], 1), one_way, BF16, count).astype(BF16)
-    width = grad_tk.shape[1]
-    caption_grad = right_product(own_text[:, :width], cross_key) + right_product(own_text[:, width:], cross_value)
-    all_text = all_gather(own_text, one_way[::-1], count)
-    share = width // count
-    caption_part = lax.dynamic_slice_in_dim(caption_states, device * share, share, 1)
-    text_weight_grads = left_product(caption_part, all_text)
-    cross_key_grad = text_weight_grads[:, :width]
-    cross_value_grad = text_weight_grads[:, width:]
-    cross_query_grad = left_product(low_two, grad_cq).astype(BF16)
-    grad_norm_two = right_product(grad_cq, cross_query)
-    cross_gain_grad = jnp.sum(grad_norm_two * unit_two, axis=0)
-    cross_bias_grad = jnp.sum(grad_norm_two, axis=0)
-    grad_one = grad_two + norm_back(grad_norm_two, unit_two, scale_two, cross_gain)
-    grad_one_low = grad_one.astype(BF16)
-
-    output_weight_grad = left_product(self_att, grad_one_low).astype(BF16)
-    middle = reduce_scatter(
-        jnp.concatenate([cross_output_grad, cross_query_grad, output_weight_grad], 1), other_way, BF16, count
-    )
-    grad_self = right_product(grad_one_low, output_weight).astype(BF16)
-    grad_q, grad_k, grad_v = attend_backward(
-        queries, near_keys, near_values, grad_self, self_att, self_lse,
-        own_ids[None, :], windows[:, :, None], numbers, True, self_sizes, self_ends,
-    )
-    grad_near = right_product(grad_k, key_weight) + right_product(grad_v, value_weight)
-    grad_own = grad_near[REACH * rows :] + right_product(grad_q, query_weight)
-    to_two = grad_near[:rows]
-    to_one = grad_near[rows : REACH * rows].astype(BF16)
-    from_swap = lax.ppermute(to_one, AXIS, swap).astype(F32)
-    to_two = (to_two + jnp.where(odd, from_swap, 0.0)).astype(BF16)
-    from_two = lax.ppermute(to_two, AXIS, behind).astype(F32)
-    near_sum = jnp.concatenate([grad_near[: REACH * rows], grad_own], 0)
-    attn_gain_grad = jnp.sum(near_sum * near_unit, axis=0)
-    attn_bias_grad = jnp.sum(near_sum, axis=0)
-    grad_norm_one = grad_own + from_two + jnp.where(odd, 0.0, from_swap)
-    unit_one = near_unit[REACH * rows :]
-    input_grad = grad_one + norm_back(grad_norm_one, unit_one, near_scale[REACH * rows :], attn_gain)
-    query_grad = left_product(low_one, grad_q).astype(BF16)
-    key_grad = left_product(near_low, grad_k).astype(BF16)
-    value_grad = left_product(near_low, grad_v).astype(BF16)
-    late = reduce_scatter(jnp.concatenate([query_grad, key_grad, value_grad], 1), one_way, BF16, count)
-    vectors = jnp.stack(
-        [attn_gain_grad, attn_bias_grad, cross_gain_grad, cross_bias_grad, mlp_gain_grad, mlp_bias_grad], 1
-    )
-    small = reduce_scatter(vectors, one_way, F32, count)
+    width = tokens.shape[1]
+    if count == 32:
+        starts = jnp.sum((near_ids[None, :] < own_ids[:, None]).astype(jnp.int32), axis=1)
+        sums, small, block_output, input_grad = layer_tail(
+            Far(
+                low_three=low_three, out_grad=out_grad, after_two=after_two,
+                up_weight=up_weight, down_weight=down_weight,
+                cross_att=cross_att, cross_q=cross_q, text_keys=text_keys, text_values=text_values,
+                low_two=low_two, after_one=after_one, captions=caption_states,
+                cross_output=cross_output, cross_key=cross_key, cross_value=cross_value, cross_query=cross_query,
+                output_weight=output_weight,
+                queries=queries, near_keys=near_keys, near_values=near_values, self_att=self_att,
+                near_low=near_low, near_tokens=near_tokens,
+                query_weight=query_weight, key_weight=key_weight, value_weight=value_weight,
+            ),
+            Near(
+                starts=starts[None, :], self_lse=self_lse, query_code=query_code[None, :], key_code=key_code[:, None],
+                cross_lse=cross_lse, gains=jnp.stack([attn_gain, cross_gain, mlp_gain]),
+            ),
+        )
+        small = lax.dynamic_slice_in_dim(small, device * (width // count), width // count, 1)
+    else:
+        hidden_pre = matmul(low_three, up_weight)
+        hidden, slope = gelu_and_slope(hidden_pre)
+        hidden_low = hidden.astype(BF16)
+        grad_pre = (slope * right_product(out_grad, down_weight)).astype(BF16)
+        block_output = (after_two + matmul(hidden_low, down_weight)).astype(BF16)
+
+        down_grad = left_product(hidden_low, out_grad).astype(BF16)
+        up_grad = left_product(low_three, grad_pre).astype(BF16)
+        z_, y_, x_, c_ = 0, 1, 2, 3
+        one_way = (c_, x_, y_, z_) if len(factors(count)) == 4 else (0,)
+        other_way = (c_, y_, x_, z_) if len(factors(count)) == 4 else (0,)
+        grad_three = right_product(grad_pre, up_weight)
+        mlp_gain_grad = jnp.sum(grad_three * unit_three, axis=0)
+        mlp_bias_grad = jnp.sum(grad_three, axis=0)
+        grad_two = out_grad.astype(F32) + norm_back(grad_three, unit_three, scale_three, mlp_gain)
+        grad_two_low = grad_two.astype(BF16)
+
+        cross_output_grad = left_product(cross_att, grad_two_low).astype(BF16)
+        grad_cross = right_product(grad_two_low, cross_output).astype(BF16)
+        grad_cq, grad_tk, grad_tv = attend_backward(
+            cross_q, text_keys, text_values, grad_cross, cross_att, cross_lse,
+            query_code[None, :], text_code[:, :, None], no_numbers, False, (text,), text_ends,
+        )
+        width = grad_tk.shape[1]
+        cross_key_grad = left_product(caption_states, grad_tk).astype(BF16)
+        cross_value_grad = left_product(caption_states, grad_tv).astype(BF16)
+        caption_grad = (right_product(grad_tk, cross_key) + right_product(grad_tv, cross_value)).astype(BF16)
+        cross_query_grad = left_product(low_two, grad_cq).astype(BF16)
+        grad_norm_two = right_product(grad_cq, cross_query)
+        cross_gain_grad = jnp.sum(grad_norm_two * unit_two, axis=0)
+        cross_bias_grad = jnp.sum(grad_norm_two, axis=0)
+        grad_one = grad_two + norm_back(grad_norm_two, unit_two, scale_two, cross_gain)
+        grad_one_low = grad_one.astype(BF16)
+
+        output_weight_grad = left_product(self_att, grad_one_low).astype(BF16)
+        grad_self = right_product(grad_one_low, output_weight).astype(BF16)
+        grad_q, grad_k, grad_v = attend_backward(
+            queries, near_keys, near_values, grad_self, self_att, self_lse,
+            own_ids[None, :], windows[:, :, None], numbers, True, self_sizes, self_ends,
+        )
+        grad_near = right_product(grad_k, key_weight) + right_product(grad_v, value_weight)
+        grad_own = grad_near[REACH * rows :] + right_product(grad_q, query_weight)
+        to_two = grad_near[:rows]
+        to_one = grad_near[rows : REACH * rows].astype(BF16)
+        from_swap = lax.ppermute(to_one, AXIS, swap).astype(F32)
+        to_two = (to_two + jnp.where(odd, from_swap, 0.0)).astype(BF16)
+        from_two = lax.ppermute(to_two, AXIS, behind).astype(F32)
+        near_sum = jnp.concatenate([grad_near[: REACH * rows], grad_own], 0)
+        attn_gain_grad = jnp.sum(near_sum * near_unit, axis=0)
+        attn_bias_grad = jnp.sum(near_sum, axis=0)
+        grad_norm_one = grad_own + from_two + jnp.where(odd, 0.0, from_swap)
+        unit_one = near_unit[REACH * rows :]
+        input_grad = grad_one + norm_back(grad_norm_one, unit_one, near_scale[REACH * rows :], attn_gain)
+        query_grad = left_product(low_one, grad_q).astype(BF16)
+        key_grad = left_product(near_low, grad_k).astype(BF16)
+        value_grad = left_product(near_low, grad_v).astype(BF16)
+        vectors = jnp.stack(
+            [attn_gain_grad, attn_bias_grad, cross_gain_grad, cross_bias_grad, mlp_gain_grad, mlp_bias_grad]
+        )
+        grads = [
+            down_grad, up_grad, cross_output_grad, cross_query_grad, cross_key_grad, cross_value_grad, output_weight_grad,
+        ]
+        sums = [
+            reduce_scatter(grad, one_way if i % 2 else other_way, BF16, count)
+            for i, grad in enumerate([*grads, query_grad, key_grad, value_grad, caption_grad])
+        ]
+        small = reduce_scatter(vectors.T, one_way, F32, count).T
+        (down_out, up_out, cross_output_out, cross_query_out, cross_key_out, cross_value_out,
+         output_out, query_out, key_out, value_out, caption_out) = sums
+        sums = Sums(
+            up=up_out, down=down_out, cross_output=cross_output_out, cross_key=cross_key_out,
+            cross_value=cross_value_out, caption=caption_out, cross_query=cross_query_out, output=output_out,
+            query=query_out, key=key_out, value=value_out,
+        )
     return (
-        block_output,
-        input_grad,
-        caption_grad,
-        late[:, :width],
-        late[:, width : 2 * width],
-        late[:, 2 * width :],
-        middle[:, 2 * width :],
-        middle[:, width : 2 * width],
-        cross_key_grad,
-        cross_value_grad,
-        middle[:, :width],
-        up_out,
-        down_out,
-        small[:, 0],
-        small[:, 1],
-        small[:, 2],
-        small[:, 3],
-        small[:, 4],
-        small[:, 5],
+        block_output, input_grad, sums.caption,
+        sums.query, sums.key, sums.value, sums.output,
+        sums.cross_query, sums.cross_key, sums.cross_value, sums.cross_output,
+        sums.up, sums.down,
+        small[0], small[1], small[2], small[3], small[4], small[5],
     )
 
 

time: 668 us -> 336 us (0.50)
  waiting for transfers between devices: 231 us -> 16.2 us
  Pallas kernels: 75.8 us -> 259 us
  matrix products: 131 us -> 16.2 us
  other arithmetic: 92.6 us -> 11.4 us
  starting transfers between devices: 77 us -> 4.98 us
  local copies, waits for them, and re-layouts: 54 us -> 21.7 us
    ppermute x44 -> x0, waiting for transfers between devices: 212 us -> none  [the longest x36 185 us: reduce_scatter(): arrived.append(lax.ppermute(sent, AXIS, peers_along(count, axis, step)))]
    pallas_call x2 -> x1, Pallas kernels: 43.9 us -> 222 us  [layer_tail(): pl.pallas_call(functools.partial(layer_kernel, rows), in_specs=[anywhere]...]
    dot_general x19 -> x0, matrix products: 88.5 us -> none  [the longest x10 44.8 us: right_product(): return lax.dot_general(left, right, NT, preferred_element_type=F32)]
    ppermute x44 -> x0, starting transfers between devices: 72 us -> none  [the longest x36 69.2 us: reduce_scatter(): arrived.append(lax.ppermute(sent, AXIS, peers_along(count, axis, step)))]
    convert_element_type x16 -> x2, other arithmetic: 31.4 us -> 1.77 us  [the longest x1 1.37 us: body(): low_three = (unit_three * mlp_gain + mlp_bias).astype(BF16)]
    dot_general x10 -> x8, matrix products: 42.1 us -> 16.2 us  [matmul(): return jnp.dot(left, right, preferred_element_type=F32)]
    concatenate x3 -> x0, other arithmetic: 19.8 us -> none  [the longest x1 13.6 us: body(): jnp.concatenate([cross_output_grad, cross_query_grad, output_weight_grad]...]
    concatenate x2 -> x1, local copies, waits for them, and re-layouts: 17.3 us -> 0.07 us  [body(): near_tokens = jnp.concatenate([block_two, block_one, tokens], 0)]
  transfers between devices with their start and end apart: 46 -> 2, of which waited for: 26 -> 1; matrix products, arithmetic and copies ran while one was open for 19% -> 3% of each run, Pallas kernels for 0% -> 0%
where the time goes in v4:
time: 336 us; the launch traced here: 331 us
  Pallas kernels  259 us (77%)
  local copies, waits for them, and re-layouts  21.7 us (6%)
  waiting for transfers between devices  16.2 us (5%)
  matrix products  16.2 us (5%)
  other arithmetic  11.4 us (3%)
  starting transfers between devices  4.98 us (1%)
    pallas_call x1, Pallas kernels, layer_tail(): pl.pallas_call(functools.partial(layer_kernel, rows), in_specs=[anywhere]...  222 us
    pallas_call x2, Pallas kernels, attend_forward(): pl.pallas_call(functools.partial(forward_kernel, causal, sizes, ends), gr...  36.9 us
    unnamed x100, local copies, waits for them, and re-layouts  16.6 us
    dot_general x8, matrix products, matmul(): return jnp.dot(left, right, preferred_element_type=F32)  16.2 us
    ppermute x1, waiting for transfers between devices, body(): block_two = lax.ppermute(tokens, AXIS, ahead)  16.2 us
  transfers between devices with their start and end apart: 2, of which 1 were waited for; matrix products, arithmetic and copies ran while one was open for 3% of the time, Pallas kernels for 0%

profile of v4, /device:TPU:0, one launch (start us, length us, event | category | flops | bytes accessed | tf_op | source)
XLA Modules:
  0.0 331.0 jit_solution(15406411122338357763)
XLA Ops:
  0.7 4.9 %collective-permute-start = (bf16[512,1024]{1,0:T(8,128)(2,1)}, bf16[512,1024]{1,0:T(8,128)(2,1)S(1)}, u32[]{:S(2)}, u32[]{:S(2)}) collective-permute-start(bf16[512,1024]{1,0:T(8,128)(2,1)} %param.23), channel_id=1, source_target_pairs={{0,2},{1,3},{2,4},{3,5},{4,6},{5,7},{6,8},{7,9},{8,10},{9,11},{10,... | collective-permute-start | bytes 3145736 | tf_op jit(solution)/shard_map/ppermute | solution.py:1122
  5.6 0.9 pad_dynamic-slice_fusion.1
  6.5 0.7 multiply_add_fusion
  7.1 0.8 pad_dynamic-slice_fusion.2
  7.9 0.1 slice.34
  8.0 0.1 select_reduce_fusion
  8.1 0.1 copy.49.qid_ref
  8.3 0.1 copy.48.qid_ref
  8.4 0.8 copy.51
  9.3 0.8 pad_dynamic-slice_fusion.3
  10.0 0.2 fusion.12
  10.2 1.1 convert_reduce_fusion.1
  11.3 0.7 fusion.14
  12.0 0.0 copy-start.39
  12.1 16.2 %collective-permute-done = bf16[512,1024]{1,0:T(8,128)(2,1)S(1)} collective-permute-done((bf16[512,1024]{1,0:T(8,128)(2,1)}, bf16[512,1024]{1,0:T(8,128)(2,1)S(1)}, u32[]{:S(2)}, u32[]{:S(2)}) %collective-permute-start) | collective-permute-done | bytes 1048608 | tf_op jit(solution)/shard_map/ppermute | solution.py:1122
  28.2 1.8 broadcast_select_fusion
  30.0 0.1 collective-permute-start.1
  30.1 0.6 pad_maximum_fusion.refs_31_
  30.7 0.7 fusion.8.refs_29_
  31.5 1.3 convolution_convert_fusion.3.k_ref.refs_7_
  32.8 0.3 copy-done.40
  33.1 1.3 convolution_convert_fusion.2.v_ref.refs_8_
  34.4 0.1 constant_dynamic-update-slice_fusion.1
  34.5 1.5 copy-done.12
  36.0 0.1 constant_dynamic-update-slice_fusion.refs_22_
  36.0 0.5 convert_reduce_fusion
  36.5 1.0 fusion.2
  37.5 0.2 copy-done.9
  37.7 1.6 fusion.5.refs_21_
  39.4 0.0 copy-start.36
  39.4 1.3 convolution_convert_fusion.5.q_ref.refs_17_
  40.6 1.4 copy-done.36
  42.1 4.8 %convolution_convert_fusion.v_ref.refs_19_ = bf16[1536,1024]{1,0:T(8,128)(2,1)} fusion(bf16[1536,1024]{1,0:T(8,128)(2,1)S(1)} %fusion.5.refs_21_, bf16[1024,1024]{1,0:T(8,128)(2,1)S(1)} %copy-done.36), kind=kOutput, calls=%fused_computation.8 | convolution fusion | flops 3222798336 | bytes 8388608 | tf_op jit(solution)/shard_map/dot_general | solution.py:1078
  46.9 3.6 %convolution_convert_fusion.1.k_ref.refs_18_ = bf16[1536,1024]{1,0:T(8,128)(2,1)S(1)} fusion(bf16[1536,1024]{1,0:T(8,128)(2,1)S(1)} %fusion.5.refs_21_, bf16[1024,1024]{1,0:T(8,128)(2,1)S(1)} %copy-done.35), kind=kOutput, calls=%fused_computation.9 | convolution fusion | flops 3222798336 | bytes 8388608 | tf_op jit(solution)/shard_map/dot_general | solution.py:1078
  50.5 19.5 %shard_map.366 = (bf16[512,1024]{1,0:T(8,128)(2,1)S(1)}, f32[8,2,512]{2,1,0:T(2,128)S(1)}) custom-call(s32[2]{0:T(128)S(1)} %subtract_clamp_fusion.n_ref, s32[512,1]{1,0:T(8,128)S(1)} %copy.48.qid_ref, s32[2,1,1280]{2,1,0:T(1,128)S(1)} %broadcast_in_dim.29.kid_ref, bf16[512,1024]{1,0:T(8,128)(2,1)S(1)} %convolution_convert_fusion.5.q_ref.refs_17_, ...), custom_call_target="tpu_custom_call" | custom-call | flops 10737418240 | bytes 8388608 | tf_op jit(solution)/shard_map/pallas_call | solution.py:83
  70.0 0.0 copy-start.7
  70.1 1.4 fusion.18
  71.5 0.3 multiply_reduce_fusion.1
  71.8 0.3 copy-done.32
  72.2 0.4 add_convert_fusion.1.refs_9_
  72.6 1.2 copy-done.38
  73.8 1.3 convolution_convert_fusion.4.q_ref.refs_6_
  75.1 17.4 %shard_map.367 = (bf16[512,1024]{1,0:T(8,128)(2,1)S(1)}, f32[8,2,512]{2,1,0:T(2,128)S(1)}) custom-call(s32[2]{0:T(128)S(1)} %broadcast.166.n_ref, s32[512,1]{1,0:T(8,128)S(1)} %copy.49.qid_ref, s32[2,1,512]{2,1,0:T(1,128)S(1)} %broadcast_in_dim_broadcast_in_dim.2.kid_ref, bf16[512,1024]{1,0:T(8,128)(2,1)S(1)} %convolution_convert_fusion.4.q_ref.refs_6_, ...), custom_call_target="tpu_custom_call" | custom-call | flops 4294967296 | bytes 8388608 | tf_op jit(solution)/shard_map/pallas_call | solution.py:83
  92.6 1.4 fusion.19
  94.0 0.0 copy-start.11
  94.0 0.3 multiply_reduce_fusion
  94.4 0.3 copy-done.33
  94.7 1.4 add_convert_fusion.refs_0_
  96.1 222.1 %shard_map.368 = (f32[32,4096]{1,0:T(8,128)}, f32[128,1024]{1,0:T(8,128)}, f32[32,1024]{1,0:T(8,128)}, f32[32,1024]{1,0:T(8,128)}, f32[32,1024]{1,0:T(8,128)}, /...) custom-call(bf16[512,1024]{1,0:T(8,128)(2,1)} %add_convert_fusion.re, ...), custom_call_target="tpu_custom_call" | custom-call | flops 17179869184 | bytes 67108864 | tf_op jit(solution)/shard_map/pallas_call | solution.py:1060
  318.2 0.9 constant_dynamic-slice_fusion
  319.1 0.5 slice_bitcast_fusion
  319.6 2.3 copy.67
  322.0 1.3 copy.68
  323.3 0.6 copy.69
  323.9 0.7 copy.70
  324.6 0.7 copy.71
  325.2 0.7 copy.72
  325.9 0.7 copy.73
  326.5 0.7 copy.74
  327.2 0.7 copy.75
  327.9 0.7 copy.76
  328.5 0.7 copy.77
  329.2 0.8 copy.78
  330.0 0.8 copy.79
  (89 shorter events, 0.3 us)
Async XLA Ops:
  0.7 27.6 %collective-permute-start = (bf16[512,1024]{1,0:T(8,128)(2,1)}, bf16[512,1024]{1,0:T(8,128)(2,1)S(1)}, u32[]{:S(2)}, u32[]{:S(2)}) collective-permute-start(bf16[512,1024]{1,0:T(8,128)(2,1)} %param.23), channel_id=1, source_target_pairs={{0,2},{1,3},{2,4},{3,5},{4,6},{5,7},{6,8},{7,9},{8,10},{9,11},{10,... | collective-permute-start | bytes 3145736 | tf_op jit(solution)/shard_map/ppermute | solution.py:1122
  8.1 21.9 %copy-start.30 = (s32[512]{0:T(512)}, s32[512]{0:T(512)S(1)}, u32[]{:S(2)}) copy-start(s32[512]{0:T(512)S(1)} %select_reduce_fusion) | copy-start | bytes 6148
  12.0 18.0 %copy-start.27 = (f32[1024]{0:T(1024)S(1)}, f32[1024]{0:T(1024)}, u32[]{:S(2)}) copy-start(f32[1024]{0:T(1024)} %param.36) | copy-start | bytes 12292
  12.0 18.1 %copy-start.28 = (f32[1024]{0:T(1024)S(1)}, f32[1024]{0:T(1024)}, u32[]{:S(2)}) copy-start(f32[1024]{0:T(1024)} %param.38) | copy-start | bytes 12292
  12.0 18.1 %copy-start.29 = (f32[1024]{0:T(1024)S(1)}, f32[1024]{0:T(1024)}, u32[]{:S(2)}) copy-start(f32[1024]{0:T(1024)} %param.40) | copy-start | bytes 12292
  12.0 19.4 %copy-start.39 = (bf16[1024,1024]{1,0:T(8,128)(2,1)S(1)}, bf16[1024,1024]{1,0:T(8,128)(2,1)}, u32[]{:S(2)}) copy-start(bf16[1024,1024]{1,0:T(8,128)(2,1)} %refs_13_.1) | copy-start | bytes 6291460
  12.1 19.4 %copy-start.42 = (bf16[512,1024]{1,0:T(8,128)(2,1)S(1)}, bf16[512,1024]{1,0:T(8,128)(2,1)}, u32[]{:S(2)}) copy-start(bf16[512,1024]{1,0:T(8,128)(2,1)} %refs_11_.1) | copy-start | bytes 3145732
  30.0 4.4 %collective-permute-start.1 = (bf16[512,1024]{1,0:T(8,128)(2,1)S(1)}, bf16[512,1024]{1,0:T(8,128)(2,1)S(1)}, u32[]{:S(2)}, u32[]{:S(2)}) collective-permute-start(bf16[512,1024]{1,0:T(8,128)(2,1)S(1)} %get-tuple-element.55), channel_id=1, source_target_pairs={{0,1},{1,0},{2,3},{3,2},{4,5},{5,4},{6,7},{7,6},{8,9},{9,8},{10,11... | collective-permute-start | bytes 3145736 | tf_op jit(solution)/shard_map/ppermute | solution.py:1123
  31.5 1.6 copy-start.40
  33.1 42.0 %copy-start.3 = (bf16[512,1024]{1,0:T(8,128)(2,1)}, bf16[512,1024]{1,0:T(8,128)(2,1)S(1)}, u32[]{:S(2)}) copy-start(bf16[512,1024]{1,0:T(8,128)(2,1)S(1)} %convolution_convert_fusion.3.k_ref.refs_7_) | copy-start | bytes 3145732
  34.3 40.8 %copy-start.4 = (bf16[512,1024]{1,0:T(8,128)(2,1)}, bf16[512,1024]{1,0:T(8,128)(2,1)S(1)}, u32[]{:S(2)}) copy-start(bf16[512,1024]{1,0:T(8,128)(2,1)S(1)} %convolution_convert_fusion.2.v_ref.refs_8_) | copy-start | bytes 3145732
  34.4 1.6 copy-start.12
  36.0 1.7 copy-start.9
  36.5 1.2 copy-start.31
  37.7 1.6 copy-start.34
  39.3 7.5 %copy-start.13 = (bf16[1536,1024]{1,0:T(8,128)(2,1)}, bf16[1536,1024]{1,0:T(8,128)(2,1)S(1)}, u32[]{:S(2)}) copy-start(bf16[1536,1024]{1,0:T(8,128)(2,1)S(1)} %fusion.5.refs_21_) | copy-start | bytes 9437188
  39.4 2.7 copy-start.36
  42.1 8.4 %copy-start.5 = (bf16[512,1024]{1,0:T(8,128)(2,1)}, bf16[512,1024]{1,0:T(8,128)(2,1)S(1)}, u32[]{:S(2)}) copy-start(bf16[512,1024]{1,0:T(8,128)(2,1)S(1)} %convolution_convert_fusion.5.q_ref.refs_17_) | copy-start | bytes 3145732
  42.1 4.8 %copy-start.35 = (bf16[1024,1024]{1,0:T(8,128)(2,1)S(1)}, bf16[1024,1024]{1,0:T(8,128)(2,1)}, u32[]{:S(2)}) copy-start(bf16[1024,1024]{1,0:T(8,128)(2,1)} %refs_24_.1) | copy-start | bytes 6291460
  50.5 19.5 %copy-start = (bf16[1536,1024]{1,0:T(8,128)(2,1)}, bf16[1536,1024]{1,0:T(8,128)(2,1)S(1)}, u32[]{:S(2)}) copy-start(bf16[1536,1024]{1,0:T(8,128)(2,1)S(1)} %convolution_convert_fusion.1.k_ref.refs_18_) | copy-start | bytes 9437188
  50.5 19.6 %copy-start.37 = (bf16[1024,1024]{1,0:T(8,128)(2,1)S(1)}, bf16[1024,1024]{1,0:T(8,128)(2,1)}, u32[]{:S(2)}) copy-start(bf16[1024,1024]{1,0:T(8,128)(2,1)} %refs_16_.1) | copy-start | bytes 6291460
  70.0 1.4 copy-start.1
  70.0 1.4 copy-start.7
  71.4 21.1 %copy-start.10 = (f32[512,1024]{1,0:T(8,128)}, f32[512,1024]{1,0:T(8,128)S(1)}, u32[]{:S(2)}) copy-start(f32[512,1024]{1,0:T(8,128)S(1)} %get-tuple-element.66.refs_10_) | copy-start | bytes 6291460
  71.4 0.7 copy-start.32
  71.8 2.0 copy-start.38
  73.8 1.3 copy-start.15
  75.1 17.5 %copy-start.6 = (bf16[512,1024]{1,0:T(8,128)(2,1)}, bf16[512,1024]{1,0:T(8,128)(2,1)S(1)}, u32[]{:S(2)}) copy-start(bf16[512,1024]{1,0:T(8,128)(2,1)S(1)} %convolution_convert_fusion.4.q_ref.refs_6_) | copy-start | bytes 3145732
  75.1 17.5 %copy-start.41 = (bf16[1024,1024]{1,0:T(8,128)(2,1)S(1)}, bf16[1024,1024]{1,0:T(8,128)(2,1)}, u32[]{:S(2)}) copy-start(bf16[1024,1024]{1,0:T(8,128)(2,1)} %refs_12_.1) | copy-start | bytes 6291460
  92.5 1.4 copy-start.2
  92.6 1.4 copy-start.8
  94.0 2.1 copy-start.11
  94.0 0.7 copy-start.33
  318.2 3.7 %copy-start.14 = (f32[512,1024]{1,0:T(8,128)S(1)}, f32[512,1024]{1,0:T(8,128)}, u32[]{:S(2)}) copy-start(f32[512,1024]{1,0:T(8,128)} %get-tuple-element.89) | copy-start | bytes 6291460
  321.9 1.4 copy-start.26
  321.9 2.0 copy-start.25
  321.9 2.7 copy-start.24
  321.9 3.3 %copy-start.23 = (f32[32,1024]{1,0:T(8,128)S(1)}, f32[32,1024]{1,0:T(8,128)}, u32[]{:S(2)}) copy-start(f32[32,1024]{1,0:T(8,128)} %get-tuple-element.93) | copy-start | bytes 393220
  321.9 4.0 %copy-start.22 = (f32[32,1024]{1,0:T(8,128)S(1)}, f32[32,1024]{1,0:T(8,128)}, u32[]{:S(2)}) copy-start(f32[32,1024]{1,0:T(8,128)} %get-tuple-element.94) | copy-start | bytes 393220
  321.9 4.6 %copy-start.21 = (f32[32,1024]{1,0:T(8,128)S(1)}, f32[32,1024]{1,0:T(8,128)}, u32[]{:S(2)}) copy-start(f32[32,1024]{1,0:T(8,128)} %get-tuple-element.95) | copy-start | bytes 393220
  321.9 5.3 %copy-start.20 = (f32[32,1024]{1,0:T(8,128)S(1)}, f32[32,1024]{1,0:T(8,128)}, u32[]{:S(2)}) copy-start(f32[32,1024]{1,0:T(8,128)} %get-tuple-element.96) | copy-start | bytes 393220
  321.9 5.9 %copy-start.19 = (f32[32,1024]{1,0:T(8,128)S(1)}, f32[32,1024]{1,0:T(8,128)}, u32[]{:S(2)}) copy-start(f32[32,1024]{1,0:T(8,128)} %get-tuple-element.97) | copy-start | bytes 393220
  321.9 6.6 %copy-start.18 = (f32[32,1024]{1,0:T(8,128)S(1)}, f32[32,1024]{1,0:T(8,128)}, u32[]{:S(2)}) copy-start(f32[32,1024]{1,0:T(8,128)} %get-tuple-element.98) | copy-start | bytes 393220
  323.3 5.9 %copy-start.17 = (f32[32,4096]{1,0:T(8,128)S(1)}, f32[32,4096]{1,0:T(8,128)}, u32[]{:S(2)}) copy-start(f32[32,4096]{1,0:T(8,128)} %get-tuple-element.99) | copy-start | bytes 1572868
  323.3 6.7 %copy-start.16 = (f32[128,1024]{1,0:T(8,128)S(1)}, f32[128,1024]{1,0:T(8,128)}, u32[]{:S(2)}) copy-start(f32[128,1024]{1,0:T(8,128)} %get-tuple-element.100) | copy-start | bytes 1572868

commit v5 on v4

--- a/solution.py
+++ b/solution.py
@@ -105,6 +105,79 @@
         compiler_params=pltpu.CompilerParams(vmem_limit_bytes=48 << 20),
         cost_estimate=pl.CostEstimate(flops=4 * flops, bytes_accessed=8 << 20, transcendentals=rows * span * HEADS),
     )(numbers, qid, kid, queries, keys, values)
+
+
+def caption_lanes(value, lines, length):
+    return jnp.concatenate([value[r * length : (r + 1) * length] for r in range(lines)], 1)
+
+
+def spread(value, in_row):
+    return jnp.concatenate([jnp.where(mask, value, jnp.zeros_like(value)) for mask in in_row], 1)
+
+
+def rows_of(code, lines, length):
+    return [(code >= r * length) & (code < (r + 1) * length) for r in range(lines)]
+
+
+def either(masks):
+    result = masks[0]
+    for mask in masks[1:]:
+        result = result | mask
+    return result
+
+
+def cross_forward_kernel(code_ref, key_ref, q_ref, k_ref, v_ref, o_ref, lse_ref):
+    lines, length = key_ref.shape
+    keys = caption_lanes(k_ref[...], lines, length)
+    values = caption_lanes(v_ref[...], lines, length)
+    lane = lax.broadcasted_iota(jnp.int32, (TILE, LANES), 1)
+    for tile in range(q_ref.shape[0] // TILE):
+        mine = slice(tile * TILE, (tile + 1) * TILE)
+        code = jnp.broadcast_to(code_ref[mine, :], (TILE, LANES))
+        in_row = rows_of(code, lines, length)
+        allowed = either([code[:, :length] == key_ref[r : r + 1, :] for r in range(lines)])
+        query = q_ref[mine, :] * jnp.asarray(0.125, BF16)
+        outs = []
+        for half in range(2):
+            scores = lax.dot_general(
+                spread(head_lanes(query, half), in_row), keys, NT, preferred_element_type=F32
+            )
+            scores = jnp.where(allowed, scores, NEG)
+            row_max = jnp.max(scores, axis=1, keepdims=True)
+            weights = jnp.exp(scores - row_max)
+            summed = jnp.sum(weights, axis=1, keepdims=True)
+            wide = jnp.dot(weights.astype(BF16), values, preferred_element_type=F32)
+            out = jnp.zeros((TILE, LANES), F32)
+            for r in range(lines):
+                out = jnp.where(in_row[r], wide[:, r * LANES : (r + 1) * LANES], out)
+            outs.append(out / summed)
+            lse = jnp.broadcast_to(row_max + jnp.log(summed), (TILE, LANES))
+            lse_ref[0, half : half + 1, mine] = jnp.transpose(lse)[:1]
+        o_ref[mine, :] = jnp.where(lane < LANES // 2, outs[0], outs[1]).astype(BF16)
+
+
+def cross_forward(queries, keys, values, query_code, key_codes):
+    rows, width = queries.shape
+    pairs = width // LANES
+    text = keys.shape[0]
+    own = pl.BlockSpec((rows, LANES), lambda h: (0, h))
+    wide = pl.BlockSpec((text, LANES), lambda h: (0, h))
+    return pl.pallas_call(
+        cross_forward_kernel,
+        grid=(pairs,),
+        in_specs=[
+            pl.BlockSpec((rows, 1), lambda h: (0, 0)), pl.BlockSpec(key_codes.shape, lambda h: (0, 0)), own, wide, wide,
+        ],
+        out_specs=[own, pl.BlockSpec((1, 2, rows), lambda h: (h, 0, 0))],
+        out_shape=[
+            jax.ShapeDtypeStruct((rows, width), BF16),
+            jax.ShapeDtypeStruct((pairs, 2, rows), F32),
+        ],
+        compiler_params=pltpu.CompilerParams(vmem_limit_bytes=32 << 20),
+        cost_estimate=pl.CostEstimate(
+            flops=4 * rows * text * width, bytes_accessed=4 << 20, transcendentals=rows * text * HEADS // 4
+        ),
+    )(query_code, key_codes, queries, keys, values)
 
 
 def backward_kernel(
@@ -1031,6 +1104,33 @@
     out_copy.wait()
 
 
+def copy_kernel(number, *refs):
+    sources, targets, staged = refs[:number], refs[number : 2 * number], refs[2 * number : 3 * number]
+    sem_in, sem_out = refs[3 * number :]
+    inward = [pltpu.make_async_copy(sources[i], staged[i], sem_in.at[i]) for i in range(number)]
+    outward = [pltpu.make_async_copy(staged[i], targets[i], sem_out.at[i]) for i in range(number)]
+    for copy in inward:
+        copy.start()
+    for i in range(number):
+        inward[i].wait()
+        outward[i].start()
+    for copy in outward:
+        copy.wait()
+
+
+def copy_all(arrays):
+    anywhere = pl.BlockSpec(memory_space=pl.ANY)
+    return pl.pallas_call(
+        functools.partial(copy_kernel, len(arrays)),
+        in_specs=[anywhere] * len(arrays),
+        out_specs=[anywhere] * len(arrays),
+        out_shape=[jax.ShapeDtypeStruct(array.shape, array.dtype) for array in arrays],
+        scratch_shapes=[pltpu.VMEM(array.shape, array.dtype) for array in arrays]
+        + [pltpu.SemaphoreType.DMA((len(arrays),))] * 2,
+        cost_estimate=pl.CostEstimate(flops=0, bytes_accessed=12 << 20, transcendentals=0),
+    )(*arrays)
+
+
 def layer_tail(far, near):
     rows, width = far.queries.shape
     count = 32
@@ -1071,7 +1171,9 @@
         compiler_params=pltpu.CompilerParams(collective_id=0, has_side_effects=True, vmem_limit_bytes=63 << 20),
         cost_estimate=pl.CostEstimate(flops=1 << 34, bytes_accessed=64 << 20, transcendentals=0),
     )(*far, *near)
-    return Sums(*results[: len(Sums._fields)]), *results[len(Sums._fields) :]
+    small = results[len(Sums._fields)]
+    copied = copy_all([*results[: len(Sums._fields)], *results[len(Sums._fields) + 1 :]])
+    return Sums(*copied[:-2]), small, *copied[-2:]
 
 
 def matmul(left, right):
@@ -1119,7 +1221,13 @@
     ahead = [(i, i + 2) for i in range(count - 2)]
     behind = [(i + 2, i) for i in range(count - 2)]
 
+    inputs = tokens.astype(F32)
+    low_one = (normalise(inputs)[0] * attn_gain + attn_bias).astype(BF16)
+    queries = matmul(low_one, query_weight).astype(BF16)
+    text_keys = matmul(caption_states, cross_key).astype(BF16)
+    text_values = matmul(caption_states, cross_value).astype(BF16)
     block_two = lax.ppermute(tokens, AXIS, ahead)
+    block_two, queries, text_keys, text_values = lax.optimization_barrier((block_two, queries, text_keys, text_values))
     block_one = lax.ppermute(jnp.where(odd, block_two, tokens), AXIS, swap)
     near_tokens = jnp.concatenate([block_two, block_one, tokens], 0)
 
@@ -1147,11 +1255,8 @@
     no_numbers = jnp.zeros((tiles,), jnp.int32)
     text_ends = (text, 0)
 
-    inputs = tokens.astype(F32)
     near_unit, near_scale = normalise(near_tokens.astype(F32))
     near_low = (near_unit * attn_gain + attn_bias).astype(BF16)
-    low_one = near_low[REACH * rows :]
-    queries = matmul(low_one, query_weight).astype(BF16)
     near_keys = matmul(near_low, key_weight).astype(BF16)
     near_values = matmul(near_low, value_weight).astype(BF16)
     self_att, self_lse = attend_forward(
@@ -1161,10 +1266,8 @@
     unit_two, scale_two = normalise(after_one)
     low_two = (unit_two * cross_gain + cross_bias).astype(BF16)
     cross_q = matmul(low_two, cross_query).astype(BF16)
-    text_keys = matmul(caption_states, cross_key).astype(BF16)
-    text_values = matmul(caption_states, cross_value).astype(BF16)
-    cross_att, cross_lse = attend_forward(
-        cross_q, text_keys, text_values, query_code[:, None], text_code[:, None, :], no_numbers, False, (text,), text_ends
+    cross_att, cross_lse = cross_forward(
+        cross_q, text_keys, text_values, query_code[:, None], key_code.reshape(-1, caption_len)
     )
     after_two = after_one + matmul(cross_att, cross_output)
     unit_three, scale_three = normalise(after_two)

time: 336 us -> 323 us (0.961)
  local copies, waits for them, and re-layouts: 21.7 us -> 4.43 us
  waiting for transfers between devices: 16.2 us -> 10.7 us
  Pallas kernels: 259 us -> 263 us
  matrix products: 16.2 us -> 19.9 us
    pallas_call x0 -> x2, Pallas kernels: none -> 20.3 us  [the longest x1 15 us: cross_forward(): pl.pallas_call(cross_forward_kernel, grid=(pairs,), in_specs=[pl.BlockSpe...]
    pallas_call x2 -> x1, Pallas kernels: 36.9 us -> 19.6 us  [attend_forward(): pl.pallas_call(functools.partial(forward_kernel, causal, sizes, ends), gr...]
    unnamed x100 -> x67, local copies, waits for them, and re-layouts: 16.6 us -> 2.27 us
    ppermute x1, waiting for transfers between devices: 16.2 us -> 10.2 us  [body(): block_two = lax.ppermute(tokens, AXIS, ahead)]
    dot_general x8, matrix products: 16.2 us -> 19.9 us  [matmul(): return jnp.dot(left, right, preferred_element_type=F32)]
  transfers between devices with their start and end apart: 2 -> 2, of which waited for: 1 -> 2; matrix products, arithmetic and copies ran while one was open for 3% -> 5% of each run, Pallas kernels for 0% -> 0%
where the time goes in v5:
time: 323 us; the launch traced here: 317 us
  Pallas kernels  263 us (81%)
  matrix products  19.9 us (6%)
  other arithmetic  12.1 us (4%)
  waiting for transfers between devices  10.7 us (3%)
  starting transfers between devices  5.11 us (2%)
  local copies, waits for them, and re-layouts  4.43 us (1%)
    pallas_call x1, Pallas kernels, layer_tail(): pl.pallas_call(functools.partial(layer_kernel, rows), in_specs=[anywhere]...  224 us
    dot_general x8, matrix products, matmul(): return jnp.dot(left, right, preferred_element_type=F32)  19.9 us
    pallas_call x1, Pallas kernels, attend_forward(): pl.pallas_call(functools.partial(forward_kernel, causal, sizes, ends), gr...  19.6 us
    pallas_call x1, Pallas kernels, cross_forward(): pl.pallas_call(cross_forward_kernel, grid=(pairs,), in_specs=[pl.BlockSpe...  15 us
    ppermute x1, waiting for transfers between devices, body(): block_two = lax.ppermute(tokens, AXIS, ahead)  10.2 us
  transfers between devices with their start and end apart: 2, of which 2 were waited for; matrix products, arithmetic and copies ran while one was open for 5% of the time, Pallas kernels for 0%

profile of v5, /device:TPU:0, one launch (start us, length us, event | category | flops | bytes accessed | tf_op | source)
XLA Modules:
  0.0 317.2 jit_solution(3005585070399146386)
XLA Ops:
  0.7 0.0 copy-start.30
  0.7 5.0 %collective-permute-start = (bf16[512,1024]{1,0:T(8,128)(2,1)}, bf16[512,1024]{1,0:T(8,128)(2,1)S(1)}, u32[]{:S(2)}, u32[]{:S(2)}) collective-permute-start(bf16[512,1024]{1,0:T(8,128)(2,1)} %param.23), channel_id=1, source_target_pairs={{0,2},{1,3},{2,4},{3,5},{4,6},{5,7},{6,8},{7,9},{8,10},{9,11},{10,... | collective-permute-start | bytes 3145736 | tf_op jit(solution)/shard_map/ppermute | solution.py:1229
  5.8 1.4 convert_reduce_fusion.2
  7.2 1.6 fusion.8
  8.8 0.1 pad_dynamic-slice_fusion.2
  8.9 0.1 pad_dynamic-slice_fusion.1
  9.0 0.0 copy-done.31
  9.0 0.0 copy-done.32
  9.1 0.1 select_reduce_fusion
  9.2 0.0 copy-start.16
  9.2 0.0 copy-start.17
  9.2 0.0 copy-start.18
  9.2 0.0 copy-start.19
  9.2 2.9 convolution_convert_fusion.4.k_ref.refs_7_
  12.1 0.7 pad_maximum_fusion.refs_31_
  12.9 0.1 slice.31
  13.0 0.1 copy.49.code_ref
  13.1 0.1 copy.48.qid_ref
  13.3 0.1 copy.51
  13.5 0.0 copy-start.10
  13.5 0.0 copy-start.21
  13.5 0.0 copy-start.24
  13.5 3.3 %convolution_convert_fusion.3.v_ref.refs_8_ = bf16[512,1024]{1,0:T(8,128)(2,1)S(1)} fusion(bf16[512,1024]{1,0:T(8,128)(2,1)} %refs_11_.1, bf16[1024,1024]{1,0:T(8,128)(2,1)} %refs_14_.1), kind=kOutput, calls=%fused_computation.26 | convolution fusion | flops 1074266112 | bytes 4194304 | tf_op jit(solution)/shard_map/dot_general | solution.py:1180
  16.9 1.3 convolution_convert_fusion.5.q_ref.refs_17_
  18.2 10.2 %collective-permute-done = bf16[512,1024]{1,0:T(8,128)(2,1)S(1)} collective-permute-done((bf16[512,1024]{1,0:T(8,128)(2,1)}, bf16[512,1024]{1,0:T(8,128)(2,1)S(1)}, u32[]{:S(2)}, u32[]{:S(2)}) %collective-permute-start) | collective-permute-done | bytes 1048608 | tf_op jit(solution)/shard_map/ppermute | solution.py:1229
  28.4 0.6 broadcast_select_fusion
  29.0 0.1 collective-permute-start.1
  29.0 0.1 pad_dynamic-slice_fusion.3
  29.1 0.2 fusion.22
  29.3 1.1 convert_reduce_fusion.1
  30.4 0.7 fusion.18.refs_29_
  31.2 0.5 collective-permute-done.1
  31.7 0.1 constant_dynamic-update-slice_fusion.1
  31.8 0.1 constant_dynamic-update-slice_fusion.refs_22_
  31.9 0.5 convert_reduce_fusion
  32.3 1.0 fusion.2
  33.3 0.2 copy-done.9
  33.5 1.6 fusion.5.refs_21_
  35.1 0.0 copy-start.25
  35.2 4.8 %convolution_convert_fusion.v_ref.refs_19_ = bf16[1536,1024]{1,0:T(8,128)(2,1)} fusion(bf16[1536,1024]{1,0:T(8,128)(2,1)S(1)} %fusion.5.refs_21_, bf16[1024,1024]{1,0:T(8,128)(2,1)S(1)} %copy-done.26), kind=kOutput, calls=%fused_computation.8 | convolution fusion | flops 3222798336 | bytes 8388608 | tf_op jit(solution)/shard_map/dot_general | solution.py:1180
  39.9 3.6 %convolution_convert_fusion.1.k_ref.refs_18_ = bf16[1536,1024]{1,0:T(8,128)(2,1)S(1)} fusion(bf16[1536,1024]{1,0:T(8,128)(2,1)S(1)} %fusion.5.refs_21_, bf16[1024,1024]{1,0:T(8,128)(2,1)S(1)} %copy-done.25), kind=kOutput, calls=%fused_computation.9 | convolution fusion | flops 3222798336 | bytes 8388608 | tf_op jit(solution)/shard_map/dot_general | solution.py:1180
  43.6 0.0 copy-start.27
  43.6 19.6 %shard_map.366 = (bf16[512,1024]{1,0:T(8,128)(2,1)S(1)}, f32[8,2,512]{2,1,0:T(2,128)S(1)}) custom-call(s32[2]{0:T(128)S(1)} %subtract_clamp_fusion.n_ref, s32[512,1]{1,0:T(8,128)S(1)} %copy.48.qid_ref, s32[2,1,1280]{2,1,0:T(1,128)S(1)} %broadcast_in_dim.29.kid_ref, bf16[512,1024]{1,0:T(8,128)(2,1)S(1)} %convolution_convert_fusion.5.q_ref.refs_17_, ...), custom_call_target="tpu_custom_call" | custom-call | flops 10737418240 | bytes 8388608 | tf_op jit(solution)/shard_map/pallas_call | solution.py:83
  63.2 0.0 copy-start.8
  63.3 1.4 fusion.28
  64.6 0.0 copy-start.22
  64.7 0.3 multiply_reduce_fusion.1
  65.0 0.3 copy-done.22
  65.4 0.4 add_convert_fusion.1.refs_9_
  65.8 1.2 copy-done.28
  67.0 1.3 convolution_convert_fusion.2.q_ref.refs_6_
  68.3 0.0 copy-start.29
  68.3 15.0 %shard_map.367 = (bf16[512,1024]{1,0:T(8,128)(2,1)S(1)}, f32[8,2,512]{2,1,0:T(2,128)S(1)}) custom-call(s32[512,1]{1,0:T(8,128)S(1)} %copy.49.code_ref, s32[4,128]{1,0:T(4,128)S(1)} %fusion.25.key_ref, bf16[512,1024]{1,0:T(8,128)(2,1)S(1)} %convolution_convert_fusion.2.q_ref.refs_6_, bf16[512,1024]{1,0:T(8,128)(2,1)S(1)} %convolution_convert_fusion.4.k_ref.refs_7_, ...), custom_call_target="tpu_custom_call" | custom-call | flops 1073741824 | bytes 4194304 | tf_op jit(solution)/shard_map/pallas_call | solution.py:165
  83.3 0.0 copy-start.7
  83.3 1.3 fusion.29
  84.7 0.0 copy-start.12
  84.7 0.0 copy-start.23
  84.7 0.3 multiply_reduce_fusion
  85.1 0.3 copy-done.23
  85.4 1.4 add_convert_fusion.refs_0_
  86.8 223.5 %shard_map.368 = (f32[32,4096]{1,0:T(8,128)}, f32[128,1024]{1,0:T(8,128)}, f32[32,1024]{1,0:T(8,128)}, f32[32,1024]{1,0:T(8,128)}, f32[32,1024]{1,0:T(8,128)}, /...) custom-call(bf16[512,1024]{1,0:T(8,128)(2,1)} %add_convert_fusion.re, ...), custom_call_target="tpu_custom_call" | custom-call | flops 17179869184 | bytes 67108864 | tf_op jit(solution)/shard_map/pallas_call | solution.py:1160
  310.3 0.8 constant_dynamic-slice_fusion
  311.1 0.5 slice_bitcast_fusion
  311.6 5.3 %shard_map.369 = (f32[32,4096]{1,0:T(8,128)}, f32[128,1024]{1,0:T(8,128)}, f32[32,1024]{1,0:T(8,128)}, f32[32,1024]{1,0:T(8,128)}, f32[32,1024]{1,0:T(8,128)}, /...) custom-call(f32[32,4096]{1,0:T(8,128)} %get-tuple-element.62.refs_0_, ...), custom_call_target="tpu_custom_call" | custom-call | bytes 12582912 | tf_op jit(solution)/shard_map/pallas_call | solution.py:1123
  (59 shorter events, 0.2 us)
Async XLA Ops:
  0.7 8.2 %copy-start.15 = (s32[16384]{0:T(1024)S(1)}, s32[16384]{0:T(1024)}, u32[]{:S(2)}) copy-start(s32[16384]{0:T(1024)} %param.42) | copy-start | bytes 196612
  0.7 8.4 %copy-start.31 = (s32[24]{0:T(128)S(1)}, s32[24]{0:T(128)}, u32[]{:S(2)}) copy-start(s32[24]{0:T(128)} %param.45) | copy-start | bytes 292
  0.7 8.4 %copy-start.32 = (s32[24]{0:T(128)S(1)}, s32[24]{0:T(128)}, u32[]{:S(2)}) copy-start(s32[24]{0:T(128)} %param.44) | copy-start | bytes 292
  0.7 8.5 %copy-start.30 = (bf16[512,1024]{1,0:T(8,128)(2,1)S(1)}, bf16[512,1024]{1,0:T(8,128)(2,1)}, u32[]{:S(2)}) copy-start(bf16[512,1024]{1,0:T(8,128)(2,1)} %refs_11_.1) | copy-start | bytes 3145732
  0.7 27.7 %collective-permute-start = (bf16[512,1024]{1,0:T(8,128)(2,1)}, bf16[512,1024]{1,0:T(8,128)(2,1)S(1)}, u32[]{:S(2)}, u32[]{:S(2)}) collective-permute-start(bf16[512,1024]{1,0:T(8,128)(2,1)} %param.23), channel_id=1, source_target_pairs={{0,2},{1,3},{2,4},{3,5},{4,6},{5,7},{6,8},{7,9},{8,10},{9,11},{10,... | collective-permute-start | bytes 3145736 | tf_op jit(solution)/shard_map/ppermute | solution.py:1229
  9.1 3.8 %copy-start.20 = (s32[512]{0:T(512)}, s32[512]{0:T(512)S(1)}, u32[]{:S(2)}) copy-start(s32[512]{0:T(512)S(1)} %select_reduce_fusion) | copy-start | bytes 6148
  9.2 2.9 copy-start.16
  9.2 2.9 copy-start.17
  9.2 2.9 copy-start.18
  9.2 4.1 %copy-start.19 = (s32[4,128]{1,0:T(4,128)S(1)}, s32[4,128]{1,0:T(4,128)}, u32[]{:S(2)}) copy-start(s32[4,128]{1,0:T(4,128)} %param.43) | copy-start | bytes 6148
  12.1 56.1 %copy-start = (bf16[512,1024]{1,0:T(8,128)(2,1)}, bf16[512,1024]{1,0:T(8,128)(2,1)S(1)}, u32[]{:S(2)}) copy-start(bf16[512,1024]{1,0:T(8,128)(2,1)S(1)} %convolution_convert_fusion.4.k_ref.refs_7_) | copy-start | bytes 3145732
  13.5 3.4 %copy-start.10 = (bf16[512,1024]{1,0:T(8,128)(2,1)S(1)}, bf16[512,1024]{1,0:T(8,128)(2,1)}, u32[]{:S(2)}) copy-start(bf16[512,1024]{1,0:T(8,128)(2,1)} %param.23) | copy-start | bytes 3145732
  13.5 3.4 %copy-start.21 = (f32[1024]{0:T(1024)S(1)}, f32[1024]{0:T(1024)}, u32[]{:S(2)}) copy-start(f32[1024]{0:T(1024)} %param.37) | copy-start | bytes 12292
  13.5 3.4 %copy-start.24 = (bf16[1024,1024]{1,0:T(8,128)(2,1)S(1)}, bf16[1024,1024]{1,0:T(8,128)(2,1)}, u32[]{:S(2)}) copy-start(bf16[1024,1024]{1,0:T(8,128)(2,1)} %refs_23_.1) | copy-start | bytes 6291460
  16.8 51.4 %copy-start.1 = (bf16[512,1024]{1,0:T(8,128)(2,1)}, bf16[512,1024]{1,0:T(8,128)(2,1)S(1)}, u32[]{:S(2)}) copy-start(bf16[512,1024]{1,0:T(8,128)(2,1)S(1)} %convolution_convert_fusion.3.v_ref.refs_8_) | copy-start | bytes 3145732
  18.2 25.4 %copy-start.6 = (bf16[512,1024]{1,0:T(8,128)(2,1)}, bf16[512,1024]{1,0:T(8,128)(2,1)S(1)}, u32[]{:S(2)}) copy-start(bf16[512,1024]{1,0:T(8,128)(2,1)S(1)} %convolution_convert_fusion.5.q_ref.refs_17_) | copy-start | bytes 3145732
  29.0 2.7 collective-permute-start.1
  31.8 1.6 copy-start.9
  33.5 1.6 copy-start.26
  35.1 4.8 %copy-start.13 = (bf16[1536,1024]{1,0:T(8,128)(2,1)}, bf16[1536,1024]{1,0:T(8,128)(2,1)S(1)}, u32[]{:S(2)}) copy-start(bf16[1536,1024]{1,0:T(8,128)(2,1)S(1)} %fusion.5.refs_21_) | copy-start | bytes 9437188
  35.1 4.8 %copy-start.25 = (bf16[1024,1024]{1,0:T(8,128)(2,1)S(1)}, bf16[1024,1024]{1,0:T(8,128)(2,1)}, u32[]{:S(2)}) copy-start(bf16[1024,1024]{1,0:T(8,128)(2,1)} %refs_24_.1) | copy-start | bytes 6291460
  43.6 19.6 %copy-start.4 = (bf16[1536,1024]{1,0:T(8,128)(2,1)}, bf16[1536,1024]{1,0:T(8,128)(2,1)S(1)}, u32[]{:S(2)}) copy-start(bf16[1536,1024]{1,0:T(8,128)(2,1)S(1)} %convolution_convert_fusion.1.k_ref.refs_18_) | copy-start | bytes 9437188
  43.6 19.7 %copy-start.27 = (bf16[1024,1024]{1,0:T(8,128)(2,1)S(1)}, bf16[1024,1024]{1,0:T(8,128)(2,1)}, u32[]{:S(2)}) copy-start(bf16[1024,1024]{1,0:T(8,128)(2,1)} %refs_16_.1) | copy-start | bytes 6291460
  63.2 1.4 copy-start.5
  63.2 1.4 copy-start.8
  64.6 18.7 %copy-start.11 = (f32[512,1024]{1,0:T(8,128)}, f32[512,1024]{1,0:T(8,128)S(1)}, u32[]{:S(2)}) copy-start(f32[512,1024]{1,0:T(8,128)S(1)} %get-tuple-element.100.refs_10_) | copy-start | bytes 6291460
  64.6 0.7 copy-start.22
  65.0 2.0 copy-start.28
  67.0 1.3 copy-start.14
  68.3 16.4 %copy-start.2 = (bf16[512,1024]{1,0:T(8,128)(2,1)}, bf16[512,1024]{1,0:T(8,128)(2,1)S(1)}, u32[]{:S(2)}) copy-start(bf16[512,1024]{1,0:T(8,128)(2,1)S(1)} %convolution_convert_fusion.2.q_ref.refs_6_) | copy-start | bytes 3145732
  68.3 15.0 %copy-start.29 = (bf16[1024,1024]{1,0:T(8,128)(2,1)S(1)}, bf16[1024,1024]{1,0:T(8,128)(2,1)}, u32[]{:S(2)}) copy-start(bf16[1024,1024]{1,0:T(8,128)(2,1)} %refs_12_.1) | copy-start | bytes 6291460
  83.3 1.4 copy-start.3
  83.3 1.4 copy-start.7
  84.7 2.1 copy-start.12
  84.7 0.7 copy-start.23

commit v6 on v5

--- a/solution.py
+++ b/solution.py
@@ -102,7 +102,7 @@
             jax.ShapeDtypeStruct((rows, width), BF16),
             jax.ShapeDtypeStruct((pairs, 2, rows), F32),
         ],
-        compiler_params=pltpu.CompilerParams(vmem_limit_bytes=48 << 20),
+        compiler_params=pltpu.CompilerParams(vmem_limit_bytes=24 << 20),
         cost_estimate=pl.CostEstimate(flops=4 * flops, bytes_accessed=8 << 20, transcendentals=rows * span * HEADS),
     )(numbers, qid, kid, queries, keys, values)
 
@@ -173,7 +173,7 @@
             jax.ShapeDtypeStruct((rows, width), BF16),
             jax.ShapeDtypeStruct((pairs, 2, rows), F32),
         ],
-        compiler_params=pltpu.CompilerParams(vmem_limit_bytes=32 << 20),
+        compiler_params=pltpu.CompilerParams(vmem_limit_bytes=16 << 20),
         cost_estimate=pl.CostEstimate(
             flops=4 * rows * text * width, bytes_accessed=4 << 20, transcendentals=rows * text * HEADS // 4
         ),

time: 323 us -> 321 us (level)
  no operation moved by 1% of the time
where the time goes in v6:
time: 321 us; the launch traced here: 315 us
  Pallas kernels  263 us (82%)
  matrix products  18.7 us (6%)
  other arithmetic  12 us (4%)
  waiting for transfers between devices  10.7 us (3%)
  starting transfers between devices  5.11 us (2%)
  local copies, waits for them, and re-layouts  4.43 us (1%)
    pallas_call x1, Pallas kernels, layer_tail(): pl.pallas_call(functools.partial(layer_kernel, rows), in_specs=[anywhere]...  224 us
    dot_general x8, matrix products, matmul(): return jnp.dot(left, right, preferred_element_type=F32)  18.7 us
    pallas_call x1, Pallas kernels, attend_forward(): pl.pallas_call(functools.partial(forward_kernel, causal, sizes, ends), gr...  18.4 us
    pallas_call x1, Pallas kernels, cross_forward(): pl.pallas_call(cross_forward_kernel, grid=(pairs,), in_specs=[pl.BlockSpe...  15 us
    ppermute x1, waiting for transfers between devices, body(): block_two = lax.ppermute(tokens, AXIS, ahead)  10.2 us
  transfers between devices with their start and end apart: 2, of which 2 were waited for; matrix products, arithmetic and copies ran while one was open for 5% of the time, Pallas kernels for 0%

profile of v6, /device:TPU:0, one launch (start us, length us, event | category | flops | bytes accessed | tf_op | source)
XLA Modules:
  0.0 315.2 jit_solution(8807738461668794518)
XLA Ops:
  0.7 0.0 copy-start.16
  0.7 0.0 copy-start.32
  0.7 0.0 copy-start.31
  0.7 5.0 %collective-permute-start = (bf16[512,1024]{1,0:T(8,128)(2,1)}, bf16[512,1024]{1,0:T(8,128)(2,1)S(1)}, u32[]{:S(2)}, u32[]{:S(2)}) collective-permute-start(bf16[512,1024]{1,0:T(8,128)(2,1)} %param.23), channel_id=1, source_target_pairs={{0,2},{1,3},{2,4},{3,5},{4,6},{5,7},{6,8},{7,9},{8,10},{9,11},{10,... | collective-permute-start | bytes 3145736 | tf_op jit(solution)/shard_map/ppermute | solution.py:1229
  5.8 1.4 convert_reduce_fusion.2
  7.2 1.6 fusion.8
  8.8 0.1 pad_dynamic-slice_fusion.2
  8.9 0.1 pad_dynamic-slice_fusion.1
  9.1 0.1 select_reduce_fusion
  9.2 0.0 copy-start.17
  9.2 0.0 copy-start.18
  9.2 0.0 copy-start.19
  9.2 0.0 copy-start.20
  9.2 2.9 convolution_convert_fusion.4.k_ref.refs_7_
  12.1 0.7 pad_maximum_fusion.refs_31_
  12.9 0.1 slice.31
  13.0 0.1 copy.49.code_ref
  13.1 0.1 copy.48.qid_ref
  13.3 0.1 copy.51
  13.5 0.0 copy-start.11
  13.5 0.0 copy-start.22
  13.5 0.0 copy-start.25
  13.5 3.3 %convolution_convert_fusion.3.v_ref.refs_8_ = bf16[512,1024]{1,0:T(8,128)(2,1)S(1)} fusion(bf16[512,1024]{1,0:T(8,128)(2,1)} %refs_11_.1, bf16[1024,1024]{1,0:T(8,128)(2,1)} %refs_14_.1), kind=kOutput, calls=%fused_computation.26 | convolution fusion | flops 1074266112 | bytes 4194304 | tf_op jit(solution)/shard_map/dot_general | solution.py:1180
  16.8 1.3 convolution_convert_fusion.5.q_ref.refs_17_
  18.2 10.2 %collective-permute-done = bf16[512,1024]{1,0:T(8,128)(2,1)S(1)} collective-permute-done((bf16[512,1024]{1,0:T(8,128)(2,1)}, bf16[512,1024]{1,0:T(8,128)(2,1)S(1)}, u32[]{:S(2)}, u32[]{:S(2)}) %collective-permute-start) | collective-permute-done | bytes 1048608 | tf_op jit(solution)/shard_map/ppermute | solution.py:1229
  28.4 0.5 broadcast_select_fusion
  28.9 0.1 collective-permute-start.1
  29.0 0.1 pad_dynamic-slice_fusion.3
  29.1 0.2 fusion.22
  29.3 1.1 convert_reduce_fusion.1
  30.4 0.7 fusion.18.refs_29_
  31.1 0.5 collective-permute-done.1
  31.6 0.1 constant_dynamic-update-slice_fusion.1
  31.7 0.1 constant_dynamic-update-slice_fusion.refs_22_
  31.8 0.5 convert_reduce_fusion
  32.3 1.0 fusion.2
  33.3 0.2 copy-done.10
  33.4 1.6 fusion.5.refs_21_
  35.1 0.0 copy-start.26
  35.1 3.6 %convolution_convert_fusion.v_ref.refs_19_ = bf16[1536,1024]{1,0:T(8,128)(2,1)S(1)} fusion(bf16[1536,1024]{1,0:T(8,128)(2,1)S(1)} %fusion.5.refs_21_, bf16[1024,1024]{1,0:T(8,128)(2,1)S(1)} %copy-done.27), kind=kOutput, calls=%fused_computation.8 | convolution fusion | flops 3222798336 | bytes 8388608 | tf_op jit(solution)/shard_map/dot_general | solution.py:1180
  38.8 3.6 %convolution_convert_fusion.1.k_ref.refs_18_ = bf16[1536,1024]{1,0:T(8,128)(2,1)S(1)} fusion(bf16[1536,1024]{1,0:T(8,128)(2,1)S(1)} %fusion.5.refs_21_, bf16[1024,1024]{1,0:T(8,128)(2,1)S(1)} %copy-done.26), kind=kOutput, calls=%fused_computation.9 | convolution fusion | flops 3222798336 | bytes 8388608 | tf_op jit(solution)/shard_map/dot_general | solution.py:1180
  42.4 0.0 copy-start.28
  42.5 18.4 %shard_map.366 = (bf16[512,1024]{1,0:T(8,128)(2,1)S(1)}, f32[8,2,512]{2,1,0:T(2,128)S(1)}) custom-call(s32[2]{0:T(128)S(1)} %subtract_clamp_fusion.n_ref, s32[512,1]{1,0:T(8,128)S(1)} %copy.48.qid_ref, s32[2,1,1280]{2,1,0:T(1,128)S(1)} %broadcast_in_dim.29.kid_ref, bf16[512,1024]{1,0:T(8,128)(2,1)S(1)} %convolution_convert_fusion.5.q_ref.refs_17_, ...), custom_call_target="tpu_custom_call" | custom-call | flops 10737418240 | bytes 8388608 | tf_op jit(solution)/shard_map/pallas_call | solution.py:83
  60.9 0.0 copy-start.9
  60.9 1.4 fusion.28
  62.3 0.0 copy-start.23
  62.3 0.3 multiply_reduce_fusion.1
  62.7 0.3 copy-done.23
  63.0 0.4 add_convert_fusion.1.refs_9_
  63.4 1.2 copy-done.29
  64.6 1.2 convolution_convert_fusion.2.q_ref.refs_6_
  65.9 0.0 copy-start.30
  65.9 15.0 %shard_map.367 = (bf16[512,1024]{1,0:T(8,128)(2,1)S(1)}, f32[8,2,512]{2,1,0:T(2,128)S(1)}) custom-call(s32[512,1]{1,0:T(8,128)S(1)} %copy.49.code_ref, s32[4,128]{1,0:T(4,128)S(1)} %fusion.25.key_ref, bf16[512,1024]{1,0:T(8,128)(2,1)S(1)} %convolution_convert_fusion.2.q_ref.refs_6_, bf16[512,1024]{1,0:T(8,128)(2,1)S(1)} %convolution_convert_fusion.4.k_ref.refs_7_, ...), custom_call_target="tpu_custom_call" | custom-call | flops 1073741824 | bytes 4194304 | tf_op jit(solution)/shard_map/pallas_call | solution.py:165
  81.0 0.0 copy-start.8
  81.0 1.3 fusion.29
  82.3 0.0 copy-start.13
  82.4 0.0 copy-start.24
  82.4 0.3 multiply_reduce_fusion
  82.7 0.3 copy-done.24
  83.1 1.4 add_convert_fusion.refs_0_
  84.4 224.0 %shard_map.368 = (f32[32,4096]{1,0:T(8,128)}, f32[128,1024]{1,0:T(8,128)}, f32[32,1024]{1,0:T(8,128)}, f32[32,1024]{1,0:T(8,128)}, f32[32,1024]{1,0:T(8,128)}, /...) custom-call(bf16[512,1024]{1,0:T(8,128)(2,1)} %add_convert_fusion.re, ...), custom_call_target="tpu_custom_call" | custom-call | flops 17179869184 | bytes 67108864 | tf_op jit(solution)/shard_map/pallas_call | solution.py:1160
  308.4 0.8 constant_dynamic-slice_fusion
  309.2 0.5 slice_bitcast_fusion
  309.7 5.3 %shard_map.369 = (f32[32,4096]{1,0:T(8,128)}, f32[128,1024]{1,0:T(8,128)}, f32[32,1024]{1,0:T(8,128)}, f32[32,1024]{1,0:T(8,128)}, f32[32,1024]{1,0:T(8,128)}, /...) custom-call(f32[32,4096]{1,0:T(8,128)} %get-tuple-element.62.refs_0_, ...), custom_call_target="tpu_custom_call" | custom-call | bytes 12582912 | tf_op jit(solution)/shard_map/pallas_call | solution.py:1123
  (61 shorter events, 0.2 us)
Async XLA Ops:
  0.7 8.2 %copy-start.16 = (s32[16384]{0:T(1024)S(1)}, s32[16384]{0:T(1024)}, u32[]{:S(2)}) copy-start(s32[16384]{0:T(1024)} %param.42) | copy-start | bytes 196612
  0.7 8.4 %copy-start.32 = (s32[24]{0:T(128)S(1)}, s32[24]{0:T(128)}, u32[]{:S(2)}) copy-start(s32[24]{0:T(128)} %param.45) | copy-start | bytes 292
  0.7 8.4 %copy-start.33 = (s32[24]{0:T(128)S(1)}, s32[24]{0:T(128)}, u32[]{:S(2)}) copy-start(s32[24]{0:T(128)} %param.44) | copy-start | bytes 292
  0.7 8.5 %copy-start.31 = (bf16[512,1024]{1,0:T(8,128)(2,1)S(1)}, bf16[512,1024]{1,0:T(8,128)(2,1)}, u32[]{:S(2)}) copy-start(bf16[512,1024]{1,0:T(8,128)(2,1)} %refs_11_.1) | copy-start | bytes 3145732
  0.7 27.7 %collective-permute-start = (bf16[512,1024]{1,0:T(8,128)(2,1)}, bf16[512,1024]{1,0:T(8,128)(2,1)S(1)}, u32[]{:S(2)}, u32[]{:S(2)}) collective-permute-start(bf16[512,1024]{1,0:T(8,128)(2,1)} %param.23), channel_id=1, source_target_pairs={{0,2},{1,3},{2,4},{3,5},{4,6},{5,7},{6,8},{7,9},{8,10},{9,11},{10,... | collective-permute-start | bytes 3145736 | tf_op jit(solution)/shard_map/ppermute | solution.py:1229
  9.1 3.8 %copy-start.21 = (s32[512]{0:T(512)}, s32[512]{0:T(512)S(1)}, u32[]{:S(2)}) copy-start(s32[512]{0:T(512)S(1)} %select_reduce_fusion) | copy-start | bytes 6148
  9.2 2.9 copy-start.17
  9.2 2.9 copy-start.18
  9.2 2.9 copy-start.19
  9.2 4.1 %copy-start.20 = (s32[4,128]{1,0:T(4,128)S(1)}, s32[4,128]{1,0:T(4,128)}, u32[]{:S(2)}) copy-start(s32[4,128]{1,0:T(4,128)} %param.43) | copy-start | bytes 6148
  12.1 53.8 %copy-start = (bf16[512,1024]{1,0:T(8,128)(2,1)}, bf16[512,1024]{1,0:T(8,128)(2,1)S(1)}, u32[]{:S(2)}) copy-start(bf16[512,1024]{1,0:T(8,128)(2,1)S(1)} %convolution_convert_fusion.4.k_ref.refs_7_) | copy-start | bytes 3145732
  13.5 3.4 %copy-start.11 = (bf16[512,1024]{1,0:T(8,128)(2,1)S(1)}, bf16[512,1024]{1,0:T(8,128)(2,1)}, u32[]{:S(2)}) copy-start(bf16[512,1024]{1,0:T(8,128)(2,1)} %param.23) | copy-start | bytes 3145732
  13.5 3.4 %copy-start.22 = (f32[1024]{0:T(1024)S(1)}, f32[1024]{0:T(1024)}, u32[]{:S(2)}) copy-start(f32[1024]{0:T(1024)} %param.37) | copy-start | bytes 12292
  13.5 3.4 %copy-start.25 = (bf16[1024,1024]{1,0:T(8,128)(2,1)S(1)}, bf16[1024,1024]{1,0:T(8,128)(2,1)}, u32[]{:S(2)}) copy-start(bf16[1024,1024]{1,0:T(8,128)(2,1)} %refs_23_.1) | copy-start | bytes 6291460
  16.8 49.1 %copy-start.1 = (bf16[512,1024]{1,0:T(8,128)(2,1)}, bf16[512,1024]{1,0:T(8,128)(2,1)S(1)}, u32[]{:S(2)}) copy-start(bf16[512,1024]{1,0:T(8,128)(2,1)S(1)} %convolution_convert_fusion.3.v_ref.refs_8_) | copy-start | bytes 3145732
  18.2 24.2 %copy-start.7 = (bf16[512,1024]{1,0:T(8,128)(2,1)}, bf16[512,1024]{1,0:T(8,128)(2,1)S(1)}, u32[]{:S(2)}) copy-start(bf16[512,1024]{1,0:T(8,128)(2,1)S(1)} %convolution_convert_fusion.5.q_ref.refs_17_) | copy-start | bytes 3145732
  28.9 2.7 collective-permute-start.1
  31.8 1.6 copy-start.10
  33.4 1.6 copy-start.27
  35.1 3.7 %copy-start.14 = (bf16[1536,1024]{1,0:T(8,128)(2,1)}, bf16[1536,1024]{1,0:T(8,128)(2,1)S(1)}, u32[]{:S(2)}) copy-start(bf16[1536,1024]{1,0:T(8,128)(2,1)S(1)} %fusion.5.refs_21_) | copy-start | bytes 9437188
  35.1 3.7 %copy-start.26 = (bf16[1024,1024]{1,0:T(8,128)(2,1)S(1)}, bf16[1024,1024]{1,0:T(8,128)(2,1)}, u32[]{:S(2)}) copy-start(bf16[1024,1024]{1,0:T(8,128)(2,1)} %refs_24_.1) | copy-start | bytes 6291460
  38.8 3.7 %copy-start.4 = (bf16[1536,1024]{1,0:T(8,128)(2,1)}, bf16[1536,1024]{1,0:T(8,128)(2,1)S(1)}, u32[]{:S(2)}) copy-start(bf16[1536,1024]{1,0:T(8,128)(2,1)S(1)} %convolution_convert_fusion.v_ref.refs_19_) | copy-start | bytes 9437188
  42.4 18.4 %copy-start.5 = (bf16[1536,1024]{1,0:T(8,128)(2,1)}, bf16[1536,1024]{1,0:T(8,128)(2,1)S(1)}, u32[]{:S(2)}) copy-start(bf16[1536,1024]{1,0:T(8,128)(2,1)S(1)} %convolution_convert_fusion.1.k_ref.refs_18_) | copy-start | bytes 9437188
  42.4 18.5 %copy-start.28 = (bf16[1024,1024]{1,0:T(8,128)(2,1)S(1)}, bf16[1024,1024]{1,0:T(8,128)(2,1)}, u32[]{:S(2)}) copy-start(bf16[1024,1024]{1,0:T(8,128)(2,1)} %refs_16_.1) | copy-start | bytes 6291460
  60.9 1.4 copy-start.6
  60.9 1.4 copy-start.9
  62.3 18.7 %copy-start.12 = (f32[512,1024]{1,0:T(8,128)}, f32[512,1024]{1,0:T(8,128)S(1)}, u32[]{:S(2)}) copy-start(f32[512,1024]{1,0:T(8,128)S(1)} %get-tuple-element.100.refs_10_) | copy-start | bytes 6291460
  62.3 0.7 copy-start.23
  62.7 2.0 copy-start.29
  64.6 1.3 copy-start.15
  65.9 15.0 %copy-start.2 = (bf16[512,1024]{1,0:T(8,128)(2,1)}, bf16[512,1024]{1,0:T(8,128)(2,1)S(1)}, u32[]{:S(2)}) copy-start(bf16[512,1024]{1,0:T(8,128)(2,1)S(1)} %convolution_convert_fusion.2.q_ref.refs_6_) | copy-start | bytes 3145732
  65.9 15.0 %copy-start.30 = (bf16[1024,1024]{1,0:T(8,128)(2,1)S(1)}, bf16[1024,1024]{1,0:T(8,128)(2,1)}, u32[]{:S(2)}) copy-start(bf16[1024,1024]{1,0:T(8,128)(2,1)} %refs_12_.1) | copy-start | bytes 6291460
  80.9 1.4 copy-start.3
  81.0 1.4 copy-start.8
  82.3 2.1 copy-start.13
  82.4 0.7 copy-start.24

commit v7 on v6

--- a/solution.py
+++ b/solution.py
@@ -1082,19 +1082,19 @@
     def _():
         send_back.wait_recv()
 
+    second(16)
     each_step(norm_one)
     out_copy = start_copy(sums.at[1], input_grad)
     step.wait()
     vec[...] += vec_in[1]
     step = vec_step(2, y_peer)
     third(14)
-    second(16)
+    third(15)
     step.wait()
     vec[...] += vec_in[2]
     steps = [vec_step(3 + m, z_peers[m]) for m in range(3)]
     for c in range(total - 3):
         last(c)
-    third(15)
     third(16)
     for step in steps:
         step.wait()

time: 321 us -> 323 us (level)
  no operation moved by 1% of the time
where the time goes in v7:
time: 323 us; the launch traced here: 316 us
  Pallas kernels  264 us (82%)
  matrix products  18.7 us (6%)
  other arithmetic  12 us (4%)
  waiting for transfers between devices  10.7 us (3%)
  starting transfers between devices  5.11 us (2%)
  local copies, waits for them, and re-layouts  4.43 us (1%)
    pallas_call x1, Pallas kernels, layer_tail(): pl.pallas_call(functools.partial(layer_kernel, rows), in_specs=[anywhere]...  225 us
    dot_general x8, matrix products, matmul(): return jnp.dot(left, right, preferred_element_type=F32)  18.7 us
    pallas_call x1, Pallas kernels, attend_forward(): pl.pallas_call(functools.partial(forward_kernel, causal, sizes, ends), gr...  18.4 us
    pallas_call x1, Pallas kernels, cross_forward(): pl.pallas_call(cross_forward_kernel, grid=(pairs,), in_specs=[pl.BlockSpe...  15 us
    ppermute x1, waiting for transfers between devices, body(): block_two = lax.ppermute(tokens, AXIS, ahead)  10.2 us
  transfers between devices with their start and end apart: 2, of which 2 were waited for; matrix products, arithmetic and copies ran while one was open for 5% of the time, Pallas kernels for 0%

profile of v7, /device:TPU:0, one launch (start us, length us, event | category | flops | bytes accessed | tf_op | source)
XLA Modules:
  0.0 316.5 jit_solution(14065675746362480487)
XLA Ops:
  0.7 0.0 copy-start.16
  0.7 0.0 copy-start.32
  0.7 0.0 copy-start.31
  0.7 5.0 %collective-permute-start = (bf16[512,1024]{1,0:T(8,128)(2,1)}, bf16[512,1024]{1,0:T(8,128)(2,1)S(1)}, u32[]{:S(2)}, u32[]{:S(2)}) collective-permute-start(bf16[512,1024]{1,0:T(8,128)(2,1)} %param.23), channel_id=1, source_target_pairs={{0,2},{1,3},{2,4},{3,5},{4,6},{5,7},{6,8},{7,9},{8,10},{9,11},{10,... | collective-permute-start | bytes 3145736 | tf_op jit(solution)/shard_map/ppermute | solution.py:1229
  5.8 1.4 convert_reduce_fusion.2
  7.2 1.6 fusion.8
  8.8 0.1 pad_dynamic-slice_fusion.2
  8.9 0.1 pad_dynamic-slice_fusion.1
  9.1 0.1 select_reduce_fusion
  9.2 0.0 copy-start.17
  9.2 0.0 copy-start.18
  9.2 0.0 copy-start.19
  9.2 0.0 copy-start.20
  9.2 2.9 convolution_convert_fusion.4.k_ref.refs_7_
  12.1 0.7 pad_maximum_fusion.refs_31_
  12.9 0.1 slice.31
  13.0 0.1 copy.49.code_ref
  13.1 0.1 copy.48.qid_ref
  13.3 0.1 copy.51
  13.5 0.0 copy-start.11
  13.5 0.0 copy-start.22
  13.5 0.0 copy-start.25
  13.5 3.3 %convolution_convert_fusion.3.v_ref.refs_8_ = bf16[512,1024]{1,0:T(8,128)(2,1)S(1)} fusion(bf16[512,1024]{1,0:T(8,128)(2,1)} %refs_11_.1, bf16[1024,1024]{1,0:T(8,128)(2,1)} %refs_14_.1), kind=kOutput, calls=%fused_computation.26 | convolution fusion | flops 1074266112 | bytes 4194304 | tf_op jit(solution)/shard_map/dot_general | solution.py:1180
  16.8 1.3 convolution_convert_fusion.5.q_ref.refs_17_
  18.2 10.2 %collective-permute-done = bf16[512,1024]{1,0:T(8,128)(2,1)S(1)} collective-permute-done((bf16[512,1024]{1,0:T(8,128)(2,1)}, bf16[512,1024]{1,0:T(8,128)(2,1)S(1)}, u32[]{:S(2)}, u32[]{:S(2)}) %collective-permute-start) | collective-permute-done | bytes 1048608 | tf_op jit(solution)/shard_map/ppermute | solution.py:1229
  28.4 0.5 broadcast_select_fusion
  28.9 0.1 collective-permute-start.1
  29.0 0.1 pad_dynamic-slice_fusion.3
  29.1 0.2 fusion.22
  29.3 1.1 convert_reduce_fusion.1
  30.4 0.7 fusion.18.refs_29_
  31.1 0.5 collective-permute-done.1
  31.6 0.1 constant_dynamic-update-slice_fusion.1
  31.7 0.1 constant_dynamic-update-slice_fusion.refs_22_
  31.8 0.5 convert_reduce_fusion
  32.3 1.0 fusion.2
  33.3 0.2 copy-done.10
  33.4 1.6 fusion.5.refs_21_
  35.1 0.0 copy-start.26
  35.1 3.6 %convolution_convert_fusion.v_ref.refs_19_ = bf16[1536,1024]{1,0:T(8,128)(2,1)S(1)} fusion(bf16[1536,1024]{1,0:T(8,128)(2,1)S(1)} %fusion.5.refs_21_, bf16[1024,1024]{1,0:T(8,128)(2,1)S(1)} %copy-done.27), kind=kOutput, calls=%fused_computation.8 | convolution fusion | flops 3222798336 | bytes 8388608 | tf_op jit(solution)/shard_map/dot_general | solution.py:1180
  38.8 3.6 %convolution_convert_fusion.1.k_ref.refs_18_ = bf16[1536,1024]{1,0:T(8,128)(2,1)S(1)} fusion(bf16[1536,1024]{1,0:T(8,128)(2,1)S(1)} %fusion.5.refs_21_, bf16[1024,1024]{1,0:T(8,128)(2,1)S(1)} %copy-done.26), kind=kOutput, calls=%fused_computation.9 | convolution fusion | flops 3222798336 | bytes 8388608 | tf_op jit(solution)/shard_map/dot_general | solution.py:1180
  42.4 0.0 copy-start.28
  42.5 18.4 %shard_map.366 = (bf16[512,1024]{1,0:T(8,128)(2,1)S(1)}, f32[8,2,512]{2,1,0:T(2,128)S(1)}) custom-call(s32[2]{0:T(128)S(1)} %subtract_clamp_fusion.n_ref, s32[512,1]{1,0:T(8,128)S(1)} %copy.48.qid_ref, s32[2,1,1280]{2,1,0:T(1,128)S(1)} %broadcast_in_dim.29.kid_ref, bf16[512,1024]{1,0:T(8,128)(2,1)S(1)} %convolution_convert_fusion.5.q_ref.refs_17_, ...), custom_call_target="tpu_custom_call" | custom-call | flops 10737418240 | bytes 8388608 | tf_op jit(solution)/shard_map/pallas_call | solution.py:83
  60.9 0.0 copy-start.9
  60.9 1.4 fusion.28
  62.3 0.0 copy-start.23
  62.3 0.3 multiply_reduce_fusion.1
  62.7 0.3 copy-done.23
  63.0 0.4 add_convert_fusion.1.refs_9_
  63.4 1.2 copy-done.29
  64.6 1.2 convolution_convert_fusion.2.q_ref.refs_6_
  65.9 0.0 copy-start.30
  65.9 15.0 %shard_map.367 = (bf16[512,1024]{1,0:T(8,128)(2,1)S(1)}, f32[8,2,512]{2,1,0:T(2,128)S(1)}) custom-call(s32[512,1]{1,0:T(8,128)S(1)} %copy.49.code_ref, s32[4,128]{1,0:T(4,128)S(1)} %fusion.25.key_ref, bf16[512,1024]{1,0:T(8,128)(2,1)S(1)} %convolution_convert_fusion.2.q_ref.refs_6_, bf16[512,1024]{1,0:T(8,128)(2,1)S(1)} %convolution_convert_fusion.4.k_ref.refs_7_, ...), custom_call_target="tpu_custom_call" | custom-call | flops 1073741824 | bytes 4194304 | tf_op jit(solution)/shard_map/pallas_call | solution.py:165
  81.0 0.0 copy-start.8
  81.0 1.3 fusion.29
  82.3 0.0 copy-start.13
  82.4 0.0 copy-start.24
  82.4 0.3 multiply_reduce_fusion
  82.7 0.3 copy-done.24
  83.1 1.4 add_convert_fusion.refs_0_
  84.4 225.2 %shard_map.368 = (f32[32,4096]{1,0:T(8,128)}, f32[128,1024]{1,0:T(8,128)}, f32[32,1024]{1,0:T(8,128)}, f32[32,1024]{1,0:T(8,128)}, f32[32,1024]{1,0:T(8,128)}, /...) custom-call(bf16[512,1024]{1,0:T(8,128)(2,1)} %add_convert_fusion.re, ...), custom_call_target="tpu_custom_call" | custom-call | flops 17179869184 | bytes 67108864 | tf_op jit(solution)/shard_map/pallas_call | solution.py:1160
  309.6 0.8 constant_dynamic-slice_fusion
  310.4 0.5 slice_bitcast_fusion
  310.9 5.3 %shard_map.369 = (f32[32,4096]{1,0:T(8,128)}, f32[128,1024]{1,0:T(8,128)}, f32[32,1024]{1,0:T(8,128)}, f32[32,1024]{1,0:T(8,128)}, f32[32,1024]{1,0:T(8,128)}, /...) custom-call(f32[32,4096]{1,0:T(8,128)} %get-tuple-element.62.refs_0_, ...), custom_call_target="tpu_custom_call" | custom-call | bytes 12582912 | tf_op jit(solution)/shard_map/pallas_call | solution.py:1123
  (61 shorter events, 0.2 us)
Async XLA Ops:
  0.7 8.2 %copy-start.16 = (s32[16384]{0:T(1024)S(1)}, s32[16384]{0:T(1024)}, u32[]{:S(2)}) copy-start(s32[16384]{0:T(1024)} %param.42) | copy-start | bytes 196612
  0.7 8.4 %copy-start.32 = (s32[24]{0:T(128)S(1)}, s32[24]{0:T(128)}, u32[]{:S(2)}) copy-start(s32[24]{0:T(128)} %param.45) | copy-start | bytes 292
  0.7 8.4 %copy-start.33 = (s32[24]{0:T(128)S(1)}, s32[24]{0:T(128)}, u32[]{:S(2)}) copy-start(s32[24]{0:T(128)} %param.44) | copy-start | bytes 292
  0.7 8.5 %copy-start.31 = (bf16[512,1024]{1,0:T(8,128)(2,1)S(1)}, bf16[512,1024]{1,0:T(8,128)(2,1)}, u32[]{:S(2)}) copy-start(bf16[512,1024]{1,0:T(8,128)(2,1)} %refs_11_.1) | copy-start | bytes 3145732
  0.7 27.7 %collective-permute-start = (bf16[512,1024]{1,0:T(8,128)(2,1)}, bf16[512,1024]{1,0:T(8,128)(2,1)S(1)}, u32[]{:S(2)}, u32[]{:S(2)}) collective-permute-start(bf16[512,1024]{1,0:T(8,128)(2,1)} %param.23), channel_id=1, source_target_pairs={{0,2},{1,3},{2,4},{3,5},{4,6},{5,7},{6,8},{7,9},{8,10},{9,11},{10,... | collective-permute-start | bytes 3145736 | tf_op jit(solution)/shard_map/ppermute | solution.py:1229
  9.1 3.8 %copy-start.21 = (s32[512]{0:T(512)}, s32[512]{0:T(512)S(1)}, u32[]{:S(2)}) copy-start(s32[512]{0:T(512)S(1)} %select_reduce_fusion) | copy-start | bytes 6148
  9.2 2.9 copy-start.17
  9.2 2.9 copy-start.18
  9.2 2.9 copy-start.19
  9.2 4.1 %copy-start.20 = (s32[4,128]{1,0:T(4,128)S(1)}, s32[4,128]{1,0:T(4,128)}, u32[]{:S(2)}) copy-start(s32[4,128]{1,0:T(4,128)} %param.43) | copy-start | bytes 6148
  12.1 53.8 %copy-start = (bf16[512,1024]{1,0:T(8,128)(2,1)}, bf16[512,1024]{1,0:T(8,128)(2,1)S(1)}, u32[]{:S(2)}) copy-start(bf16[512,1024]{1,0:T(8,128)(2,1)S(1)} %convolution_convert_fusion.4.k_ref.refs_7_) | copy-start | bytes 3145732
  13.5 3.4 %copy-start.11 = (bf16[512,1024]{1,0:T(8,128)(2,1)S(1)}, bf16[512,1024]{1,0:T(8,128)(2,1)}, u32[]{:S(2)}) copy-start(bf16[512,1024]{1,0:T(8,128)(2,1)} %param.23) | copy-start | bytes 3145732
  13.5 3.4 %copy-start.22 = (f32[1024]{0:T(1024)S(1)}, f32[1024]{0:T(1024)}, u32[]{:S(2)}) copy-start(f32[1024]{0:T(1024)} %param.37) | copy-start | bytes 12292
  13.5 3.4 %copy-start.25 = (bf16[1024,1024]{1,0:T(8,128)(2,1)S(1)}, bf16[1024,1024]{1,0:T(8,128)(2,1)}, u32[]{:S(2)}) copy-start(bf16[1024,1024]{1,0:T(8,128)(2,1)} %refs_23_.1) | copy-start | bytes 6291460
  16.8 49.1 %copy-start.1 = (bf16[512,1024]{1,0:T(8,128)(2,1)}, bf16[512,1024]{1,0:T(8,128)(2,1)S(1)}, u32[]{:S(2)}) copy-start(bf16[512,1024]{1,0:T(8,128)(2,1)S(1)} %convolution_convert_fusion.3.v_ref.refs_8_) | copy-start | bytes 3145732
  18.2 24.2 %copy-start.7 = (bf16[512,1024]{1,0:T(8,128)(2,1)}, bf16[512,1024]{1,0:T(8,128)(2,1)S(1)}, u32[]{:S(2)}) copy-start(bf16[512,1024]{1,0:T(8,128)(2,1)S(1)} %convolution_convert_fusion.5.q_ref.refs_17_) | copy-start | bytes 3145732
  28.9 2.7 collective-permute-start.1
  31.8 1.6 copy-start.10
  33.4 1.6 copy-start.27
  35.1 3.7 %copy-start.14 = (bf16[1536,1024]{1,0:T(8,128)(2,1)}, bf16[1536,1024]{1,0:T(8,128)(2,1)S(1)}, u32[]{:S(2)}) copy-start(bf16[1536,1024]{1,0:T(8,128)(2,1)S(1)} %fusion.5.refs_21_) | copy-start | bytes 9437188
  35.1 3.7 %copy-start.26 = (bf16[1024,1024]{1,0:T(8,128)(2,1)S(1)}, bf16[1024,1024]{1,0:T(8,128)(2,1)}, u32[]{:S(2)}) copy-start(bf16[1024,1024]{1,0:T(8,128)(2,1)} %refs_24_.1) | copy-start | bytes 6291460
  38.8 3.7 %copy-start.4 = (bf16[1536,1024]{1,0:T(8,128)(2,1)}, bf16[1536,1024]{1,0:T(8,128)(2,1)S(1)}, u32[]{:S(2)}) copy-start(bf16[1536,1024]{1,0:T(8,128)(2,1)S(1)} %convolution_convert_fusion.v_ref.refs_19_) | copy-start | bytes 9437188
  42.4 18.4 %copy-start.5 = (bf16[1536,1024]{1,0:T(8,128)(2,1)}, bf16[1536,1024]{1,0:T(8,128)(2,1)S(1)}, u32[]{:S(2)}) copy-start(bf16[1536,1024]{1,0:T(8,128)(2,1)S(1)} %convolution_convert_fusion.1.k_ref.refs_18_) | copy-start | bytes 9437188
  42.4 18.5 %copy-start.28 = (bf16[1024,1024]{1,0:T(8,128)(2,1)S(1)}, bf16[1024,1024]{1,0:T(8,128)(2,1)}, u32[]{:S(2)}) copy-start(bf16[1024,1024]{1,0:T(8,128)(2,1)} %refs_16_.1) | copy-start | bytes 6291460
  60.9 1.4 copy-start.6
  60.9 1.4 copy-start.9
  62.3 18.7 %copy-start.12 = (f32[512,1024]{1,0:T(8,128)}, f32[512,1024]{1,0:T(8,128)S(1)}, u32[]{:S(2)}) copy-start(f32[512,1024]{1,0:T(8,128)S(1)} %get-tuple-element.100.refs_10_) | copy-start | bytes 6291460
  62.3 0.7 copy-start.23
  62.7 2.0 copy-start.29
  64.6 1.3 copy-start.15
  65.9 15.0 %copy-start.2 = (bf16[512,1024]{1,0:T(8,128)(2,1)}, bf16[512,1024]{1,0:T(8,128)(2,1)S(1)}, u32[]{:S(2)}) copy-start(bf16[512,1024]{1,0:T(8,128)(2,1)S(1)} %convolution_convert_fusion.2.q_ref.refs_6_) | copy-start | bytes 3145732
  65.9 15.0 %copy-start.30 = (bf16[1024,1024]{1,0:T(8,128)(2,1)S(1)}, bf16[1024,1024]{1,0:T(8,128)(2,1)}, u32[]{:S(2)}) copy-start(bf16[1024,1024]{1,0:T(8,128)(2,1)} %refs_12_.1) | copy-start | bytes 6291460
  80.9 1.4 copy-start.3
  81.0 1.4 copy-start.8
  82.3 2.1 copy-start.13
  82.4 0.7 copy-start.24
